TPU v7x, 32 devices: a whole 2x2x4 slice. The times are simulated.
32 devices in a mesh: seq: 4 (over x, core), rows: 8 (over z, y).
Axes of the slice: x: 2, y: 2, z: 4, core: 2. Of those that a mesh axis runs over, the one named last changes fastest.
Arguments:
- patches: bfloat16 [16, 1024, 768], P('rows', 'seq'), may hold values from -6 to 6
- segments: int32 [16, 1024], P('rows', 'seq'), may hold values from 0 to 8, as said below
- masked: int32 [16, 1024], P('rows', 'seq'), may hold values 0 or 1
- mask_embedding: bfloat16 [768], P(('seq', 'rows')), may hold values from -5 to 5
- norm1_gain: bfloat16 [768], P(('seq', 'rows')), may hold values from 0.5 to 1.5
- norm1_bias: bfloat16 [768], P(('seq', 'rows')), may hold values from -4 to 4
- qkv_weight: bfloat16 [768, 2304], P(('seq', 'rows')), may hold values from -0.21875 to 0.21875
- query_bias: bfloat16 [768], P(('seq', 'rows')), may hold values from -4 to 4
- value_bias: bfloat16 [768], P(('seq', 'rows')), may hold values from -0.75 to 0.75
- out_weight: bfloat16 [768, 768], P(('seq', 'rows')), may hold values from -3.5 to 3.5
- out_bias: bfloat16 [768], P(('seq', 'rows')), may hold values from -4 to 4
- norm2_gain: bfloat16 [768], P(('seq', 'rows')), may hold values from 0.5 to 1.5
- norm2_bias: bfloat16 [768], P(('seq', 'rows')), may hold values from -4 to 4
- up_weight: bfloat16 [768, 3072], P(('seq', 'rows')), may hold values from -0.21875 to 0.21875
- up_bias: bfloat16 [3072], P(('seq', 'rows')), may hold values from -4 to 4
- down_weight: bfloat16 [3072, 768], P(('seq', 'rows')), may hold values from -0.109375 to 0.109375
- down_bias: bfloat16 [768], P(('seq', 'rows')), may hold values from -4 to 4
- cotangent: bfloat16 [16, 1024, 768], P('rows', 'seq'), may hold values from -6 to 6
Outputs:
- output: bfloat16 [16, 1024, 768], P('rows', 'seq')
- input_grad: float32 [16, 1024, 768], P('rows', 'seq')
- mask_embedding_grad: float32 [768], P(('seq', 'rows'))
- norm1_gain_grad: float32 [768], P(('seq', 'rows'))
- norm1_bias_grad: float32 [768], P(('seq', 'rows'))
- qkv_weight_grad: float32 [768, 2304], P(('seq', 'rows'))
- query_bias_grad: float32 [768], P(('seq', 'rows'))
- value_bias_grad: float32 [768], P(('seq', 'rows'))
- out_weight_grad: float32 [768, 768], P(('seq', 'rows'))
- out_bias_grad: float32 [768], P(('seq', 'rows'))
- norm2_gain_grad: float32 [768], P(('seq', 'rows'))
- norm2_bias_grad: float32 [768], P(('seq', 'rows'))
- up_weight_grad: float32 [768, 3072], P(('seq', 'rows'))
- up_bias_grad: float32 [3072], P(('seq', 'rows'))
- down_weight_grad: float32 [3072, 768], P(('seq', 'rows'))
- down_bias_grad: float32 [768], P(('seq', 'rows'))
Inputs may be any that keep to these rules, and one draw needn't show every extreme that they name: `segments`: along each row the ids never fall except to 0; 0 (padding) stands only in the last fewer than 64 positions of a row; in the first of every 2 rows one clip covers patches of every index of seq.
All inputs are finite; a program needn't handle non-finite values. No bound on the sum of `masked` on one device may be relied on, other than what follows from the above.
Results may differ from a plain program's by a relative error of at most 0.017.
Values may be sent and summed in bfloat16 or wider, within the bound.
No kernel may reach another device: no remote copies, remote signals or barrier semaphores. Data moves between devices by JAX's collectives and lax.ppermute only.
A program may use at most 192 MiB of HBM per device.

v0:
```python
import jax
import jax.numpy as jnp
from jax import lax
from jax.experimental import pallas as pl
from jax.experimental.pallas import tpu as pltpu
from jax.sharding import PartitionSpec as P

HEAD_SIZE = 64
LANES = 128
CHUNK = 256
PAIRS = 6
PAIRS_BACK = 6
MASKED = 16
EPSILON = 1e-06
FLOOR_SCORE = -1e30
HALF_ROOT = 0.7071067811865476
MIB = 2**20
EVERY = ("seq", "rows")
BF16 = jnp.bfloat16
F32 = jnp.float32
EMBED, GAIN1, SHIFT1, QBIAS, VBIAS, OBIAS, GAIN2, SHIFT2, DBIAS, UBIAS = range(10)
KINDS = 16


def dot(left, right, left_dim, right_dim):
    return lax.dot_general(
        left, right, (((left_dim,), (right_dim,)), ((), ())), preferred_element_type=F32
    )


def column(row):
    return jnp.broadcast_to(row, (8, row.shape[1])).T[:, :1]


def segment_of(flags):
    return flags - jnp.where(flags >= MASKED, float(MASKED), 0.0)


def norm_parts(values):
    mean = jnp.mean(values, axis=-1, keepdims=True)
    centered = values - mean
    rate = lax.rsqrt(jnp.mean(centered * centered, axis=-1, keepdims=True) + EPSILON)
    return centered * rate, rate


def norm_back(pulled, hat, rate):
    first = jnp.mean(pulled, axis=-1, keepdims=True)
    second = jnp.mean(pulled * hat, axis=-1, keepdims=True)
    return rate * (pulled - first - hat * second)


def parted(value, mine, depth):
    sent, kept = [], []
    for x in range(value.shape[0] // (2 * depth)):
        low = value[2 * x * depth : (2 * x + 1) * depth]
        high = value[(2 * x + 1) * depth : (2 * x + 2) * depth]
        sent.append(jnp.where(mine == 0, high, low))
        kept.append(jnp.where(mine == 0, low, high))
    return sent, kept


def whole(*shape):
    return pl.BlockSpec(shape, lambda *_: (0,) * len(shape))


ANYWHERE = pl.BlockSpec(memory_space=pl.ANY)


def shaped(dtype, *shape):
    return jax.ShapeDtypeStruct(shape, dtype)


def placed(dtype, *shape):
    return pltpu.HBM(shape, dtype)


def far(array):
    return pltpu.with_memory_space_constraint(array, pltpu.HBM)


def parameters(mib=32):
    return pltpu.CompilerParams(vmem_limit_bytes=mib * MIB)


def cost(flops, nbytes, transcendentals=0):
    return pl.CostEstimate(flops=flops, bytes_accessed=nbytes, transcendentals=transcendentals)


def split_heads(pair):
    lane = lax.broadcasted_iota(jnp.int32, pair.shape, 1)
    zero = jnp.zeros_like(pair)
    return jnp.concatenate(
        [jnp.where(lane < HEAD_SIZE, pair, zero), jnp.where(lane < HEAD_SIZE, zero, pair)], axis=0
    )


def join_heads(both, count):
    row = lax.broadcasted_iota(jnp.int32, (both.shape[0], count), 0)
    return jnp.where(row < HEAD_SIZE, both[:, :count], both[:, count:]).T


def set_bias(flags_ref, bias):
    blocks, size = flags_ref.shape[0], flags_ref.shape[3]
    asked = segment_of(flags_ref[0, 0])
    for j in range(blocks):
        keys = column(segment_of(flags_ref[j, 0]))
        bias[pl.ds(j * size, size), :] = jnp.where((keys == asked) & (keys > 0.0), 0.0, FLOOR_SCORE)


def attend_kernel(q_ref, k_ref, v_ref, flags_ref, mix_ref, full_ref, lse_ref, bias, held):
    count, blocks, size = q_ref.shape[1], k_ref.shape[0], k_ref.shape[2]

    @pl.when(pl.program_id(1) == 0)
    def _():
        set_bias(flags_ref, bias)

    live = segment_of(flags_ref[0, 0]) > 0.0
    live = jnp.concatenate([live, live], axis=1)
    for u in range(PAIRS):
        lanes = slice(u * LANES, (u + 1) * LANES)
        asked = split_heads(q_ref[0, :, lanes])
        top = None
        for j in range(blocks):
            rows = pl.ds(j * size, size)
            part = bias[rows, :]
            scores = dot(k_ref[j, 0, :, lanes], asked, 1, 1) + jnp.concatenate([part, part], axis=1)
            held[u % 2, rows, :] = scores
            high = jnp.max(scores, axis=0, keepdims=True)
            top = high if top is None else jnp.maximum(top, high)
        total, mixed = 0.0, 0.0
        for j in range(blocks):
            weights = jnp.exp(held[u % 2, pl.ds(j * size, size), :] - top)
            total = total + jnp.sum(weights, axis=0, keepdims=True)
            mixed = mixed + dot(v_ref[j, 0, :, lanes].T, weights.astype(BF16), 1, 0)
        result = join_heads(mixed * jnp.where(live, 1.0 / total, 0.0), count)
        mix_ref[0, :, lanes] = result.astype(BF16)
        full_ref[0, :, lanes] = result
        lse_ref[0, u] = jnp.where(live, top + jnp.log(total), 0.0)


def attend_back_kernel(
    q_ref, k_ref, v_ref, dm_ref, full_ref, lse_ref, flags_ref,
    dq_ref, dk_ref, dv_ref, qsum_ref, vsum_ref, bias,
):
    count, blocks, size = q_ref.shape[1], k_ref.shape[0], k_ref.shape[2]

    @pl.when(pl.program_id(0) == 0)
    def _():
        set_bias(flags_ref, bias)

    for u in range(PAIRS_BACK):
        lanes = slice(u * LANES, (u + 1) * LANES)
        d_mixed = dm_ref[0, :, lanes]
        asked, pulled = split_heads(q_ref[0, :, lanes]), split_heads(d_mixed)
        product = (d_mixed.astype(F32) * full_ref[0, :, lanes]).T
        delta = jnp.concatenate(
            [
                jnp.sum(product[:HEAD_SIZE], axis=0, keepdims=True),
                jnp.sum(product[HEAD_SIZE:], axis=0, keepdims=True),
            ],
            axis=1,
        )
        lse = lse_ref[0, u]
        d_query, v_sum = 0.0, 0.0
        for j in range(blocks):
            keys = k_ref[j, 0, :, lanes]
            part = bias[pl.ds(j * size, size), :]
            scores = dot(keys, asked, 1, 1) + jnp.concatenate([part, part], axis=1)
            probs = jnp.exp(scores - lse)
            d_probs = dot(v_ref[j, 0, :, lanes], pulled, 1, 1)
            d_scores = (probs * (d_probs - delta)).astype(BF16)
            d_value = dot(probs.astype(BF16), pulled, 1, 0)
            dv_ref[j, 0, :, lanes] = d_value.astype(BF16)
            dk_ref[j, 0, :, lanes] = dot(d_scores, asked, 1, 0).astype(BF16)
            v_sum = v_sum + jnp.sum(d_value, axis=0, keepdims=True)
            d_query = d_query + dot(keys.T, d_scores, 1, 0)
        d_query = join_heads(d_query, count) * HEAD_SIZE**-0.5
        dq_ref[0, :, lanes] = d_query.astype(BF16)
        qsum_ref[0, u] = jnp.sum(d_query, axis=0, keepdims=True)
        vsum_ref[0, u] = v_sum


def attend(queries, key_values, flags):
    rows, count, width = queries.shape
    blocks, _, size, _ = key_values.shape
    pairs = width // LANES
    tile = pl.BlockSpec((1, count, PAIRS * LANES), lambda r, p: (r, 0, p))
    steps = pairs // PAIRS
    area = rows * count * blocks * size
    return pl.pallas_call(
        attend_kernel,
        grid=(rows, steps),
        in_specs=[
            tile,
            pl.BlockSpec((blocks, 1, size, PAIRS * LANES), lambda r, p: (0, r, 0, p)),
            pl.BlockSpec((blocks, 1, size, PAIRS * LANES), lambda r, p: (0, r, 0, steps + p)),
            pl.BlockSpec((blocks, 1, 1, size), lambda r, p: (0, r, 0, 0)),
        ],
        out_specs=[tile, tile, pl.BlockSpec((1, PAIRS, 1, 2 * count), lambda r, p: (r, p, 0, 0))],
        out_shape=[
            shaped(BF16, *queries.shape),
            placed(F32, *queries.shape),
            shaped(F32, rows, pairs, 1, 2 * count),
        ],
        scratch_shapes=[
            pltpu.VMEM((blocks * size, count), F32),
            pltpu.VMEM((2, blocks * size, 2 * count), F32),
        ],
        compiler_params=parameters(),
        cost_estimate=cost(16 * area * width, 8 * rows * blocks * size * width, area * 12),
        name="attend",
    )(far(queries), far(key_values), far(key_values), flags)


def attend_back(row, held, queries, key_values, d_mixed, mixed_full, lse, flags, after):
    rows, count, width = queries.shape
    blocks, _, size, _ = key_values.shape
    pairs = width // LANES
    tile = pl.BlockSpec((1, count, PAIRS_BACK * LANES), lambda p: (row, 0, p))
    steps = pairs // PAIRS_BACK
    keys = pl.BlockSpec((blocks, 1, size, PAIRS_BACK * LANES), lambda p: (0, row, 0, p))
    line = lambda w: pl.BlockSpec((1, PAIRS_BACK, 1, w), lambda p: (row, p, 0, 0))
    area = count * blocks * size
    grads = placed(BF16, blocks, rows, size, width)
    sums = shaped(F32, rows, pairs, 1, LANES)
    given = [queries, key_values, key_values, d_mixed, mixed_full, lse, flags]
    extra = [*(held or []), *after]

    def kernel(*refs):
        attend_back_kernel(*refs[: len(given)], *refs[len(given) + len(extra) :])

    return pl.pallas_call(
        kernel,
        grid=(steps,),
        in_specs=[
            tile, keys, pl.BlockSpec((blocks, 1, size, PAIRS_BACK * LANES), lambda p: (0, row, 0, steps + p)),
            tile, tile, line(2 * count), pl.BlockSpec((blocks, 1, 1, size), lambda p: (0, row, 0, 0)),
            *[ANYWHERE] * len(extra),
        ],
        out_specs=[tile, keys, keys, line(LANES), line(LANES)],
        out_shape=[placed(BF16, *queries.shape), grads, grads, sums, sums],
        scratch_shapes=[pltpu.VMEM((blocks * size, count), F32)],
        input_output_aliases={len(given) + i: i for i in range(len(held or []))},
        compiler_params=parameters(),
        cost_estimate=cost(32 * area * width, 16 * blocks * size * width, area * 12),
        name=f"attend_back_{row}",
    )(*given, *extra)


def project(near, sources, flags, left, left_other, right, right_other):
    own, width = sources[0].shape
    blocks, row_count, _, size = flags.shape
    total, steps = own * blocks, blocks
    halves, depth, part = left.shape
    half = width // 2

    def kernel(near_ref, *refs):
        first_ref, ahead_ref, lm_ref, lo_ref, rm_ref, ro_ref = refs[blocks : blocks + 6]
        rows_out, turned_ref, q_ref, kv_ref, w_out, vec_ref = refs[blocks + 6 : blocks + 12]
        rows, weights, normed, columns, sems, out_sems = refs[blocks + 12 :]
        step = pl.program_id(0)
        outward = [
            pltpu.make_async_copy(rows, rows_out, out_sems.at[0]),
            pltpu.make_async_copy(weights, w_out, out_sems.at[1]),
        ]

        def norm(at, slot, flags_ref):
            gain, shift = vec_ref[GAIN1 : GAIN1 + 1], vec_ref[SHIFT1 : SHIFT1 + 1]
            embed = vec_ref[EMBED : EMBED + 1]
            for r in range(row_count):
                masked = column(flags_ref[0, r]) >= MASKED
                here = rows[pl.ds(pl.multiple_of(at * own + r * size, size), size), :].astype(F32)
                hat, _ = norm_parts(jnp.where(masked, embed, here))
                normed[slot, r * size : (r + 1) * size, :] = (hat * gain + shift).astype(BF16)

        @pl.when(step == 0)
        def _():
            near_place = near_ref[0]
            later, first = [], []
            for which in range(2):
                mine = near_place if which == 0 else 1 - near_place
                low, high = (lm_ref, rm_ref) if which == 0 else (lo_ref, ro_ref)
                for x in range(halves):
                    at = pl.ds(pl.multiple_of(x * 2 * depth + mine * depth, depth), depth)
                    first.append((high.at[x, :, pl.ds(part, LANES)], columns.at[at, :]))
                    for side, source in enumerate((low, high)):
                        for kind in range(4):
                            later.append(
                                (
                                    source.at[x, :, pl.ds(kind * half, half)],
                                    weights.at[at, pl.ds(kind * width + side * half, half)],
                                )
                            )
            first += [(refs[i], rows.at[pl.ds(i * own, own), :]) for i in range(blocks)]
            copies = [
                pltpu.make_async_copy(a, b, sems.at[i]) for i, (a, b) in enumerate([*first, *later])
            ]
            for copy in copies:
                copy.start()
            for copy in copies[: len(first)]:
                copy.wait()
            outward[0].start()
            vec_ref[...] = columns[...].astype(F32).T[:KINDS]
            norm(0, 0, first_ref)
            for copy in copies[len(first) :]:
                copy.wait()
            outward[1].start()

        slot = lax.rem(step, 2)
        here = normed[slot]
        kv_ref[:, :width] = dot(here, weights[:, width : 2 * width], 1, 0).astype(BF16)
        values = dot(here, weights[:, 2 * width : 3 * width], 1, 0)
        kv_ref[:, width:] = (values + vec_ref[VBIAS : VBIAS + 1]).astype(BF16)
        turned_ref[...] = here.T
        norm(jnp.minimum(step + 1, steps - 1), 1 - slot, ahead_ref)

        @pl.when(step == 0)
        def _():
            asked = dot(here, weights[:, :width], 1, 0) + vec_ref[QBIAS : QBIAS + 1]
            q_ref[...] = (asked * HEAD_SIZE**-0.5).astype(BF16)

        @pl.when(step == steps - 1)
        def _():
            for copy in outward:
                copy.wait()

    def ahead(t, _):
        return (jnp.minimum(t + 1, steps - 1), 0, 0, 0)

    return pl.pallas_call(
        kernel,
        grid_spec=pltpu.PrefetchScalarGridSpec(
            num_scalar_prefetch=1,
            grid=(steps,),
            in_specs=[
                *[ANYWHERE] * blocks,
                whole(1, row_count, 1, size),
                pl.BlockSpec((1, row_count, 1, size), ahead),
                *[ANYWHERE] * 4,
            ],
            out_specs=[
                ANYWHERE,
                pl.BlockSpec((width, own), lambda t, _: (0, t)),
                whole(own, width),
                pl.BlockSpec((own, 2 * width), lambda t, _: (t, 0)),
                ANYWHERE,
                whole(KINDS, width),
            ],
            scratch_shapes=[
                pltpu.VMEM((total, width), BF16),
                pltpu.VMEM((width, 4 * width), BF16),
                pltpu.VMEM((2, own, width), BF16),
                pltpu.VMEM((width, LANES), BF16),
                pltpu.SemaphoreType.DMA((18 * halves + blocks,)),
                pltpu.SemaphoreType.DMA((2,)),
            ],
        ),
        out_shape=[
            placed(BF16, total, width),
            placed(BF16, width, total),
            placed(BF16, own, width),
            placed(BF16, total, 2 * width),
            placed(BF16, width, 4 * width),
            shaped(F32, KINDS, width),
        ],
        compiler_params=parameters(40),
        cost_estimate=cost(5 * total * width * width, 8 * total * width + 16 * width * width, total),
        name="project",
    )(near, *sources, flags, flags, left, left_other, right, right_other)


def open_branch(mixed, rows_all, flags, vectors, weights):
    tokens, width = mixed.shape
    _, row_count, _, size = flags.shape

    def kernel(mixed_ref, rows_ref, flags_ref, vec_ref, w_ref, normed_ref, middle_ref):
        masked = column(flags_ref[0, 0]) >= MASKED
        embed, bias = vec_ref[EMBED : EMBED + 1], vec_ref[OBIAS : OBIAS + 1]
        gain, shift = vec_ref[GAIN2 : GAIN2 + 1], vec_ref[SHIFT2 : SHIFT2 + 1]
        added = dot(mixed_ref[...], w_ref[...], 1, 0)
        for c in range(0, size, CHUNK):
            cut = slice(c, c + CHUNK)
            values = jnp.where(masked[cut], embed, rows_ref[cut].astype(F32))
            middle = values + added[cut] + bias
            middle_ref[cut] = middle
            hat, _ = norm_parts(middle)
            normed_ref[cut] = (hat * gain + shift).astype(BF16)

    tile = pl.BlockSpec((size, width), lambda t: (t, 0))
    return pl.pallas_call(
        kernel,
        grid=(row_count,),
        in_specs=[
            tile, tile, pl.BlockSpec((1, 1, 1, size), lambda t: (0, t, 0, 0)), whole(KINDS, width),
            pl.BlockSpec((width, width), lambda t: (0, 3)),
        ],
        out_specs=[tile, tile],
        out_shape=[placed(BF16, tokens, width), placed(F32, tokens, width)],
        compiler_params=parameters(),
        cost_estimate=cost(2 * tokens * width * width, 10 * tokens * width),
        name="open_branch",
    )(mixed, rows_all, flags, vectors, weights)


def branch(places, normed, normed_other, pulled, pulled_other, vectors, rest):
    tokens, width = normed.shape
    groups = rest.shape[1] // 2
    cores, length = rest.shape[0], rest.shape[2]
    depth = length // 2
    both = 2 * tokens
    size = both

    def kernel(
        places_ref, n_ref, no_ref, c_ref, co_ref, vec_ref, down_ref, up_ref,
        total_ref, dn_ref, away_ref, sdown_ref, kdown_ref, gup_ref, gbias_ref,
        normed_all, turned, pulled_all, totals, d_normed, activated, d_hidden, up, down,
    ):
        step = pl.program_id(0)

        @pl.when(step == 0)
        def _():
            normed_all[:tokens] = n_ref[...]
            normed_all[tokens:] = no_ref[...]
            turned[:, :tokens] = n_ref[...].T
            turned[:, tokens:] = no_ref[...].T
            pulled_all[:tokens] = c_ref[...]
            pulled_all[tokens:] = co_ref[...]

        at = 0
        for x in range(2):
            for core in range(cores):
                up[at : at + depth] = up_ref[core, 0, x * depth : (x + 1) * depth]
                down[at : at + depth] = down_ref[core, 0, x * depth : (x + 1) * depth]
                at += depth
        bias = vec_ref[pl.ds(UBIAS + groups * places_ref[0] + step, 1), :]
        bias_grad = 0.0
        for c in range(0, both, size):
            cut = slice(c, c + size)
            hidden = dot(normed_all[cut], up[...], 1, 0) + bias
            d_active = dot(pulled_all[cut], down[...], 1, 1)
            phi = 0.5 * (1.0 + lax.erf(hidden * HALF_ROOT))
            slope = phi + hidden * (0.3989422804014327 * jnp.exp(-0.5 * hidden * hidden))
            activated[cut] = (hidden * phi).astype(BF16)
            grad = (d_active * slope).astype(BF16)
            d_hidden[cut] = grad
            bias_grad += jnp.sum(grad.astype(F32), axis=0, keepdims=True)
        gbias_ref[0] = bias_grad
        for c in range(0, both, size):
            cut = slice(c, c + size)
            more = dot(activated[cut], down[...], 1, 0)
            more_back = dot(d_hidden[cut], up[...], 1, 1)

            @pl.when(step == 0)
            def _(cut=cut, more=more, more_back=more_back):
                totals[cut] = more
                d_normed[cut] = more_back

            @pl.when(step > 0)
            def _(cut=cut, more=more, more_back=more_back):
                totals[cut] += more
                d_normed[cut] += more_back

        gup_ref[0] = dot(turned[...], d_hidden[...], 1, 0).astype(BF16)
        grads = dot(activated[...], pulled_all[...], 0, 0).astype(BF16)
        (sent,), (kept,) = parted(grads, places_ref[1], length)
        for core in range(cores):
            sdown_ref[0, core] = sent[core * depth : (core + 1) * depth]
            kdown_ref[0, core] = kept[core * depth : (core + 1) * depth]

        @pl.when(step == pl.num_programs(0) - 1)
        def _():
            total_ref[...] = totals[:tokens]
            dn_ref[...] = d_normed[:tokens]
            away_ref[0] = totals[tokens:].astype(BF16)
            away_ref[1] = d_normed[tokens:].astype(BF16)

    weight = lambda f: pl.BlockSpec((cores, 1, length, width), lambda k, _: (0, f(k), 0, 0))
    piece = pl.BlockSpec((1, cores, depth, width), lambda k, _: (k, 0, 0, 0))
    square = pl.BlockSpec((1, width, width), lambda k, _: (k, 0, 0))
    patch = whole(tokens, width)
    return pl.pallas_call(
        kernel,
        grid_spec=pltpu.PrefetchScalarGridSpec(
            num_scalar_prefetch=1,
            grid=(groups,),
            in_specs=[
                patch, patch, patch, patch, whole(KINDS, width), weight(lambda k: k),
                weight(lambda k: groups + k),
            ],
            out_specs=[
                patch, patch, whole(2, tokens, width), piece, piece, square,
                pl.BlockSpec((1, 1, width), lambda k, _: (k, 0, 0)),
            ],
            scratch_shapes=[
                pltpu.VMEM((both, width), BF16),
                pltpu.VMEM((width, both), BF16),
                pltpu.VMEM((both, width), BF16),
                pltpu.VMEM((both, width), F32),
                pltpu.VMEM((both, width), F32),
                pltpu.VMEM((both, width), BF16),
                pltpu.VMEM((both, width), BF16),
                pltpu.VMEM((width, width), BF16),
                pltpu.VMEM((width, width), BF16),
            ],
        ),
        out_shape=[
            placed(F32, tokens, width),
            placed(F32, tokens, width),
            placed(BF16, 2, tokens, width),
            placed(BF16, groups, cores, depth, width),
            placed(BF16, groups, cores, depth, width),
            placed(BF16, groups, width, width),
            shaped(F32, groups, 1, width),
        ],
        compiler_params=parameters(52),
        cost_estimate=cost(
            12 * groups * both * width * width, 20 * width * width, 2 * both * width * groups
        ),
        name="branch",
    )(places, normed, normed_other, pulled, pulled_other, vectors, rest, rest)


def between(near, d_normed, d_normed_other, middle, pulled, vectors, mixed, weights, halves):
    tokens, width = mixed.shape
    depth = width // (2 * halves)
    size = tokens // 2

    def kernel(
        near_ref, dn_ref, more_ref, middle_ref, cot_ref, vec_ref, mixed_ref, w_ref,
        dmiddle_ref, dmixed_ref, sent_ref, kept_ref, sums_ref, d_attn, grads,
    ):
        step = pl.program_id(0)
        gain = vec_ref[GAIN2 : GAIN2 + 1]
        sums = 0.0
        for c in range(0, size, CHUNK):
            cut = slice(c, c + CHUNK)
            d_out = dn_ref[cut] + more_ref[0, cut].astype(F32)
            cot = cot_ref[cut].astype(F32)
            hat, rate = norm_parts(middle_ref[cut])
            d_middle = cot + norm_back(d_out * gain, hat, rate)
            dmiddle_ref[cut] = d_middle
            low = d_middle.astype(BF16)
            d_attn[cut] = low
            parts = [low.astype(F32), d_out * hat, d_out, cot]
            sums += jnp.concatenate([jnp.sum(s, axis=0, keepdims=True) for s in parts], axis=0)
        sums = jnp.concatenate([sums, jnp.zeros_like(sums)], axis=0)
        dmixed_ref[...] = dot(d_attn[...], w_ref[...], 1, 1).astype(BF16)
        more = dot(mixed_ref[...], d_attn[...], 0, 0)

        @pl.when(step == 0)
        def _():
            sums_ref[...] = sums
            grads[...] = more

        @pl.when(step == 1)
        def _():
            sums_ref[...] += sums
            value = (grads[...] + more).astype(BF16)
            for x, (sent, kept) in enumerate(zip(*parted(value, near_ref[0], depth), strict=True)):
                sent_ref[x] = sent
                kept_ref[x] = kept

    tile = pl.BlockSpec((size, width), lambda t, _: (t, 0))
    piece = whole(halves, depth, width)
    return pl.pallas_call(
        kernel,
        grid_spec=pltpu.PrefetchScalarGridSpec(
            num_scalar_prefetch=1,
            grid=(2,),
            in_specs=[
                tile, pl.BlockSpec((1, size, width), lambda t, _: (1, t, 0)), tile, tile,
                whole(KINDS, width), tile, pl.BlockSpec((width, width), lambda t, _: (0, 3)),
            ],
            out_specs=[tile, tile, piece, piece, whole(8, width)],
            scratch_shapes=[pltpu.VMEM((size, width), BF16), pltpu.VMEM((width, width), F32)],
        ),
        out_shape=[
            placed(F32, tokens, width),
            shaped(BF16, tokens, width),
            placed(BF16, halves, depth, width),
            placed(BF16, halves, depth, width),
            shaped(F32, 8, width),
        ],
        compiler_params=parameters(),
        cost_estimate=cost(4 * tokens * width * width, 16 * tokens * width),
        name="between",
    )(near, d_normed, d_normed_other, middle, pulled, vectors, mixed, far(weights))


def weight_grads(near, turned, d_key, d_value, d_query, halves, after):
    width, total = turned.shape
    own = d_query.shape[0]
    depth = width // (2 * halves)

    def kernel(near_ref, turned_ref, dk_ref, dv_ref, dq_ref, *refs):
        sa_ref, ka_ref, sb_ref, kb_ref = refs[len(after) :]
        step = pl.program_id(0)

        def put(value, sent_ref, kept_ref, at):
            pieces = zip(*parted(value.astype(BF16), near_ref[0], depth), strict=True)
            for x, (sent, kept) in enumerate(pieces):
                sent_ref[x, :, at : at + width] = sent
                kept_ref[x, :, at : at + width] = kept

        @pl.when(step == 0)
        def _():
            put(dot(turned_ref[:, :own], dq_ref[...], 1, 0), sa_ref, ka_ref, 0)

        @pl.when(step == 1)
        def _():
            put(dot(turned_ref[...], dk_ref[...], 1, 0), sa_ref, ka_ref, width)

        @pl.when(step == 2)
        def _():
            put(dot(turned_ref[...], dv_ref[...], 1, 0), sb_ref, kb_ref, 0)

    pair, single = whole(halves, depth, 2 * width), whole(halves, depth, width)
    return pl.pallas_call(
        kernel,
        grid_spec=pltpu.PrefetchScalarGridSpec(
            num_scalar_prefetch=1,
            grid=(3,),
            in_specs=[
                whole(width, total), whole(total, width), whole(total, width), whole(own, width),
                *[ANYWHERE] * len(after),
            ],
            out_specs=[pair, pair, single, single],
        ),
        out_shape=[
            placed(BF16, halves, depth, 2 * width),
            placed(BF16, halves, depth, 2 * width),
            placed(BF16, halves, depth, width),
            placed(BF16, halves, depth, width),
        ],
        compiler_params=parameters(36),
        cost_estimate=cost(5 * total * width * width, 8 * total * width + 12 * width * width),
        name="weight_grads",
    )(near, turned, d_key, d_value, d_query, *after)


def first_norm(
    near, d_key, d_value, d_query, rows_all, flags, vectors, weights, d_middle, sums, gbias, qsum, vsum, halves, after,
):
    total, width = rows_all.shape
    blocks, row_count, _, size = flags.shape
    own = d_query.shape[0]
    depth = width // (2 * halves)
    groups = gbias.shape[0]

    def kernel(near_ref, *refs):
        (
            dk_ref, dv_ref, dq_ref, rows_ref, flags_ref, vec_ref, w_ref, dmiddle_ref, sums_ref,
            gbias_ref, qsum_ref, vsum_ref,
        ) = refs[:12]
        far_ref, near_share_ref, own_ref, sent_ref, kept_ref, totals = refs[12 + len(after) :]
        step = pl.program_id(0)

        def put_share(step, cut, value):
            @pl.when(step < blocks // 2)
            def _():
                far_ref[0, cut] = value

            @pl.when(step >= blocks // 2)
            def _():
                near_share_ref[0, cut] = value

        def one(mine):
            d_all = dot(dk_ref[...], w_ref[:, width : 2 * width], 1, 1)
            d_all += dot(dv_ref[...], w_ref[:, 2 * width :], 1, 1)
            if mine:
                d_all += dot(dq_ref[...], w_ref[:, :width], 1, 1)
            gain, embed = vec_ref[GAIN1 : GAIN1 + 1], vec_ref[EMBED : EMBED + 1]
            more = 0.0
            for r in range(row_count):
                cut = slice(r * size, (r + 1) * size)
                masked = column(flags_ref[0, r]) >= MASKED
                d_normed = d_all[cut]
                hat, rate = norm_parts(jnp.where(masked, embed, rows_ref[cut].astype(F32)))
                d_embedded = norm_back(d_normed * gain, hat, rate)
                if mine:
                    d_embedded = d_embedded + dmiddle_ref[cut]
                    own_ref[cut] = d_embedded
                else:
                    put_share(step, cut, d_embedded.astype(BF16))
                parts = [jnp.where(masked, d_embedded, 0.0), d_normed * hat, d_normed]
                more += jnp.concatenate([jnp.sum(s, axis=0, keepdims=True) for s in parts], axis=0)
            return more

        @pl.when(step == 0)
        def _():
            totals[:3] = one(True)

        @pl.when(step > 0)
        def _():
            totals[:3] += one(False)

        @pl.when(step == blocks - 1)
        def _():
            def line(ref):
                rows, pairs = ref.shape[0], ref.shape[1]
                return sum(
                    jnp.concatenate([ref[r, p] for p in range(pairs)], axis=1) for r in range(rows)
                )

            bias = jnp.concatenate([gbias_ref[k] for k in range(groups)], axis=0)
            none = jnp.zeros_like(bias)
            low = near_ref[0] == 0
            kinds = [
                totals[:3], line(qsum_ref), line(vsum_ref), sums_ref[:4],
                jnp.where(low, bias, none), jnp.where(low, none, bias),
            ]
            kinds.append(jnp.zeros((LANES - UBIAS - 2 * groups, width), F32))
            small = jnp.concatenate(kinds, axis=0).T.astype(BF16)
            for x, (sent, kept) in enumerate(zip(*parted(small, near_ref[0], depth), strict=True)):
                sent_ref[x] = sent
                kept_ref[x] = kept

    tile = pl.BlockSpec((own, width), lambda t, _: (t, 0))
    piece = whole(halves, depth, LANES)
    return pl.pallas_call(
        kernel,
        grid_spec=pltpu.PrefetchScalarGridSpec(
            num_scalar_prefetch=1,
            grid=(blocks,),
            in_specs=[
                tile, tile, whole(own, width), tile,
                pl.BlockSpec((1, row_count, 1, size), lambda t, _: (t, 0, 0, 0)),
                whole(KINDS, width), whole(width, 3 * width), whole(own, width),
                whole(*sums.shape), whole(*gbias.shape), whole(*qsum.shape), whole(*vsum.shape),
                *[ANYWHERE] * len(after),
            ],
            out_specs=[
                pl.BlockSpec((1, own, width), lambda t, _: (jnp.clip(t - 1, 0, blocks // 2 - 2), 0, 0)),
                pl.BlockSpec((1, own, width), lambda t, _: (jnp.maximum(t - blocks // 2, 0), 0, 0)),
                whole(own, width), piece, piece,
            ],
            scratch_shapes=[pltpu.VMEM((8, width), F32)],
        ),
        out_shape=[
            placed(BF16, blocks // 2 - 1, own, width),
            placed(BF16, blocks // 2, own, width),
            placed(F32, own, width),
            shaped(BF16, halves, depth, LANES),
            shaped(BF16, halves, depth, LANES),
        ],
        compiler_params=parameters(36),
        cost_estimate=cost(5 * total * width * width, 8 * total * width + 12 * width * width, total),
        name="first_norm",
    )(near, far(d_key), far(d_value), d_query, rows_all, flags, vectors, weights, d_middle, sums, gbias, qsum, vsum, *after)


def after(value, *others):
    return lax.optimization_barrier((value, *others))[0]


class Links:
    def __init__(self, seq, rows):
        self.sizes = {"seq": seq, "rows": rows}
        order = []
        for axis in EVERY:
            mask = self.sizes[axis] // 2
            while mask:
                order.append((axis, mask))
                mask //= 2
        self.order = order
        place = {axis: lax.axis_index(axis) for axis in EVERY}
        self.value = {(a, m): ((place[a] // m) % 2).astype(jnp.int32) for a, m in order}
        self.near = ("seq", 1)
        self.first = ("seq", 2)
        self.second = ("rows", 1)
        self.others = [b for b in order if b[0] == "rows" and b[1] > 1]

    def swap(self, array, bit):
        axis, mask = bit
        return lax.ppermute(array, axis, [(i, i ^ mask) for i in range(self.sizes[axis])])

    def pick(self, array, bit, other=False, axis=0):
        at = 1 - self.value[bit] if other else self.value[bit]
        return lax.dynamic_index_in_dim(array, at, axis, keepdims=False)

    def gather(self, shard, bits, wanted):
        held, have = shard, []
        for i, bit in enumerate(bits):
            if i in wanted:
                held = after(held, *wanted[i])
            have = sorted([*have, bit], key=self.order.index)
            parts = held.reshape(2 ** have.index(bit), -1, held.shape[-1])
            other = self.swap(held, bit).reshape(parts.shape)
            upper = self.value[bit] == 1
            low = jnp.where(upper, other, parts)
            high = jnp.where(upper, parts, other)
            held = jnp.stack([low, high], axis=1).reshape(-1, held.shape[-1])
        return held

    def half(self, held, have, bit, other):
        before = 1
        for key in have[: have.index(bit)]:
            before *= key if isinstance(key, int) else 2
        parts = held.reshape(before, 2, -1, held.shape[-1])
        return self.pick(parts, bit, other, 1).reshape(-1, held.shape[-1])

    def add(self, kept, came, have, bit):
        def part(other):
            first, second = (self.half(a, have, bit, other) for a in (kept, came))
            return (first.astype(F32) + second.astype(F32)).astype(BF16)

        return part(True), part(False), [b for b in have if b != bit]


def body(
    patches, segments, masked, mask_embedding, norm1_gain, norm1_bias, qkv_weight, query_bias,
    value_bias, out_weight, out_bias, norm2_gain, norm2_bias, up_weight, up_bias, down_weight,
    down_bias, cotangent, *, seq, rows,
):
    links = Links(seq, rows)
    row_count, patch_count, width = patches.shape
    tokens = row_count * patch_count
    n = qkv_weight.shape[0]
    devices = seq * rows
    groups = up_weight.shape[1] // width
    mine = groups // 2
    half = width // 2
    halves = seq // 2
    depth = rows * n
    near, first, second, others = links.near, links.first, links.second, links.others
    near_place = links.value[near].reshape(1)

    packed = jnp.stack(
        [
            down_weight.reshape(2, mine, n, width),
            up_weight.reshape(n, devices, groups, n).transpose(2, 0, 1, 3).reshape(2, mine, n, width),
        ],
        axis=1,
    ).reshape(2, 2 * mine, n, width)
    packed_kept, packed_sent = links.pick(packed, near), links.pick(packed, near, True)
    packed_came = links.swap(packed_sent, near)

    flags = (segments + MASKED * masked).astype(BF16).reshape(1, row_count, patch_count)
    sources = [after(patches.reshape(tokens, width), packed_sent)]
    for bit in (first, near):
        flags = jnp.concatenate([flags, links.swap(flags, bit)], axis=0)
        sources += [links.swap(source, bit) for source in sources]
    early_ones, late_ones = [sources[1], flags], sources[2:]
    flags = flags.astype(F32).reshape(seq, row_count, 1, patch_count)
    small = [
        mask_embedding, norm1_gain, norm1_bias, query_bias, value_bias, out_bias, norm2_gain,
        norm2_bias, down_bias,
    ]
    columns = jnp.concatenate([jnp.stack(small), up_bias.reshape(groups, n)], axis=0).T
    columns = jnp.pad(columns, ((0, 0), (0, LANES - columns.shape[1])))
    fourths = [qkv_weight[:, i * half : (i + 1) * half] for i in range(6)]
    fourths += [out_weight[:, :half], out_weight[:, half:]]
    left = jnp.concatenate(fourths[::2], axis=1)
    right = jnp.concatenate([*fourths[1::2], columns], axis=1)
    left = links.gather(left, [*others, second, first], {2: early_ones, 3: late_ones}).reshape(halves, depth, -1)
    right = links.gather(right, [*others, first, second], {}).reshape(halves, depth, -1)
    left_other, right_other = links.swap(left, near), links.swap(right, near)

    low = links.value[near] == 0
    packed = jnp.stack([jnp.where(low, packed_kept, packed_came), jnp.where(low, packed_came, packed_kept)], axis=0)
    same_core = [
        [(x * 2 + core) * rows + r for x in range(halves) for r in range(rows)] for core in range(2)
    ]
    rest = lax.all_gather(packed, EVERY, axis=2, tiled=True, axis_index_groups=same_core)

    rows_all, turned, queries, key_values, weights, vectors = project(
        near_place, sources, flags, left, left_other, right, right_other
    )
    queries = queries.reshape(row_count, patch_count, width)
    key_values = key_values.reshape(seq, row_count, patch_count, 2 * width)
    mixed, mixed_full, lse = attend(queries, key_values, flags)
    mixed = mixed.reshape(tokens, width)
    d_branch = cotangent.reshape(tokens, width)
    d_branch_other = links.swap(d_branch, near)
    normed_two, middle = open_branch(mixed, rows_all, flags, vectors, weights)
    places = jnp.stack([links.value[near], links.value[first]])
    added, d_normed, away, down_sent, down_kept, grad_up, grad_up_bias = branch(
        places, normed_two, links.swap(normed_two, near), d_branch, d_branch_other, vectors, rest
    )

    row_bits = [*others, second]
    have = [first, *row_bits]
    flat = lambda held: held.reshape(-1, held.shape[-1])
    down_sent, down_kept = flat(down_sent), flat(down_kept)
    up_order = [mine, first, near, *row_bits]
    grad_up = flat(grad_up)
    up_sent = links.half(grad_up, up_order, second, True)
    up_kept = links.half(grad_up, up_order, second, False)
    up_order = [mine, first, near, *others]
    away = links.swap(away, near)
    down_came, up_came = links.swap(down_sent, first), links.swap(up_sent, second)
    d_middle, d_mixed, out_sent, out_kept, sums = between(
        near_place, d_normed, away, middle, d_branch, vectors, mixed, weights, halves
    )
    out_came = links.swap(out_sent, near)
    d_mixed = d_mixed.reshape(row_count, patch_count, width)

    given = (queries, key_values, d_mixed, mixed_full, lse, flags)
    grads = None
    for row in range(row_count):
        grads = list(attend_back(row, grads, *given, [down_sent, up_sent] if row == 0 else []))
    d_query, d_key, d_value, query_sums, value_sums = grads

    down_sent, down_kept, down_order = links.add(
        after(down_kept, d_query), down_came, [mine, near, *row_bits], second
    )
    down_came = links.swap(down_sent, second)
    up_sent, up_kept, up_order = links.add(after(up_kept, down_sent), up_came, up_order, first)
    up_came = links.swap(up_sent, first)
    d_query = d_query.reshape(tokens, width)
    d_key = d_key.reshape(-1, width)
    d_value = d_value.reshape(-1, width)
    pair_sent, pair_kept, value_sent, value_kept = weight_grads(
        near_place, turned, d_key, d_value, d_query, halves, [down_sent, up_sent]
    )
    early_kept = jnp.concatenate([after(down_kept, pair_sent), up_kept], axis=0)
    early_came = jnp.concatenate([after(down_came, pair_sent), up_came], axis=0)
    early_order = [2 * mine, near, *others]
    early_sent, early_kept, early_order = links.add(early_kept, early_came, early_order, others[-1])
    early = [early_kept, links.swap(early_sent, others[-1]), early_order]
    pair_came = links.swap(flat(after(pair_sent, early_sent)), near)
    value_came = links.swap(flat(after(value_sent, early_sent)), near)
    pair_sent, pair_kept, pair_order = links.add(flat(pair_kept), pair_came, have, second)
    pair_came = links.swap(pair_sent, second)
    last_kept = jnp.concatenate([flat(value_kept), flat(out_kept)], axis=1)
    last_came = jnp.concatenate([value_came, flat(out_came)], axis=1)
    last_sent, last_kept, last_order = links.add(after(last_kept, pair_sent), last_came, have, first)
    last_came = links.swap(last_sent, first)
    far_share, near_share, own, small_sent, small_kept = first_norm(
        near_place, d_key, d_value, d_query, rows_all, flags, vectors, weights, d_middle, sums,
        grad_up_bias, query_sums, value_sums, halves, [early_sent, pair_sent, last_sent],
    )

    pair = [pair_kept, pair_came, pair_order]
    last = [last_kept, last_came, last_order]

    def go(item, bit, gone):
        gone, item[0], item[2] = links.add(after(item[0], gone), item[1], item[2], bit)
        item[1] = links.swap(gone, bit)
        return gone

    rest_bits = others[-2::-1]
    gone = own
    for bit in rest_bits:
        gone = go(early, bit, gone)
    gone = go(pair, first, gone)
    gone = go(last, second, gone)
    near_share = links.swap(after(near_share, gone), near)
    small = [flat(small_kept), links.swap(flat(after(small_sent, gone)), near), have]
    gone = go(small, first, gone)
    gone = (after(far_share, gone).astype(F32) + near_share[1:].astype(F32)).astype(BF16)
    far_share = links.swap(gone, first)
    gone = go(small, second, gone)
    gone = go(pair, others[-1], gone)
    output = after(middle, gone) + added + away[0].astype(F32) + vectors[DBIAS]
    output = output.astype(BF16)
    last[0] = jnp.concatenate([after(last[0], output), small[0]], axis=1)
    last[1] = jnp.concatenate([last[1], small[1]], axis=1)
    gone = go(last, others[-1], gone)
    low = links.value[near] == 0
    for i, bit in enumerate(rest_bits):
        gone = go(pair, bit, gone)
        if i == len(rest_bits) - 1:
            early_sum = after(early[0], gone).astype(F32) + early[1].astype(F32)
            early_sum = early_sum.reshape(2 * mine, 2, n, width)
            far_sum = links.pick(early_sum, near, True, 1).astype(BF16)
            far_sum = links.swap(far_sum, near).astype(F32)
            early_sum = links.pick(early_sum, near, False, 1)
            joined = jnp.stack(
                [jnp.where(low, early_sum, far_sum), jnp.where(low, far_sum, early_sum)], axis=0
            )
            down_sum = joined[:, :mine].reshape(-1, width)
            up_sum = joined[:, mine:].reshape(groups, n, devices, n)
            up_sum = up_sum.transpose(1, 2, 0, 3).reshape(n, -1)
            gone = up_sum
        gone = go(last, bit, gone)
    pair, last = (a.astype(F32) + b.astype(F32) for a, b, _ in (pair, last))
    input_grad = after(own, up_sum, gone) + near_share[0].astype(F32) + far_share[0].astype(F32)
    is_masked = masked.reshape(tokens, 1) == 1
    input_grad = jnp.where(is_masked, 0.0, input_grad)
    project_sum = jnp.concatenate([pair, last[:, :width]], axis=1)
    out_sum = last[:, width : 2 * width]
    tail = last[:, 2 * width :].T
    shape = (row_count, patch_count, width)
    return (
        output.reshape(shape), input_grad.reshape(shape), tail[EMBED], tail[GAIN1], tail[SHIFT1],
        project_sum, tail[QBIAS], tail[VBIAS], out_sum, tail[OBIAS], tail[GAIN2], tail[SHIFT2],
        up_sum, tail[UBIAS : UBIAS + groups].reshape(-1), down_sum, tail[DBIAS],
    )


def solution(mesh):
    one, two = P(EVERY), P(EVERY, None)
    rows, flags = P("rows", "seq", None), P("rows", "seq")
    seq, row_groups = mesh.shape["seq"], mesh.shape["rows"]

    def run(*arguments):
        return body(*arguments, seq=seq, rows=row_groups)

    return jax.shard_map(
        run,
        mesh=mesh,
        in_specs=(
            rows, flags, flags, one, one, one, two, one, one, two, one, one, one, two, one, two,
            one, rows,
        ),
        out_specs=(
            rows, rows, one, one, one, two, one, one, two, one, one, one, two, one, two, one,
        ),
        check_vma=False,
    )
```

profile of v0, /device:TPU:0, one launch (start us, length us, event | category | flops | bytes accessed | tf_op | source)
XLA Modules:
  0.0 260.2 jit_solution(1203228486388772780)
XLA Ops:
  11.0 3.0 %collective-permute-start = (bf16[512,768]{1,0:T(8,128)(2,1)S(1)}, bf16[512,768]{1,0:T(8,128)(2,1)S(1)}, u32[]{:S(2)}, u32[]{:S(2)}) collective-permute-start(bf16[512,768]{1,0:T(8,128)(2,1)S(1)} %bitcast.251), channel_id=1, source_target_pairs={{0,16},{8,24},{16,0},{24,8},{1,17},{9,25},{17,1},{25,9},{2,18},{10... | collective-permute-start | bytes 2359304 | tf_op jit(solution)/shard_map/ppermute | solution.py:775
  14.6 2.7 %collective-permute-start.5 = (bf16[24,1536]{1,0:T(8,128)(2,1)S(1)}, bf16[24,1536]{1,0:T(8,128)(2,1)S(1)}, u32[]{:S(2)}, u32[]{:S(2)}) collective-permute-start(bf16[24,1536]{1,0:T(8,128)(2,1)S(1)} %pad_maximum_fusion.16), channel_id=1, source_target_pairs={{0,4},{1,5},{2,6},{3,7},{4,0},{5,1},{6,2},{7,3},{8,12},{9,13},{10,... | collective-permute-start | bytes 221192 | tf_op jit(solution)/shard_map/ppermute | solution.py:775
  18.8 4.1 %collective-permute-done.5 = bf16[24,1536]{1,0:T(8,128)(2,1)S(1)} collective-permute-done((bf16[24,1536]{1,0:T(8,128)(2,1)S(1)}, bf16[24,1536]{1,0:T(8,128)(2,1)S(1)}, u32[]{:S(2)}, u32[]{:S(2)}) %collective-permute-start.5) | collective-permute-done | bytes 73760 | tf_op jit(solution)/shard_map/ppermute | solution.py:775
  27.2 7.0 %collective-permute-done.11 = bf16[48,1664]{1,0:T(8,128)(2,1)S(1)} collective-permute-done((bf16[48,1664]{1,0:T(8,128)(2,1)S(1)}, bf16[48,1664]{1,0:T(8,128)(2,1)S(1)}, u32[]{:S(2)}, u32[]{:S(2)}) %collective-permute-start.11) | collective-permute-done | bytes 159776 | tf_op jit(solution)/shard_map/ppermute | solution.py:775
  38.2 3.1 %collective-permute-done.12 = bf16[96,1664]{1,0:T(8,128)(2,1)S(1)} collective-permute-done((bf16[96,1664]{1,0:T(8,128)(2,1)S(1)}, bf16[96,1664]{1,0:T(8,128)(2,1)S(1)}, u32[]{:S(2)}, u32[]{:S(2)}) %collective-permute-start.12) | collective-permute-done | bytes 319520 | tf_op jit(solution)/shard_map/ppermute | solution.py:775
  44.7 17.9 %collective-permute-done.13 = bf16[192,1664]{1,0:T(8,128)(2,1)S(1)} collective-permute-done((bf16[192,1664]{1,0:T(8,128)(2,1)S(1)}, bf16[192,1664]{1,0:T(8,128)(2,1)S(1)}, u32[]{:S(2)}, u32[]{:S(2)}) %collective-permute-start.13) | collective-permute-done | bytes 639008 | tf_op jit(solution)/shard_map/ppermute | solution.py:775
  63.0 4.6 %collective-permute-done.8 = bf16[192,1536]{1,0:T(8,128)(2,1)S(1)} collective-permute-done((bf16[192,1536]{1,0:T(8,128)(2,1)S(1)}, bf16[192,1536]{1,0:T(8,128)(2,1)S(1)}, u32[]{:S(2)}, u32[]{:S(2)}) %collective-permute-start.8) | collective-permute-done | bytes 589856 | tf_op jit(solution)/shard_map/ppermute | solution.py:775
  69.2 2.6 %collective-permute-done.3 = bf16[1,2,256]{2,1,0:T(2,128)(2,1)S(1)} collective-permute-done((bf16[1,2,256]{2,1,0:T(2,128)(2,1)S(1)}, bf16[1,2,256]{2,1,0:T(2,128)(2,1)S(1)}, u32[]{:S(2)}, u32[]{:S(2)}) %collective-permute-start.3) | collective-permute-done | bytes 1056 | tf_op jit(solution)/shard_map/ppermute | solution.py:775
  73.1 12.0 %project.1 = (bf16[2048,768]{1,0:T(8,128)(2,1)}, bf16[768,2048]{1,0:T(8,128)(2,1)}, bf16[512,768]{1,0:T(8,128)(2,1)}, bf16[2048,1536]{1,0:T(8,128)(2,1)}, bf16[7...) custom-call(s32[1]{0:T(128)} %bitcast.near_ref, bf16[512,768]{1,0:T(8,128)(2,1)S(1)} %bitcast.253, ...), custom_call_target="tpu_custom_call" | custom-call | flops 6039797760 | bytes 22020096 | tf_op jit(solution)/shard_map/project/pallas_call | solution.py:330
  85.2 14.7 %attend.1 = (bf16[2,256,768]{2,1,0:T(8,128)(2,1)S(1)}, f32[2,256,768]{2,1,0:T(8,128)}, f32[2,6,1,512]{3,2,1,0:T(1,128)S(1)}) custom-call(bf16[2,256,768]{2,1,0:T(8,128)(2,1)} %bitcast.267, bf16[4,2,256,1536]{3,2,1,0:T(8,128)(2,1)} %bitcast.257, bf16[4,2,256,1536]{3,2,1,0:T(8,128)(2,1)} %bitcast.258, ...), custom_call_target="tpu_custom_call" | custom-call | flops 6442450944 | bytes 12582912 | tf_op jit(solution)/shard_map/attend/pallas_call | solution.py:190
  99.9 2.5 open_branch.1
  104.9 4.9 %all-gather.2.cloned.1.call-done.down_ref.up_ref = bf16[2,4,384,768]{3,2,1,0:T(8,128)(2,1)} async-done(((bf16[2,4,24,768]{3,2,1,0:T(8,128)(2,1)}), bf16[2,4,384,768]{3,2,1,0:T(8,128)(2,1)}) %all-gather.2.cloned.1.call-update) | async-done | bytes 4718608 | tf_op jit(solution)/shard_map/all_gather | solution.py:864
  110.9 23.0 %branch.1 = (f32[512,768]{1,0:T(8,128)}, f32[512,768]{1,0:T(8,128)}, bf16[2,512,768]{2,1,0:T(8,128)(2,1)}, bf16[2,2,192,768]{3,2,1,0:T(8,128)(2,1)}, bf16[2,2,19...) custom-call(s32[2]{0:T(128)S(1)} %pad_add_fusion.places_ref, ...), custom_call_target="tpu_custom_call" | custom-call | flops 14495514624 | bytes 11796480 | tf_op jit(solution)/shard_map/branch/pallas_call | solution.py:481
  138.3 6.1 %between.1 = (f32[512,768]{1,0:T(8,128)}, bf16[512,768]{1,0:T(8,128)(2,1)S(1)}, bf16[2,192,768]{2,1,0:T(8,128)(2,1)}, bf16[2,192,768]{2,1,0:T(8,128)(2,1)}, f32[8,768]{1,0:T(8,128)S(1)}) custom-call(s32[1]{0:T(128)} %bitcast.near_ref, f32[512,768]{1,0:T(8,128)S(1)} %copy-done.3, bf16[2,512,768]{2,1,0:T(8,128)(2,1)} %collective-permute-done.18.more_ref, ...), custom_call_target="tpu_custom_call" | custom-call | flops 1207959552 | bytes 6291456 | tf_op jit(solution)/shard_map/between/pallas_call | solution.py:565
  144.5 9.9 %attend_back_0.1 = (bf16[2,256,768]{2,1,0:T(8,128)(2,1)}, bf16[4,2,256,768]{3,2,1,0:T(8,128)(2,1)}, bf16[4,2,256,768]{3,2,1,0:T(8,128)(2,1)}, f32[2,6,1,128]{3,2,1,0:T(1,128)S(1)}, f32[2,6,1,128]{3,2,1,0:T(1,128)S(1)}) custom-call(bf16[2,256,768]{2,1,0:T(8,128)(2,1)S(1)} %bitcast.268, bf16[4,2,256,1536]{3,2,1,0:T(8,128)(2,1)S(1)} %bitcast.259, ...), custom_call_target="tpu_custom_call" | custom-call | flops 6442450944 | bytes 12582912 | tf_op jit(solution)/shard_map/attend_back_0/pallas_call | solution.py:232
  154.4 10.1 %attend_back_1.1 = (bf16[2,256,768]{2,1,0:T(8,128)(2,1)}, bf16[4,2,256,768]{3,2,1,0:T(8,128)(2,1)}, bf16[4,2,256,768]{3,2,1,0:T(8,128)(2,1)}, f32[2,6,1,128]{3,2,1,0:T(1,128)S(1)}, f32[2,6,1,128]{3,2,1,0:T(1,128)S(1)}) custom-call(bf16[2,256,768]{2,1,0:T(8,128)(2,1)S(1)} %bitcast.269, ...), custom_call_target="tpu_custom_call", output_to_operand_aliasing={{0}: (7, {}), {1}: (8, {}), {2}: (9, {}), {3}: (10, {}), {4... | custom-call | flops 6442450944 | bytes 12582912 | tf_op jit(solution)/shard_map/attend_back_1/pallas_call | solution.py:232
  168.1 7.9 %weight_grads.1 = (bf16[2,192,1536]{2,1,0:T(8,128)(2,1)}, bf16[2,192,1536]{2,1,0:T(8,128)(2,1)}, bf16[2,192,768]{2,1,0:T(8,128)(2,1)}, bf16[2,192,768]{2,1,0:T(8,128)(2,1)}) custom-call(s32[1]{0:T(128)} %bitcast.near_ref, bf16[768,2048]{1,0:T(8,128)(2,1)S(1)} %copy-done.21, bf16[2048,768]{1,0:T(8,128)(2,1)S(1)} %bitcast.264, ...), custom_call_target="tpu_custom_call" | custom-call | flops 6039797760 | bytes 19660800 | tf_op jit(solution)/shard_map/weight_grads/pallas_call | solution.py:618
  176.1 4.2 %collective-permute-done.21 = bf16[384,768]{1,0:T(8,128)(2,1)S(1)} collective-permute-done((bf16[384,768]{1,0:T(8,128)(2,1)S(1)}, bf16[384,768]{1,0:T(8,128)(2,1)S(1)}, u32[]{:S(2)}, u32[]{:S(2)}) %collective-permute-start.21) | collective-permute-done | bytes 589856 | tf_op jit(solution)/shard_map/ppermute | solution.py:775
  193.1 14.6 %first_norm.1 = (bf16[1,512,768]{2,1,0:T(8,128)(2,1)}, bf16[2,512,768]{2,1,0:T(8,128)(2,1)}, f32[512,768]{1,0:T(8,128)}, bf16[2,192,128]{2,1,0:T(8,128)(2,1)S(1)}, bf16[2,192,128]{2,1,0:T(8,128)(2,1)S(1)}) custom-call(s32[1]{0:T(128)} %bitcast.near_ref, bf16[2048,768]{1,0:T(8,128)(2,1)} %bitcast.263, bf16[2048,768]{1,0:T(8,128)(2,1)} %bitcast.265, ...), custom_call_target="tpu_custom_call" | custom-call | flops 6039797760 | bytes 19660800 | tf_op jit(solution)/shard_map/first_norm/pallas_call | solution.py:720
  216.9 4.3 %collective-permute-done.31 = bf16[192,128]{1,0:T(8,128)(2,1)S(1)} collective-permute-done((bf16[192,128]{1,0:T(8,128)(2,1)S(1)}, bf16[192,128]{1,0:T(8,128)(2,1)S(1)}, u32[]{:S(2)}, u32[]{:S(2)}) %collective-permute-start.31) | collective-permute-done | bytes 49184 | tf_op jit(solution)/shard_map/ppermute | solution.py:775
  230.5 2.5 collective-permute-start.41
  236.3 2.6 reshape.780
  241.3 4.9 %collective-permute-done.40 = bf16[24,1664]{1,0:T(8,128)(2,1)S(1)} collective-permute-done((bf16[24,1664]{1,0:T(8,128)(2,1)S(1)}, bf16[24,1664]{1,0:T(8,128)(2,1)S(1)}, u32[]{:S(2)}, u32[]{:S(2)}) %collective-permute-start.40) | collective-permute-done | bytes 79904 | tf_op jit(solution)/shard_map/ppermute | solution.py:775
  250.1 2.8 %fusion = f32[512,768]{1,0:T(8,128)} fusion(f32[512,768]{1,0:T(8,128)S(1)} %copy-done.23, bf16[2,512,768]{2,1,0:T(8,128)(2,1)} %copy-done.24, bf16[1,512,768]{2,1,0:T(8,128)(2,1)} %collective-permute-done.39, pred[512]{0:T(512)(128)(4,1)S(1)} %eq.47), kind=kLoop, calls=%fused_computation.1 | loop fusion | flops 1966080 | bytes 4719104 | tf_op jit(solution)/shard_map/jit(_where)/select_n | solution.py:980
  (257 shorter events, 72.7 us)
Async XLA Ops:
  7.2 102.6 %all-gather.2.cloned.1.call-start = ((), (), s32[]{:S(2)}) async-start(), calls=%async_computation | async-start | bytes 5013504 | tf_op jit(solution)/shard_map/all_gather | solution.py:864
  11.0 25.7 %collective-permute-start = (bf16[512,768]{1,0:T(8,128)(2,1)S(1)}, bf16[512,768]{1,0:T(8,128)(2,1)S(1)}, u32[]{:S(2)}, u32[]{:S(2)}) collective-permute-start(bf16[512,768]{1,0:T(8,128)(2,1)S(1)} %bitcast.251), channel_id=1, source_target_pairs={{0,16},{8,24},{16,0},{24,8},{1,17},{9,25},{17,1},{25,9},{2,18},{10... | collective-permute-start | bytes 2359304 | tf_op jit(solution)/shard_map/ppermute | solution.py:775
  14.0 29.8 %collective-permute-start.1 = (bf16[512,768]{1,0:T(8,128)(2,1)S(1)}, bf16[512,768]{1,0:T(8,128)(2,1)S(1)}, u32[]{:S(2)}, u32[]{:S(2)}) collective-permute-start(bf16[512,768]{1,0:T(8,128)(2,1)S(1)} %bitcast.252), channel_id=1, source_target_pairs={{0,8},{8,0},{16,24},{24,16},{1,9},{9,1},{17,25},{25,17},{2,10},{10... | collective-permute-start | bytes 2359304 | tf_op jit(solution)/shard_map/ppermute | solution.py:775
  14.6 8.3 %collective-permute-start.5 = (bf16[24,1536]{1,0:T(8,128)(2,1)S(1)}, bf16[24,1536]{1,0:T(8,128)(2,1)S(1)}, u32[]{:S(2)}, u32[]{:S(2)}) collective-permute-start(bf16[24,1536]{1,0:T(8,128)(2,1)S(1)} %pad_maximum_fusion.16), channel_id=1, source_target_pairs={{0,4},{1,5},{2,6},{3,7},{4,0},{5,1},{6,2},{7,3},{8,12},{9,13},{10,... | collective-permute-start | bytes 221192 | tf_op jit(solution)/shard_map/ppermute | solution.py:775
  25.0 9.2 %collective-permute-start.11 = (bf16[48,1664]{1,0:T(8,128)(2,1)S(1)}, bf16[48,1664]{1,0:T(8,128)(2,1)S(1)}, u32[]{:S(2)}, u32[]{:S(2)}) collective-permute-start(bf16[48,1664]{1,0:T(8,128)(2,1)S(1)} %bitcast.323), channel_id=1, source_target_pairs={{0,2},{1,3},{2,0},{3,1},{4,6},{5,7},{6,4},{7,5},{8,10},{9,11},{10,... | collective-permute-start | bytes 479240 | tf_op jit(solution)/shard_map/ppermute | solution.py:775
  25.6 11.1 %collective-permute-start.6 = (bf16[48,1536]{1,0:T(8,128)(2,1)S(1)}, bf16[48,1536]{1,0:T(8,128)(2,1)S(1)}, u32[]{:S(2)}, u32[]{:S(2)}) collective-permute-start(bf16[48,1536]{1,0:T(8,128)(2,1)S(1)} %bitcast.327), channel_id=1, source_target_pairs={{0,2},{1,3},{2,0},{3,1},{4,6},{5,7},{6,4},{7,5},{8,10},{9,11},{10,... | collective-permute-start | bytes 442376 | tf_op jit(solution)/shard_map/ppermute | solution.py:775
  41.6 21.1 %collective-permute-start.13 = (bf16[192,1664]{1,0:T(8,128)(2,1)S(1)}, bf16[192,1664]{1,0:T(8,128)(2,1)S(1)}, u32[]{:S(2)}, u32[]{:S(2)}) collective-permute-start(bf16[192,1664]{1,0:T(8,128)(2,1)S(1)} %bitcast.278), channel_id=1, source_target_pairs={{0,1},{1,0},{2,3},{3,2},{4,5},{5,4},{6,7},{7,6},{8,9},{9,8},{10,11... | collective-permute-start | bytes 1916936 | tf_op jit(solution)/shard_map/ppermute | solution.py:775
  43.8 23.7 %collective-permute-start.8 = (bf16[192,1536]{1,0:T(8,128)(2,1)S(1)}, bf16[192,1536]{1,0:T(8,128)(2,1)S(1)}, u32[]{:S(2)}, u32[]{:S(2)}) collective-permute-start(bf16[192,1536]{1,0:T(8,128)(2,1)S(1)} %bitcast.281), channel_id=1, source_target_pairs={{0,16},{8,24},{16,0},{24,8},{1,17},{9,25},{17,1},{25,9},{2,18},{10... | collective-permute-start | bytes 1769480 | tf_op jit(solution)/shard_map/ppermute | solution.py:775
  62.9 10.2 %collective-permute-start.14 = (bf16[2,192,1664]{2,1,0:T(8,128)(2,1)S(1)}, bf16[2,192,1664]{2,1,0:T(8,128)(2,1)S(1)}, u32[]{:S(2)}, u32[]{:S(2)}) collective-permute-start(bf16[2,192,1664]{2,1,0:T(8,128)(2,1)S(1)} %bitcast.233), channel_id=1, source_target_pairs={{0,8},{8,0},{16,24},{24,16},{1,9},{9,1},{17,25},{25,17},{2,10},{10... | collective-permute-start | bytes 3833864 | tf_op jit(solution)/shard_map/ppermute | solution.py:775
  69.2 33.4 %collective-permute-start.16 = (bf16[512,768]{1,0:T(8,128)(2,1)S(1)}, bf16[512,768]{1,0:T(8,128)(2,1)S(1)}, u32[]{:S(2)}, u32[]{:S(2)}) collective-permute-start(bf16[512,768]{1,0:T(8,128)(2,1)S(1)} %bitcast.238), channel_id=1, source_target_pairs={{0,8},{8,0},{16,24},{24,16},{1,9},{9,1},{17,25},{25,17},{2,10},{10... | collective-permute-start | bytes 2359304 | tf_op jit(solution)/shard_map/ppermute | solution.py:775
  134.0 30.5 %collective-permute-start.19 = (bf16[768,768]{1,0:T(8,128)(2,1)}, bf16[768,768]{1,0:T(8,128)(2,1)S(1)}, u32[]{:S(2)}, u32[]{:S(2)}) collective-permute-start(bf16[768,768]{1,0:T(8,128)(2,1)} %bitcast.249), channel_id=1, source_target_pairs={{0,16},{8,24},{16,0},{24,8},{1,17},{9,25},{17,1},{25,9},{2,18},{10... | collective-permute-start | bytes 3538952 | tf_op jit(solution)/shard_map/ppermute | solution.py:775
  137.4 28.7 %collective-permute-start.20 = (bf16[768,768]{1,0:T(8,128)(2,1)S(1)}, bf16[768,768]{1,0:T(8,128)(2,1)S(1)}, u32[]{:S(2)}, u32[]{:S(2)}) collective-permute-start(bf16[768,768]{1,0:T(8,128)(2,1)S(1)} %bitcast.235), channel_id=1, source_target_pairs={{0,1},{1,0},{2,3},{3,2},{4,5},{5,4},{6,7},{7,6},{8,9},{9,8},{10,11... | collective-permute-start | bytes 3538952 | tf_op jit(solution)/shard_map/ppermute | solution.py:775
  164.8 15.4 %collective-permute-start.21 = (bf16[384,768]{1,0:T(8,128)(2,1)S(1)}, bf16[384,768]{1,0:T(8,128)(2,1)S(1)}, u32[]{:S(2)}, u32[]{:S(2)}) collective-permute-start(bf16[384,768]{1,0:T(8,128)(2,1)S(1)} %bitcast.244), channel_id=1, source_target_pairs={{0,1},{1,0},{2,3},{3,2},{4,5},{5,4},{6,7},{7,6},{8,9},{9,8},{10,11... | collective-permute-start | bytes 1769480 | tf_op jit(solution)/shard_map/ppermute | solution.py:775
  166.5 14.9 %collective-permute-start.22 = (bf16[384,768]{1,0:T(8,128)(2,1)S(1)}, bf16[384,768]{1,0:T(8,128)(2,1)S(1)}, u32[]{:S(2)}, u32[]{:S(2)}) collective-permute-start(bf16[384,768]{1,0:T(8,128)(2,1)S(1)} %bitcast.246), channel_id=1, source_target_pairs={{0,16},{8,24},{16,0},{24,8},{1,17},{9,25},{17,1},{25,9},{2,18},{10... | collective-permute-start | bytes 1769480 | tf_op jit(solution)/shard_map/ppermute | solution.py:775
  184.6 23.2 %collective-permute-start.26 = (bf16[384,768]{1,0:T(8,128)(2,1)S(1)}, bf16[384,768]{1,0:T(8,128)(2,1)S(1)}, u32[]{:S(2)}, u32[]{:S(2)}) collective-permute-start(bf16[384,768]{1,0:T(8,128)(2,1)S(1)} %bitcast.240), channel_id=1, source_target_pairs={{0,2},{1,3},{2,0},{3,1},{4,6},{5,7},{6,4},{7,5},{8,10},{9,11},{10,... | collective-permute-start | bytes 1769480 | tf_op jit(solution)/shard_map/ppermute | solution.py:775
  188.1 19.8 %collective-permute-start.27 = (bf16[192,1536]{1,0:T(8,128)(2,1)S(1)}, bf16[192,1536]{1,0:T(8,128)(2,1)S(1)}, u32[]{:S(2)}, u32[]{:S(2)}) collective-permute-start(bf16[192,1536]{1,0:T(8,128)(2,1)S(1)} %bitcast.242), channel_id=1, source_target_pairs={{0,1},{1,0},{2,3},{3,2},{4,5},{5,4},{6,7},{7,6},{8,9},{9,8},{10,11... | collective-permute-start | bytes 1769480 | tf_op jit(solution)/shard_map/ppermute | solution.py:775
  190.8 17.2 %collective-permute-start.28 = (bf16[192,1536]{1,0:T(8,128)(2,1)S(1)}, bf16[192,1536]{1,0:T(8,128)(2,1)S(1)}, u32[]{:S(2)}, u32[]{:S(2)}) collective-permute-start(bf16[192,1536]{1,0:T(8,128)(2,1)S(1)} %get-tuple-element.162.refs_14_), channel_id=1, source_target_pairs={{0,16},{8,24},{16,0},{24,8},{1,17},{9,25},{17,1},{25,9},{2,18},{10... | collective-permute-start | bytes 1769480 | tf_op jit(solution)/shard_map/ppermute | solution.py:775
  209.8 19.4 %collective-permute-start.36 = (bf16[192,768]{1,0:T(8,128)(2,1)S(1)}, bf16[192,768]{1,0:T(8,128)(2,1)S(1)}, u32[]{:S(2)}, u32[]{:S(2)}) collective-permute-start(bf16[192,768]{1,0:T(8,128)(2,1)S(1)} %bitcast.318), channel_id=1, source_target_pairs={{0,4},{1,5},{2,6},{3,7},{4,0},{5,1},{6,2},{7,3},{8,12},{9,13},{10,... | collective-permute-start | bytes 884744 | tf_op jit(solution)/shard_map/ppermute | solution.py:775
  211.5 9.7 %collective-permute-start.32 = (bf16[96,1536]{1,0:T(8,128)(2,1)S(1)}, bf16[96,1536]{1,0:T(8,128)(2,1)S(1)}, u32[]{:S(2)}, u32[]{:S(2)}) collective-permute-start(bf16[96,1536]{1,0:T(8,128)(2,1)S(1)} %get-tuple-element.180), channel_id=1, source_target_pairs={{0,16},{8,24},{16,0},{24,8},{1,17},{9,25},{17,1},{25,9},{2,18},{10... | collective-permute-start | bytes 884744 | tf_op jit(solution)/shard_map/ppermute | solution.py:775
  212.5 13.2 %collective-permute-start.33 = (bf16[96,1536]{1,0:T(8,128)(2,1)S(1)}, bf16[96,1536]{1,0:T(8,128)(2,1)S(1)}, u32[]{:S(2)}, u32[]{:S(2)}) collective-permute-start(bf16[96,1536]{1,0:T(8,128)(2,1)S(1)} %bitcast.320), channel_id=1, source_target_pairs={{0,1},{1,0},{2,3},{3,2},{4,5},{5,4},{6,7},{7,6},{8,9},{9,8},{10,11... | collective-permute-start | bytes 884744 | tf_op jit(solution)/shard_map/ppermute | solution.py:775
  221.3 7.9 %collective-permute-start.35 = (bf16[48,1536]{1,0:T(8,128)(2,1)S(1)}, bf16[48,1536]{1,0:T(8,128)(2,1)S(1)}, u32[]{:S(2)}, u32[]{:S(2)}) collective-permute-start(bf16[48,1536]{1,0:T(8,128)(2,1)S(1)} %bitcast.329), channel_id=1, source_target_pairs={{0,2},{1,3},{2,0},{3,1},{4,6},{5,7},{6,4},{7,5},{8,10},{9,11},{10,... | collective-permute-start | bytes 442376 | tf_op jit(solution)/shard_map/ppermute | solution.py:775
  229.5 20.6 %collective-permute-start.39 = (bf16[1,512,768]{2,1,0:T(8,128)(2,1)}, bf16[1,512,768]{2,1,0:T(8,128)(2,1)}, u32[]{:S(2)}, u32[]{:S(2)}) collective-permute-start(bf16[1,512,768]{2,1,0:T(8,128)(2,1)} %add_convert_fusion), channel_id=1, source_target_pairs={{0,16},{8,24},{16,0},{24,8},{1,17},{9,25},{17,1},{25,9},{2,18},{10... | collective-permute-start | bytes 2359304 | tf_op jit(solution)/shard_map/ppermute | solution.py:775
  230.5 8.3 %collective-permute-start.38 = (bf16[48,1664]{1,0:T(8,128)(2,1)}, bf16[48,1664]{1,0:T(8,128)(2,1)}, u32[]{:S(2)}, u32[]{:S(2)}) collective-permute-start(bf16[48,1664]{1,0:T(8,128)(2,1)} %bitcast.120), channel_id=1, source_target_pairs={{0,2},{1,3},{2,0},{3,1},{4,6},{5,7},{6,4},{7,5},{8,10},{9,11},{10,... | collective-permute-start | bytes 479240 | tf_op jit(solution)/shard_map/ppermute | solution.py:775
  230.5 9.8 %collective-permute-start.41 = (bf16[24,1536]{1,0:T(8,128)(2,1)S(1)}, bf16[24,1536]{1,0:T(8,128)(2,1)}, u32[]{:S(2)}, u32[]{:S(2)}) collective-permute-start(bf16[24,1536]{1,0:T(8,128)(2,1)S(1)} %fusion.17), channel_id=1, source_target_pairs={{0,4},{1,5},{2,6},{3,7},{4,0},{5,1},{6,2},{7,3},{8,12},{9,13},{10,... | collective-permute-start | bytes 221192 | tf_op jit(solution)/shard_map/ppermute | solution.py:775
  (69 other events, 397.3 us)
Sparse Core Ops, SparseCore 0:
  18.9 90.8 all-gather.1
where the time goes:
time: 265 us; the launch traced here: 260 us
  Pallas kernels  101 us (38%)
  waiting for transfers between devices  68.8 us (26%)
  starting transfers between devices  34 us (13%)
  other arithmetic  21.1 us (8%)
  local copies, waits for them, and re-layouts  20 us (8%)
  between operations  15.4 us (6%)
    ppermute x42, waiting for transfers between devices, swap(): lax.ppermute(array, axis, [(i, i ^ mask) for i in range(self.sizes[axis])])  64 us
    ppermute x42, starting transfers between devices, swap(): lax.ppermute(array, axis, [(i, i ^ mask) for i in range(self.sizes[axis])])  34 us
    pallas_call x1, Pallas kernels, branch(): pl.pallas_call(kernel, grid_spec=pltpu.PrefetchScalarGridSpec(num_scalar_...  23 us
    pallas_call x2, Pallas kernels, attend_back(): pl.pallas_call(kernel, grid=(steps,), in_specs=[tile, keys, pl.BlockSpec(...  20 us
    pallas_call x1, Pallas kernels, attend(): pl.pallas_call(attend_kernel, grid=(rows, steps), in_specs=[tile, pl.Bloc...  14.7 us
    pallas_call x1, Pallas kernels, first_norm(): pl.pallas_call(kernel, grid_spec=pltpu.PrefetchScalarGridSpec(num_scalar_...  14.6 us
    pallas_call x1, Pallas kernels, project(): pl.pallas_call(kernel, grid_spec=pltpu.PrefetchScalarGridSpec(num_scalar_...  12 us
    pallas_call x1, Pallas kernels, weight_grads(): pl.pallas_call(kernel, grid_spec=pltpu.PrefetchScalarGridSpec(num_scalar_...  7.86 us
  transfers between devices with their start and end apart: 43, of which 18 were waited for; matrix products, arithmetic and copies ran while one was open for 10% of the time, Pallas kernels for 30%

commit v1 on v0

--- a/solution.py
+++ b/solution.py
@@ -9,7 +9,6 @@
 LANES = 128
 CHUNK = 256
 PAIRS = 6
-PAIRS_BACK = 6
 MASKED = 16
 EPSILON = 1e-06
 FLOOR_SCORE = -1e30
@@ -144,11 +143,8 @@
 ):
     count, blocks, size = q_ref.shape[1], k_ref.shape[0], k_ref.shape[2]
 
-    @pl.when(pl.program_id(0) == 0)
-    def _():
-        set_bias(flags_ref, bias)
-
-    for u in range(PAIRS_BACK):
+    set_bias(flags_ref, bias)
+    for u in range(q_ref.shape[2] // LANES):
         lanes = slice(u * LANES, (u + 1) * LANES)
         d_mixed = dm_ref[0, :, lanes]
         asked, pulled = split_heads(q_ref[0, :, lanes]), split_heads(d_mixed)
@@ -212,39 +208,36 @@
     )(far(queries), far(key_values), far(key_values), flags)
 
 
-def attend_back(row, held, queries, key_values, d_mixed, mixed_full, lse, flags, after):
+def attend_back(queries, key_values, d_mixed, mixed_full, lse, flags, after):
     rows, count, width = queries.shape
     blocks, _, size, _ = key_values.shape
     pairs = width // LANES
-    tile = pl.BlockSpec((1, count, PAIRS_BACK * LANES), lambda p: (row, 0, p))
-    steps = pairs // PAIRS_BACK
-    keys = pl.BlockSpec((blocks, 1, size, PAIRS_BACK * LANES), lambda p: (0, row, 0, p))
-    line = lambda w: pl.BlockSpec((1, PAIRS_BACK, 1, w), lambda p: (row, p, 0, 0))
-    area = count * blocks * size
+    tile = pl.BlockSpec((1, count, width), lambda r: (r, 0, 0))
+    keys = pl.BlockSpec((blocks, 1, size, width), lambda r: (0, r, 0, 0))
+    line = lambda w: pl.BlockSpec((1, pairs, 1, w), lambda r: (r, 0, 0, 0))
+    area = rows * count * blocks * size
     grads = placed(BF16, blocks, rows, size, width)
     sums = shaped(F32, rows, pairs, 1, LANES)
     given = [queries, key_values, key_values, d_mixed, mixed_full, lse, flags]
-    extra = [*(held or []), *after]
 
     def kernel(*refs):
-        attend_back_kernel(*refs[: len(given)], *refs[len(given) + len(extra) :])
+        attend_back_kernel(*refs[: len(given)], *refs[len(given) + len(after) :])
 
     return pl.pallas_call(
         kernel,
-        grid=(steps,),
+        grid=(rows,),
         in_specs=[
-            tile, keys, pl.BlockSpec((blocks, 1, size, PAIRS_BACK * LANES), lambda p: (0, row, 0, steps + p)),
-            tile, tile, line(2 * count), pl.BlockSpec((blocks, 1, 1, size), lambda p: (0, row, 0, 0)),
-            *[ANYWHERE] * len(extra),
+            tile, keys, pl.BlockSpec((blocks, 1, size, width), lambda r: (0, r, 0, 1)), tile, tile,
+            line(2 * count), pl.BlockSpec((blocks, 1, 1, size), lambda r: (0, r, 0, 0)),
+            *[ANYWHERE] * len(after),
         ],
         out_specs=[tile, keys, keys, line(LANES), line(LANES)],
         out_shape=[placed(BF16, *queries.shape), grads, grads, sums, sums],
         scratch_shapes=[pltpu.VMEM((blocks * size, count), F32)],
-        input_output_aliases={len(given) + i: i for i in range(len(held or []))},
-        compiler_params=parameters(),
-        cost_estimate=cost(32 * area * width, 16 * blocks * size * width, area * 12),
-        name=f"attend_back_{row}",
-    )(*given, *extra)
+        compiler_params=parameters(40),
+        cost_estimate=cost(32 * area * width, 16 * rows * blocks * size * width, area * 12),
+        name="attend_back",
+    )(*given, *after)
 
 
 def project(near, sources, flags, left, left_other, right, right_other):
@@ -896,10 +889,7 @@
     d_mixed = d_mixed.reshape(row_count, patch_count, width)
 
     given = (queries, key_values, d_mixed, mixed_full, lse, flags)
-    grads = None
-    for row in range(row_count):
-        grads = list(attend_back(row, grads, *given, [down_sent, up_sent] if row == 0 else []))
-    d_query, d_key, d_value, query_sums, value_sums = grads
+    d_query, d_key, d_value, query_sums, value_sums = attend_back(*given, [down_sent, up_sent])
 
     down_sent, down_kept, down_order = links.add(
         after(down_kept, d_query), down_came, [mine, near, *row_bits], second
@@ -913,8 +903,10 @@
     pair_sent, pair_kept, value_sent, value_kept = weight_grads(
         near_place, turned, d_key, d_value, d_query, halves, [down_sent, up_sent]
     )
-    early_kept = jnp.concatenate([after(down_kept, pair_sent), up_kept], axis=0)
-    early_came = jnp.concatenate([after(down_came, pair_sent), up_came], axis=0)
+    output = after(middle, pair_sent) + added + away[0].astype(F32) + vectors[DBIAS]
+    output = output.astype(BF16)
+    early_kept = jnp.concatenate([after(down_kept, output), up_kept], axis=0)
+    early_came = jnp.concatenate([after(down_came, output), up_came], axis=0)
     early_order = [2 * mine, near, *others]
     early_sent, early_kept, early_order = links.add(early_kept, early_came, early_order, others[-1])
     early = [early_kept, links.swap(early_sent, others[-1]), early_order]
@@ -943,41 +935,39 @@
     gone = own
     for bit in rest_bits:
         gone = go(early, bit, gone)
-    gone = go(pair, first, gone)
+    pair_sent, pair[0], pair[2] = links.add(after(pair[0], gone), pair[1], pair[2], first)
+    gone = pair_sent
     gone = go(last, second, gone)
     near_share = links.swap(after(near_share, gone), near)
     small = [flat(small_kept), links.swap(flat(after(small_sent, gone)), near), have]
     gone = go(small, first, gone)
+    pair[1] = links.swap(after(pair_sent, gone), first)
     gone = (after(far_share, gone).astype(F32) + near_share[1:].astype(F32)).astype(BF16)
     far_share = links.swap(gone, first)
     gone = go(small, second, gone)
-    gone = go(pair, others[-1], gone)
-    output = after(middle, gone) + added + away[0].astype(F32) + vectors[DBIAS]
-    output = output.astype(BF16)
-    last[0] = jnp.concatenate([after(last[0], output), small[0]], axis=1)
-    last[1] = jnp.concatenate([last[1], small[1]], axis=1)
+    last[0] = jnp.concatenate([after(pair[0], gone), last[0], small[0]], axis=1)
+    last[1] = jnp.concatenate([pair[1], last[1], small[1]], axis=1)
     gone = go(last, others[-1], gone)
     low = links.value[near] == 0
-    for i, bit in enumerate(rest_bits):
-        gone = go(pair, bit, gone)
-        if i == len(rest_bits) - 1:
-            early_sum = after(early[0], gone).astype(F32) + early[1].astype(F32)
-            early_sum = early_sum.reshape(2 * mine, 2, n, width)
-            far_sum = links.pick(early_sum, near, True, 1).astype(BF16)
-            far_sum = links.swap(far_sum, near).astype(F32)
-            early_sum = links.pick(early_sum, near, False, 1)
-            joined = jnp.stack(
-                [jnp.where(low, early_sum, far_sum), jnp.where(low, far_sum, early_sum)], axis=0
-            )
-            down_sum = joined[:, :mine].reshape(-1, width)
-            up_sum = joined[:, mine:].reshape(groups, n, devices, n)
-            up_sum = up_sum.transpose(1, 2, 0, 3).reshape(n, -1)
-            gone = up_sum
+    early_sum = after(early[0], gone).astype(F32) + early[1].astype(F32)
+    early_sum = early_sum.reshape(2 * mine, 2, n, width)
+    far_sum = links.pick(early_sum, near, True, 1).astype(BF16)
+    far_sum = links.swap(far_sum, near).astype(F32)
+    early_sum = links.pick(early_sum, near, False, 1)
+    for bit in rest_bits:
         gone = go(last, bit, gone)
-    pair, last = (a.astype(F32) + b.astype(F32) for a, b, _ in (pair, last))
-    input_grad = after(own, up_sum, gone) + near_share[0].astype(F32) + far_share[0].astype(F32)
+    early_sum = after(early_sum, gone)
+    joined = jnp.stack(
+        [jnp.where(low, early_sum, far_sum), jnp.where(low, far_sum, early_sum)], axis=0
+    )
+    down_sum = joined[:, :mine].reshape(-1, width)
+    up_sum = joined[:, mine:].reshape(groups, n, devices, n)
+    up_sum = up_sum.transpose(1, 2, 0, 3).reshape(n, -1)
+    input_grad = after(own, up_sum) + near_share[0].astype(F32) + far_share[0].astype(F32)
     is_masked = masked.reshape(tokens, 1) == 1
     input_grad = jnp.where(is_masked, 0.0, input_grad)
+    last = after(last[0], input_grad).astype(F32) + last[1].astype(F32)
+    pair, last = last[:, : 2 * width], last[:, 2 * width :]
     project_sum = jnp.concatenate([pair, last[:, :width]], axis=1)
     out_sum = last[:, width : 2 * width]
     tail = last[:, 2 * width :].T

time: 265 us -> 255 us (0.962)
  other arithmetic: 21.1 us -> 18.1 us
    unnamed x105 -> x87, local copies, waits for them, and re-layouts: 7.13 us -> 4.05 us
    ppermute x42 -> x40, starting transfers between devices: 34 us -> 31.6 us  [swap(): lax.ppermute(array, axis, [(i, i ^ mask) for i in range(self.sizes[axis])])]
    convert_element_type x14 -> x12, other arithmetic: 7.86 us -> 6.11 us  [part(): return (first.astype(F32) + second.astype(F32)).astype(BF16)]
    pallas_call x2 -> x1, Pallas kernels: 20 us -> 18.5 us  [attend_back(): pl.pallas_call(kernel, grid=(rows,), in_specs=[tile, keys, pl.BlockSpec((...]
    ppermute x42 -> x40, waiting for transfers between devices: 64 us -> 64 us  [swap(): lax.ppermute(array, axis, [(i, i ^ mask) for i in range(self.sizes[axis])])]
  transfers between devices with their start and end apart: 43 -> 41, of which waited for: 18 -> 21; matrix products, arithmetic and copies ran while one was open for 10% -> 9% of each run, Pallas kernels for 30% -> 30%
where the time goes in v1:
time: 255 us; the launch traced here: 251 us
  Pallas kernels  99.6 us (39%)
  waiting for transfers between devices  68.7 us (27%)
  starting transfers between devices  31.7 us (12%)
  other arithmetic  18.1 us (7%)
  local copies, waits for them, and re-layouts  17.6 us (7%)
  between operations  15.2 us (6%)
    ppermute x40, waiting for transfers between devices, swap(): lax.ppermute(array, axis, [(i, i ^ mask) for i in range(self.sizes[axis])])  64 us
    ppermute x40, starting transfers between devices, swap(): lax.ppermute(array, axis, [(i, i ^ mask) for i in range(self.sizes[axis])])  31.6 us
    pallas_call x1, Pallas kernels, branch(): pl.pallas_call(kernel, grid_spec=pltpu.PrefetchScalarGridSpec(num_scalar_...  23.2 us
    pallas_call x1, Pallas kernels, attend_back(): pl.pallas_call(kernel, grid=(rows,), in_specs=[tile, keys, pl.BlockSpec((...  18.5 us
    pallas_call x1, Pallas kernels, attend(): pl.pallas_call(attend_kernel, grid=(rows, steps), in_specs=[tile, pl.Bloc...  14.7 us
    pallas_call x1, Pallas kernels, first_norm(): pl.pallas_call(kernel, grid_spec=pltpu.PrefetchScalarGridSpec(num_scalar_...  14.6 us
    pallas_call x1, Pallas kernels, project(): pl.pallas_call(kernel, grid_spec=pltpu.PrefetchScalarGridSpec(num_scalar_...  12.1 us
    pallas_call x1, Pallas kernels, weight_grads(): pl.pallas_call(kernel, grid_spec=pltpu.PrefetchScalarGridSpec(num_scalar_...  8.11 us
  transfers between devices with their start and end apart: 41, of which 21 were waited for; matrix products, arithmetic and copies ran while one was open for 9% of the time, Pallas kernels for 30%

profile of v1, /device:TPU:0, one launch (start us, length us, event | category | flops | bytes accessed | tf_op | source)
XLA Modules:
  0.0 250.9 jit_solution(7940627032367415385)
XLA Ops:
  7.2 2.1 reshape.670
  11.0 3.0 %collective-permute-start = (bf16[512,768]{1,0:T(8,128)(2,1)S(1)}, bf16[512,768]{1,0:T(8,128)(2,1)S(1)}, u32[]{:S(2)}, u32[]{:S(2)}) collective-permute-start(bf16[512,768]{1,0:T(8,128)(2,1)S(1)} %bitcast.218), channel_id=1, source_target_pairs={{0,16},{8,24},{16,0},{24,8},{1,17},{9,25},{17,1},{25,9},{2,18},{10... | collective-permute-start | bytes 2359304 | tf_op jit(solution)/shard_map/ppermute | solution.py:768
  14.6 2.7 %collective-permute-start.5 = (bf16[24,1536]{1,0:T(8,128)(2,1)S(1)}, bf16[24,1536]{1,0:T(8,128)(2,1)S(1)}, u32[]{:S(2)}, u32[]{:S(2)}) collective-permute-start(bf16[24,1536]{1,0:T(8,128)(2,1)S(1)} %pad_maximum_fusion.15), channel_id=1, source_target_pairs={{0,4},{1,5},{2,6},{3,7},{4,0},{5,1},{6,2},{7,3},{8,12},{9,13},{10,... | collective-permute-start | bytes 221192 | tf_op jit(solution)/shard_map/ppermute | solution.py:768
  18.8 4.1 %collective-permute-done.5 = bf16[24,1536]{1,0:T(8,128)(2,1)S(1)} collective-permute-done((bf16[24,1536]{1,0:T(8,128)(2,1)S(1)}, bf16[24,1536]{1,0:T(8,128)(2,1)S(1)}, u32[]{:S(2)}, u32[]{:S(2)}) %collective-permute-start.5) | collective-permute-done | bytes 73760 | tf_op jit(solution)/shard_map/ppermute | solution.py:768
  27.2 7.0 %collective-permute-done.11 = bf16[48,1664]{1,0:T(8,128)(2,1)S(1)} collective-permute-done((bf16[48,1664]{1,0:T(8,128)(2,1)S(1)}, bf16[48,1664]{1,0:T(8,128)(2,1)S(1)}, u32[]{:S(2)}, u32[]{:S(2)}) %collective-permute-start.11) | collective-permute-done | bytes 159776 | tf_op jit(solution)/shard_map/ppermute | solution.py:768
  34.4 2.3 collective-permute-done.6
  38.2 3.1 %collective-permute-done.12 = bf16[96,1664]{1,0:T(8,128)(2,1)S(1)} collective-permute-done((bf16[96,1664]{1,0:T(8,128)(2,1)S(1)}, bf16[96,1664]{1,0:T(8,128)(2,1)S(1)}, u32[]{:S(2)}, u32[]{:S(2)}) %collective-permute-start.12) | collective-permute-done | bytes 319520 | tf_op jit(solution)/shard_map/ppermute | solution.py:768
  44.7 17.9 %collective-permute-done.13 = bf16[192,1664]{1,0:T(8,128)(2,1)S(1)} collective-permute-done((bf16[192,1664]{1,0:T(8,128)(2,1)S(1)}, bf16[192,1664]{1,0:T(8,128)(2,1)S(1)}, u32[]{:S(2)}, u32[]{:S(2)}) %collective-permute-start.13) | collective-permute-done | bytes 639008 | tf_op jit(solution)/shard_map/ppermute | solution.py:768
  63.0 4.6 %collective-permute-done.8 = bf16[192,1536]{1,0:T(8,128)(2,1)S(1)} collective-permute-done((bf16[192,1536]{1,0:T(8,128)(2,1)S(1)}, bf16[192,1536]{1,0:T(8,128)(2,1)S(1)}, u32[]{:S(2)}, u32[]{:S(2)}) %collective-permute-start.8) | collective-permute-done | bytes 589856 | tf_op jit(solution)/shard_map/ppermute | solution.py:768
  69.3 2.6 %collective-permute-done.3 = bf16[1,2,256]{2,1,0:T(2,128)(2,1)S(1)} collective-permute-done((bf16[1,2,256]{2,1,0:T(2,128)(2,1)S(1)}, bf16[1,2,256]{2,1,0:T(2,128)(2,1)S(1)}, u32[]{:S(2)}, u32[]{:S(2)}) %collective-permute-start.3) | collective-permute-done | bytes 1056 | tf_op jit(solution)/shard_map/ppermute | solution.py:768
  73.2 12.1 %project.1 = (bf16[2048,768]{1,0:T(8,128)(2,1)}, bf16[768,2048]{1,0:T(8,128)(2,1)}, bf16[512,768]{1,0:T(8,128)(2,1)}, bf16[2048,1536]{1,0:T(8,128)(2,1)}, bf16[7...) custom-call(s32[1]{0:T(128)} %bitcast.near_ref, bf16[512,768]{1,0:T(8,128)(2,1)S(1)} %bitcast.220, ...), custom_call_target="tpu_custom_call" | custom-call | flops 6039797760 | bytes 22020096 | tf_op jit(solution)/shard_map/project/pallas_call | solution.py:323
  85.3 14.7 %attend.1 = (bf16[2,256,768]{2,1,0:T(8,128)(2,1)S(1)}, f32[2,256,768]{2,1,0:T(8,128)}, f32[2,6,1,512]{3,2,1,0:T(1,128)S(1)}) custom-call(bf16[2,256,768]{2,1,0:T(8,128)(2,1)} %bitcast.233, bf16[4,2,256,1536]{3,2,1,0:T(8,128)(2,1)} %bitcast.223, bf16[4,2,256,1536]{3,2,1,0:T(8,128)(2,1)} %bitcast.224, ...), custom_call_target="tpu_custom_call" | custom-call | flops 6442450944 | bytes 12582912 | tf_op jit(solution)/shard_map/attend/pallas_call | solution.py:186
  100.0 2.5 %open_branch.1 = (bf16[512,768]{1,0:T(8,128)(2,1)}, f32[512,768]{1,0:T(8,128)}) custom-call(bf16[512,768]{1,0:T(8,128)(2,1)S(1)} %bitcast.198, bf16[2048,768]{1,0:T(8,128)(2,1)S(1)} %copy-done.1, f32[4,2,1,256]{3,2,1,0:T(1,128)S(1)} %maximum_convert_fusion.refs_4_.refs_5_.flags_ref.refs_6_, f32[16,768]{1,0:T(8,128)S(1)} %get-tuple-element.87.vec_ref.refs_5_, ...), custom_call_target="tpu_custom_call" | custom-call | flops 603979776 | bytes 3932160 | tf_op jit(solution)/shard_map/open_branch/pallas_call | solution.py:383
  105.1 4.7 %all-gather.2.cloned.1.call-done.down_ref.up_ref = bf16[2,4,384,768]{3,2,1,0:T(8,128)(2,1)} async-done(((bf16[2,4,24,768]{3,2,1,0:T(8,128)(2,1)}), bf16[2,4,384,768]{3,2,1,0:T(8,128)(2,1)}) %all-gather.2.cloned.1.call-update) | async-done | bytes 4718608 | tf_op jit(solution)/shard_map/all_gather | solution.py:857
  110.9 23.2 %branch.1 = (f32[512,768]{1,0:T(8,128)}, f32[512,768]{1,0:T(8,128)}, bf16[2,512,768]{2,1,0:T(8,128)(2,1)}, bf16[2,2,192,768]{3,2,1,0:T(8,128)(2,1)}, bf16[2,2,19...) custom-call(s32[2]{0:T(128)S(1)} %pad_add_fusion.places_ref, ...), custom_call_target="tpu_custom_call" | custom-call | flops 14495514624 | bytes 11796480 | tf_op jit(solution)/shard_map/branch/pallas_call | solution.py:474
  138.5 5.8 %between.1 = (f32[512,768]{1,0:T(8,128)}, bf16[512,768]{1,0:T(8,128)(2,1)S(1)}, bf16[2,192,768]{2,1,0:T(8,128)(2,1)}, bf16[2,192,768]{2,1,0:T(8,128)(2,1)}, f32[8,768]{1,0:T(8,128)S(1)}) custom-call(s32[1]{0:T(128)} %bitcast.near_ref, f32[512,768]{1,0:T(8,128)S(1)} %copy-done.3, bf16[2,512,768]{2,1,0:T(8,128)(2,1)S(1)} %collective-permute-done.18.more_ref, ...), custom_call_target="tpu_custom_call" | custom-call | flops 1207959552 | bytes 6291456 | tf_op jit(solution)/shard_map/between/pallas_call | solution.py:558
  144.4 18.5 %attend_back.1 = (bf16[2,256,768]{2,1,0:T(8,128)(2,1)}, bf16[4,2,256,768]{3,2,1,0:T(8,128)(2,1)}, bf16[4,2,256,768]{3,2,1,0:T(8,128)(2,1)}, f32[2,6,1,128]{3,2,1,0:T(1,128)S(1)}, f32[2,6,1,128]{3,2,1,0:T(1,128)S(1)}) custom-call(bf16[2,256,768]{2,1,0:T(8,128)(2,1)S(1)} %bitcast.234, bf16[4,2,256,1536]{3,2,1,0:T(8,128)(2,1)S(1)} %bitcast.225, ...), custom_call_target="tpu_custom_call" | custom-call | flops 12884901888 | bytes 25165824 | tf_op jit(solution)/shard_map/attend_back/pallas_call | solution.py:226
  167.7 8.1 %weight_grads.1 = (bf16[2,192,1536]{2,1,0:T(8,128)(2,1)}, bf16[2,192,1536]{2,1,0:T(8,128)(2,1)}, bf16[2,192,768]{2,1,0:T(8,128)(2,1)}, bf16[2,192,768]{2,1,0:T(8,128)(2,1)}) custom-call(s32[1]{0:T(128)} %bitcast.near_ref, bf16[768,2048]{1,0:T(8,128)(2,1)S(1)} %copy-done.15, bf16[2048,768]{1,0:T(8,128)(2,1)S(1)} %bitcast.228, ...), custom_call_target="tpu_custom_call" | custom-call | flops 6039797760 | bytes 19660800 | tf_op jit(solution)/shard_map/weight_grads/pallas_call | solution.py:611
  190.6 14.6 %first_norm.1 = (bf16[1,512,768]{2,1,0:T(8,128)(2,1)}, bf16[2,512,768]{2,1,0:T(8,128)(2,1)}, f32[512,768]{1,0:T(8,128)}, bf16[2,192,128]{2,1,0:T(8,128)(2,1)S(1)}, bf16[2,192,128]{2,1,0:T(8,128)(2,1)S(1)}) custom-call(s32[1]{0:T(128)} %bitcast.near_ref, bf16[2048,768]{1,0:T(8,128)(2,1)} %bitcast.227, bf16[2048,768]{1,0:T(8,128)(2,1)} %bitcast.229, ...), custom_call_target="tpu_custom_call" | custom-call | flops 6039797760 | bytes 19660800 | tf_op jit(solution)/shard_map/first_norm/pallas_call | solution.py:713
  211.8 2.7 %add_convert_fusion = bf16[1,512,768]{2,1,0:T(8,128)(2,1)} fusion(bf16[1,512,768]{2,1,0:T(8,128)(2,1)} %get-tuple-element.132, bf16[2,512,768]{2,1,0:T(8,128)(2,1)S(1)} %collective-permute-done.30), kind=kLoop, calls=%fused_computation.6 | loop fusion | flops 1572864 | bytes 2359296 | tf_op jit(solution)/shard_map/convert_element_type | solution.py:945
  217.6 3.1 %collective-permute-done.32 = bf16[96,1536]{1,0:T(8,128)(2,1)S(1)} collective-permute-done((bf16[96,1536]{1,0:T(8,128)(2,1)S(1)}, bf16[96,1536]{1,0:T(8,128)(2,1)S(1)}, u32[]{:S(2)}, u32[]{:S(2)}) %collective-permute-start.32) | collective-permute-done | bytes 294944 | tf_op jit(solution)/shard_map/ppermute | solution.py:768
  223.5 6.3 %collective-permute-done.36 = bf16[48,3200]{1,0:T(8,128)(2,1)S(1)} collective-permute-done((bf16[48,3200]{1,0:T(8,128)(2,1)S(1)}, bf16[48,3200]{1,0:T(8,128)(2,1)S(1)}, u32[]{:S(2)}, u32[]{:S(2)}) %collective-permute-start.36) | collective-permute-done | bytes 307232 | tf_op jit(solution)/shard_map/ppermute | solution.py:768
  234.0 2.6 %reshape.726 = f32[24,3072]{1,0:T(8,128)} reshape(f32[24,32,4,24]{3,2,1,0:T(4,128)S(1)} %copy.87) | data formatting | bytes 589824 | tf_op jit(solution)/shard_map/reshape | solution.py:965
  237.0 2.8 %fusion = f32[512,768]{1,0:T(8,128)} fusion(f32[512,768]{1,0:T(8,128)S(1)} %copy-done.17, bf16[2,512,768]{2,1,0:T(8,128)(2,1)} %copy-done.18, bf16[1,512,768]{2,1,0:T(8,128)(2,1)} %collective-permute-done.38, pred[512]{0:T(512)(128)(4,1)S(1)} %eq.47), kind=kLoop, calls=%fused_computation.1 | loop fusion | flops 1966080 | bytes 4719104 | tf_op jit(solution)/shard_map/jit(_where)/select_n | solution.py:968
  (232 shorter events, 64.4 us)
Async XLA Ops:
  7.2 102.6 %all-gather.2.cloned.1.call-start = ((), (), s32[]{:S(2)}) async-start(), calls=%async_computation | async-start | bytes 5013504 | tf_op jit(solution)/shard_map/all_gather | solution.py:857
  11.0 25.7 %collective-permute-start = (bf16[512,768]{1,0:T(8,128)(2,1)S(1)}, bf16[512,768]{1,0:T(8,128)(2,1)S(1)}, u32[]{:S(2)}, u32[]{:S(2)}) collective-permute-start(bf16[512,768]{1,0:T(8,128)(2,1)S(1)} %bitcast.218), channel_id=1, source_target_pairs={{0,16},{8,24},{16,0},{24,8},{1,17},{9,25},{17,1},{25,9},{2,18},{10... | collective-permute-start | bytes 2359304 | tf_op jit(solution)/shard_map/ppermute | solution.py:768
  14.0 29.8 %collective-permute-start.1 = (bf16[512,768]{1,0:T(8,128)(2,1)S(1)}, bf16[512,768]{1,0:T(8,128)(2,1)S(1)}, u32[]{:S(2)}, u32[]{:S(2)}) collective-permute-start(bf16[512,768]{1,0:T(8,128)(2,1)S(1)} %bitcast.219), channel_id=1, source_target_pairs={{0,8},{8,0},{16,24},{24,16},{1,9},{9,1},{17,25},{25,17},{2,10},{10... | collective-permute-start | bytes 2359304 | tf_op jit(solution)/shard_map/ppermute | solution.py:768
  14.6 8.3 %collective-permute-start.5 = (bf16[24,1536]{1,0:T(8,128)(2,1)S(1)}, bf16[24,1536]{1,0:T(8,128)(2,1)S(1)}, u32[]{:S(2)}, u32[]{:S(2)}) collective-permute-start(bf16[24,1536]{1,0:T(8,128)(2,1)S(1)} %pad_maximum_fusion.15), channel_id=1, source_target_pairs={{0,4},{1,5},{2,6},{3,7},{4,0},{5,1},{6,2},{7,3},{8,12},{9,13},{10,... | collective-permute-start | bytes 221192 | tf_op jit(solution)/shard_map/ppermute | solution.py:768
  25.0 9.2 %collective-permute-start.11 = (bf16[48,1664]{1,0:T(8,128)(2,1)S(1)}, bf16[48,1664]{1,0:T(8,128)(2,1)S(1)}, u32[]{:S(2)}, u32[]{:S(2)}) collective-permute-start(bf16[48,1664]{1,0:T(8,128)(2,1)S(1)} %bitcast.283), channel_id=1, source_target_pairs={{0,2},{1,3},{2,0},{3,1},{4,6},{5,7},{6,4},{7,5},{8,10},{9,11},{10,... | collective-permute-start | bytes 479240 | tf_op jit(solution)/shard_map/ppermute | solution.py:768
  25.6 11.1 %collective-permute-start.6 = (bf16[48,1536]{1,0:T(8,128)(2,1)S(1)}, bf16[48,1536]{1,0:T(8,128)(2,1)S(1)}, u32[]{:S(2)}, u32[]{:S(2)}) collective-permute-start(bf16[48,1536]{1,0:T(8,128)(2,1)S(1)} %bitcast.285), channel_id=1, source_target_pairs={{0,2},{1,3},{2,0},{3,1},{4,6},{5,7},{6,4},{7,5},{8,10},{9,11},{10,... | collective-permute-start | bytes 442376 | tf_op jit(solution)/shard_map/ppermute | solution.py:768
  41.6 21.1 %collective-permute-start.13 = (bf16[192,1664]{1,0:T(8,128)(2,1)S(1)}, bf16[192,1664]{1,0:T(8,128)(2,1)S(1)}, u32[]{:S(2)}, u32[]{:S(2)}) collective-permute-start(bf16[192,1664]{1,0:T(8,128)(2,1)S(1)} %bitcast.241), channel_id=1, source_target_pairs={{0,1},{1,0},{2,3},{3,2},{4,5},{5,4},{6,7},{7,6},{8,9},{9,8},{10,11... | collective-permute-start | bytes 1916936 | tf_op jit(solution)/shard_map/ppermute | solution.py:768
  43.8 23.8 %collective-permute-start.8 = (bf16[192,1536]{1,0:T(8,128)(2,1)S(1)}, bf16[192,1536]{1,0:T(8,128)(2,1)S(1)}, u32[]{:S(2)}, u32[]{:S(2)}) collective-permute-start(bf16[192,1536]{1,0:T(8,128)(2,1)S(1)} %bitcast.246), channel_id=1, source_target_pairs={{0,16},{8,24},{16,0},{24,8},{1,17},{9,25},{17,1},{25,9},{2,18},{10... | collective-permute-start | bytes 1769480 | tf_op jit(solution)/shard_map/ppermute | solution.py:768
  62.9 10.3 %collective-permute-start.14 = (bf16[2,192,1664]{2,1,0:T(8,128)(2,1)S(1)}, bf16[2,192,1664]{2,1,0:T(8,128)(2,1)S(1)}, u32[]{:S(2)}, u32[]{:S(2)}) collective-permute-start(bf16[2,192,1664]{2,1,0:T(8,128)(2,1)S(1)} %bitcast.200), channel_id=1, source_target_pairs={{0,8},{8,0},{16,24},{24,16},{1,9},{9,1},{17,25},{25,17},{2,10},{10... | collective-permute-start | bytes 3833864 | tf_op jit(solution)/shard_map/ppermute | solution.py:768
  69.3 33.5 %collective-permute-start.16 = (bf16[512,768]{1,0:T(8,128)(2,1)S(1)}, bf16[512,768]{1,0:T(8,128)(2,1)S(1)}, u32[]{:S(2)}, u32[]{:S(2)}) collective-permute-start(bf16[512,768]{1,0:T(8,128)(2,1)S(1)} %bitcast.205), channel_id=1, source_target_pairs={{0,8},{8,0},{16,24},{24,16},{1,9},{9,1},{17,25},{25,17},{2,10},{10... | collective-permute-start | bytes 2359304 | tf_op jit(solution)/shard_map/ppermute | solution.py:768
  134.2 28.8 %collective-permute-start.19 = (bf16[768,768]{1,0:T(8,128)(2,1)}, bf16[768,768]{1,0:T(8,128)(2,1)S(1)}, u32[]{:S(2)}, u32[]{:S(2)}) collective-permute-start(bf16[768,768]{1,0:T(8,128)(2,1)} %bitcast.216), channel_id=1, source_target_pairs={{0,16},{8,24},{16,0},{24,8},{1,17},{9,25},{17,1},{25,9},{2,18},{10... | collective-permute-start | bytes 3538952 | tf_op jit(solution)/shard_map/ppermute | solution.py:768
  137.6 28.1 %collective-permute-start.20 = (bf16[768,768]{1,0:T(8,128)(2,1)S(1)}, bf16[768,768]{1,0:T(8,128)(2,1)S(1)}, u32[]{:S(2)}, u32[]{:S(2)}) collective-permute-start(bf16[768,768]{1,0:T(8,128)(2,1)S(1)} %bitcast.202), channel_id=1, source_target_pairs={{0,1},{1,0},{2,3},{3,2},{4,5},{5,4},{6,7},{7,6},{8,9},{9,8},{10,11... | collective-permute-start | bytes 3538952 | tf_op jit(solution)/shard_map/ppermute | solution.py:768
  163.3 15.5 %collective-permute-start.21 = (bf16[384,768]{1,0:T(8,128)(2,1)S(1)}, bf16[384,768]{1,0:T(8,128)(2,1)S(1)}, u32[]{:S(2)}, u32[]{:S(2)}) collective-permute-start(bf16[384,768]{1,0:T(8,128)(2,1)S(1)} %bitcast.211), channel_id=1, source_target_pairs={{0,1},{1,0},{2,3},{3,2},{4,5},{5,4},{6,7},{7,6},{8,9},{9,8},{10,11... | collective-permute-start | bytes 1769480 | tf_op jit(solution)/shard_map/ppermute | solution.py:768
  166.0 14.7 %collective-permute-start.22 = (bf16[384,768]{1,0:T(8,128)(2,1)S(1)}, bf16[384,768]{1,0:T(8,128)(2,1)S(1)}, u32[]{:S(2)}, u32[]{:S(2)}) collective-permute-start(bf16[384,768]{1,0:T(8,128)(2,1)S(1)} %bitcast.213), channel_id=1, source_target_pairs={{0,16},{8,24},{16,0},{24,8},{1,17},{9,25},{17,1},{25,9},{2,18},{10... | collective-permute-start | bytes 1769480 | tf_op jit(solution)/shard_map/ppermute | solution.py:768
  183.3 22.0 %collective-permute-start.26 = (bf16[384,768]{1,0:T(8,128)(2,1)S(1)}, bf16[384,768]{1,0:T(8,128)(2,1)S(1)}, u32[]{:S(2)}, u32[]{:S(2)}) collective-permute-start(bf16[384,768]{1,0:T(8,128)(2,1)S(1)} %bitcast.207), channel_id=1, source_target_pairs={{0,2},{1,3},{2,0},{3,1},{4,6},{5,7},{6,4},{7,5},{8,10},{9,11},{10,... | collective-permute-start | bytes 1769480 | tf_op jit(solution)/shard_map/ppermute | solution.py:768
  186.7 18.7 %collective-permute-start.27 = (bf16[192,1536]{1,0:T(8,128)(2,1)S(1)}, bf16[192,1536]{1,0:T(8,128)(2,1)S(1)}, u32[]{:S(2)}, u32[]{:S(2)}) collective-permute-start(bf16[192,1536]{1,0:T(8,128)(2,1)S(1)} %bitcast.209), channel_id=1, source_target_pairs={{0,1},{1,0},{2,3},{3,2},{4,5},{5,4},{6,7},{7,6},{8,9},{9,8},{10,11... | collective-permute-start | bytes 1769480 | tf_op jit(solution)/shard_map/ppermute | solution.py:768
  189.1 16.5 %collective-permute-start.28 = (bf16[192,1536]{1,0:T(8,128)(2,1)S(1)}, bf16[192,1536]{1,0:T(8,128)(2,1)S(1)}, u32[]{:S(2)}, u32[]{:S(2)}) collective-permute-start(bf16[192,1536]{1,0:T(8,128)(2,1)S(1)} %get-tuple-element.156.refs_14_), channel_id=1, source_target_pairs={{0,16},{8,24},{16,0},{24,8},{1,17},{9,25},{17,1},{25,9},{2,18},{10... | collective-permute-start | bytes 1769480 | tf_op jit(solution)/shard_map/ppermute | solution.py:768
  207.0 16.3 %collective-permute-start.35 = (bf16[192,768]{1,0:T(8,128)(2,1)S(1)}, bf16[192,768]{1,0:T(8,128)(2,1)S(1)}, u32[]{:S(2)}, u32[]{:S(2)}) collective-permute-start(bf16[192,768]{1,0:T(8,128)(2,1)S(1)} %bitcast.279), channel_id=1, source_target_pairs={{0,4},{1,5},{2,6},{3,7},{4,0},{5,1},{6,2},{7,3},{8,12},{9,13},{10,... | collective-permute-start | bytes 884744 | tf_op jit(solution)/shard_map/ppermute | solution.py:768
  208.6 8.9 %collective-permute-start.33 = (bf16[96,1536]{1,0:T(8,128)(2,1)}, bf16[96,1536]{1,0:T(8,128)(2,1)S(1)}, u32[]{:S(2)}, u32[]{:S(2)}) collective-permute-start(bf16[96,1536]{1,0:T(8,128)(2,1)} %bitcast.280), channel_id=1, source_target_pairs={{0,1},{1,0},{2,3},{3,2},{4,5},{5,4},{6,7},{7,6},{8,9},{9,8},{10,11... | collective-permute-start | bytes 884744 | tf_op jit(solution)/shard_map/ppermute | solution.py:768
  210.7 9.9 %collective-permute-start.32 = (bf16[96,1536]{1,0:T(8,128)(2,1)S(1)}, bf16[96,1536]{1,0:T(8,128)(2,1)S(1)}, u32[]{:S(2)}, u32[]{:S(2)}) collective-permute-start(bf16[96,1536]{1,0:T(8,128)(2,1)S(1)} %get-tuple-element.138), channel_id=1, source_target_pairs={{0,16},{8,24},{16,0},{24,8},{1,17},{9,25},{17,1},{25,9},{2,18},{10... | collective-permute-start | bytes 884744 | tf_op jit(solution)/shard_map/ppermute | solution.py:768
  214.5 22.5 %collective-permute-start.38 = (bf16[1,512,768]{2,1,0:T(8,128)(2,1)}, bf16[1,512,768]{2,1,0:T(8,128)(2,1)}, u32[]{:S(2)}, u32[]{:S(2)}) collective-permute-start(bf16[1,512,768]{2,1,0:T(8,128)(2,1)} %add_convert_fusion), channel_id=1, source_target_pairs={{0,16},{8,24},{16,0},{24,8},{1,17},{9,25},{17,1},{25,9},{2,18},{10... | collective-permute-start | bytes 2359304 | tf_op jit(solution)/shard_map/ppermute | solution.py:768
  220.9 8.9 %collective-permute-start.36 = (bf16[48,3200]{1,0:T(8,128)(2,1)S(1)}, bf16[48,3200]{1,0:T(8,128)(2,1)S(1)}, u32[]{:S(2)}, u32[]{:S(2)}) collective-permute-start(bf16[48,3200]{1,0:T(8,128)(2,1)S(1)} %bitcast.277), channel_id=1, source_target_pairs={{0,2},{1,3},{2,0},{3,1},{4,6},{5,7},{6,4},{7,5},{8,10},{9,11},{10,... | collective-permute-start | bytes 921608 | tf_op jit(solution)/shard_map/ppermute | solution.py:768
  223.4 7.5 %collective-permute-start.37 = (bf16[4,24,768]{2,1,0:T(8,128)(2,1)S(1)}, bf16[4,24,768]{2,1,0:T(8,128)(2,1)S(1)}, u32[]{:S(2)}, u32[]{:S(2)}) collective-permute-start(bf16[4,24,768]{2,1,0:T(8,128)(2,1)S(1)} %fusion.14), channel_id=1, source_target_pairs={{0,8},{8,0},{16,24},{24,16},{1,9},{9,1},{17,25},{25,17},{2,10},{10... | collective-permute-start | bytes 442376 | tf_op jit(solution)/shard_map/ppermute | solution.py:768
  229.9 10.0 %collective-permute-start.39 = (bf16[24,3200]{1,0:T(8,128)(2,1)S(1)}, bf16[24,3200]{1,0:T(8,128)(2,1)}, u32[]{:S(2)}, u32[]{:S(2)}) collective-permute-start(bf16[24,3200]{1,0:T(8,128)(2,1)S(1)} %get-tuple-element.180), channel_id=1, source_target_pairs={{0,4},{1,5},{2,6},{3,7},{4,0},{5,1},{6,2},{7,3},{8,12},{9,13},{10,... | collective-permute-start | bytes 460808 | tf_op jit(solution)/shard_map/ppermute | solution.py:768
  (58 other events, 339.1 us)
Sparse Core Ops, SparseCore 0:
  18.9 90.7 all-gather.1

commit v2 on v1

--- a/solution.py
+++ b/solution.py
@@ -284,7 +284,8 @@
                                     weights.at[at, pl.ds(kind * width + side * half, half)],
                                 )
                             )
-            first += [(refs[i], rows.at[pl.ds(i * own, own), :]) for i in range(blocks)]
+            first.append((refs[0], rows.at[pl.ds(0, own), :]))
+            later += [(refs[i], rows.at[pl.ds(i * own, own), :]) for i in range(1, blocks)]
             copies = [
                 pltpu.make_async_copy(a, b, sems.at[i]) for i, (a, b) in enumerate([*first, *later])
             ]
@@ -292,12 +293,12 @@
                 copy.start()
             for copy in copies[: len(first)]:
                 copy.wait()
-            outward[0].start()
             vec_ref[...] = columns[...].astype(F32).T[:KINDS]
             norm(0, 0, first_ref)
             for copy in copies[len(first) :]:
                 copy.wait()
-            outward[1].start()
+            for copy in outward:
+                copy.start()
 
         slot = lax.rem(step, 2)
         here = normed[slot]
@@ -406,7 +407,7 @@
     def kernel(
         places_ref, n_ref, no_ref, c_ref, co_ref, vec_ref, down_ref, up_ref,
         total_ref, dn_ref, away_ref, sdown_ref, kdown_ref, gup_ref, gbias_ref,
-        normed_all, turned, pulled_all, totals, d_normed, activated, d_hidden, up, down,
+        normed_all, turned, pulled_all, totals, d_normed, activated, d_hidden, up, down, staged, sems,
     ):
         step = pl.program_id(0)
 
@@ -453,6 +454,20 @@
                 totals[cut] += more
                 d_normed[cut] += more_back
 
+        last = step == pl.num_programs(0) - 1
+        outward = [
+            pltpu.make_async_copy(totals.at[pl.ds(0, tokens)], total_ref, sems.at[0]),
+            pltpu.make_async_copy(d_normed.at[pl.ds(0, tokens)], dn_ref, sems.at[1]),
+            pltpu.make_async_copy(staged, away_ref, sems.at[2]),
+        ]
+
+        @pl.when(last)
+        def _():
+            staged[0] = totals[tokens:].astype(BF16)
+            staged[1] = d_normed[tokens:].astype(BF16)
+            for copy in outward:
+                copy.start()
+
         gup_ref[0] = dot(turned[...], d_hidden[...], 1, 0).astype(BF16)
         grads = dot(activated[...], pulled_all[...], 0, 0).astype(BF16)
         (sent,), (kept,) = parted(grads, places_ref[1], length)
@@ -460,12 +475,10 @@
             sdown_ref[0, core] = sent[core * depth : (core + 1) * depth]
             kdown_ref[0, core] = kept[core * depth : (core + 1) * depth]
 
-        @pl.when(step == pl.num_programs(0) - 1)
-        def _():
-            total_ref[...] = totals[:tokens]
-            dn_ref[...] = d_normed[:tokens]
-            away_ref[0] = totals[tokens:].astype(BF16)
-            away_ref[1] = d_normed[tokens:].astype(BF16)
+        @pl.when(last)
+        def _():
+            for copy in outward:
+                copy.wait()
 
     weight = lambda f: pl.BlockSpec((cores, 1, length, width), lambda k, _: (0, f(k), 0, 0))
     piece = pl.BlockSpec((1, cores, depth, width), lambda k, _: (k, 0, 0, 0))
@@ -481,7 +494,7 @@
                 weight(lambda k: groups + k),
             ],
             out_specs=[
-                patch, patch, whole(2, tokens, width), piece, piece, square,
+                ANYWHERE, ANYWHERE, ANYWHERE, piece, piece, square,
                 pl.BlockSpec((1, 1, width), lambda k, _: (k, 0, 0)),
             ],
             scratch_shapes=[
@@ -494,6 +507,8 @@
                 pltpu.VMEM((both, width), BF16),
                 pltpu.VMEM((width, width), BF16),
                 pltpu.VMEM((width, width), BF16),
+                pltpu.VMEM((2, tokens, width), BF16),
+                pltpu.SemaphoreType.DMA((3,)),
             ],
         ),
         out_shape=[
@@ -510,7 +525,7 @@
             12 * groups * both * width * width, 20 * width * width, 2 * both * width * groups
         ),
         name="branch",
-    )(places, normed, normed_other, pulled, pulled_other, vectors, rest, rest)
+    )(places, far(normed), normed_other, pulled, pulled_other, vectors, rest, rest)
 
 
 def between(near, d_normed, d_normed_other, middle, pulled, vectors, mixed, weights, halves):
@@ -967,10 +982,8 @@
     is_masked = masked.reshape(tokens, 1) == 1
     input_grad = jnp.where(is_masked, 0.0, input_grad)
     last = after(last[0], input_grad).astype(F32) + last[1].astype(F32)
-    pair, last = last[:, : 2 * width], last[:, 2 * width :]
-    project_sum = jnp.concatenate([pair, last[:, :width]], axis=1)
-    out_sum = last[:, width : 2 * width]
-    tail = last[:, 2 * width :].T
+    project_sum, out_sum = last[:, : 3 * width], last[:, 3 * width : 4 * width]
+    tail = last[:, 4 * width :].T
     shape = (row_count, patch_count, width)
     return (
         output.reshape(shape), input_grad.reshape(shape), tail[EMBED], tail[GAIN1], tail[SHIFT1],

time: 255 us -> 253 us (level)
  transfers between devices with their start and end apart: 41 -> 41, of which waited for: 21 -> 20; matrix products, arithmetic and copies ran while one was open for 9% -> 10% of each run, Pallas kernels for 30% -> 31%
where the time goes in v2:
time: 253 us; the launch traced here: 248 us
  Pallas kernels  98 us (39%)
  waiting for transfers between devices  69.1 us (27%)
  starting transfers between devices  31 us (12%)
  other arithmetic  18.1 us (7%)
  local copies, waits for them, and re-layouts  16.7 us (7%)
  between operations  15.3 us (6%)
    ppermute x40, waiting for transfers between devices, swap(): lax.ppermute(array, axis, [(i, i ^ mask) for i in range(self.sizes[axis])])  64.3 us
    ppermute x40, starting transfers between devices, swap(): lax.ppermute(array, axis, [(i, i ^ mask) for i in range(self.sizes[axis])])  31 us
    pallas_call x1, Pallas kernels, branch(): pl.pallas_call(kernel, grid_spec=pltpu.PrefetchScalarGridSpec(num_scalar_...  21.7 us
    pallas_call x1, Pallas kernels, attend_back(): pl.pallas_call(kernel, grid=(rows,), in_specs=[tile, keys, pl.BlockSpec((...  18.5 us
    pallas_call x1, Pallas kernels, attend(): pl.pallas_call(attend_kernel, grid=(rows, steps), in_specs=[tile, pl.Bloc...  14.7 us
    pallas_call x1, Pallas kernels, first_norm(): pl.pallas_call(kernel, grid_spec=pltpu.PrefetchScalarGridSpec(num_scalar_...  14.6 us
    pallas_call x1, Pallas kernels, project(): pl.pallas_call(kernel, grid_spec=pltpu.PrefetchScalarGridSpec(num_scalar_...  12.1 us
    pallas_call x1, Pallas kernels, weight_grads(): pl.pallas_call(kernel, grid_spec=pltpu.PrefetchScalarGridSpec(num_scalar_...  8.11 us
  transfers between devices with their start and end apart: 41, of which 20 were waited for; matrix products, arithmetic and copies ran while one was open for 10% of the time, Pallas kernels for 31%

profile of v2, /device:TPU:0, one launch (start us, length us, event | category | flops | bytes accessed | tf_op | source)
XLA Modules:
  0.0 248.3 jit_solution(7981032174380394203)
XLA Ops:
  7.2 2.1 reshape.670
  11.0 3.0 %collective-permute-start = (bf16[512,768]{1,0:T(8,128)(2,1)S(1)}, bf16[512,768]{1,0:T(8,128)(2,1)S(1)}, u32[]{:S(2)}, u32[]{:S(2)}) collective-permute-start(bf16[512,768]{1,0:T(8,128)(2,1)S(1)} %bitcast.218), channel_id=1, source_target_pairs={{0,16},{8,24},{16,0},{24,8},{1,17},{9,25},{17,1},{25,9},{2,18},{10... | collective-permute-start | bytes 2359304 | tf_op jit(solution)/shard_map/ppermute | solution.py:783
  14.6 2.7 %collective-permute-start.5 = (bf16[24,1536]{1,0:T(8,128)(2,1)S(1)}, bf16[24,1536]{1,0:T(8,128)(2,1)S(1)}, u32[]{:S(2)}, u32[]{:S(2)}) collective-permute-start(bf16[24,1536]{1,0:T(8,128)(2,1)S(1)} %pad_maximum_fusion.15), channel_id=1, source_target_pairs={{0,4},{1,5},{2,6},{3,7},{4,0},{5,1},{6,2},{7,3},{8,12},{9,13},{10,... | collective-permute-start | bytes 221192 | tf_op jit(solution)/shard_map/ppermute | solution.py:783
  18.8 4.1 %collective-permute-done.5 = bf16[24,1536]{1,0:T(8,128)(2,1)S(1)} collective-permute-done((bf16[24,1536]{1,0:T(8,128)(2,1)S(1)}, bf16[24,1536]{1,0:T(8,128)(2,1)S(1)}, u32[]{:S(2)}, u32[]{:S(2)}) %collective-permute-start.5) | collective-permute-done | bytes 73760 | tf_op jit(solution)/shard_map/ppermute | solution.py:783
  27.2 7.0 %collective-permute-done.11 = bf16[48,1664]{1,0:T(8,128)(2,1)S(1)} collective-permute-done((bf16[48,1664]{1,0:T(8,128)(2,1)S(1)}, bf16[48,1664]{1,0:T(8,128)(2,1)S(1)}, u32[]{:S(2)}, u32[]{:S(2)}) %collective-permute-start.11) | collective-permute-done | bytes 159776 | tf_op jit(solution)/shard_map/ppermute | solution.py:783
  34.4 2.3 collective-permute-done.6
  38.2 3.1 %collective-permute-done.12 = bf16[96,1664]{1,0:T(8,128)(2,1)S(1)} collective-permute-done((bf16[96,1664]{1,0:T(8,128)(2,1)S(1)}, bf16[96,1664]{1,0:T(8,128)(2,1)S(1)}, u32[]{:S(2)}, u32[]{:S(2)}) %collective-permute-start.12) | collective-permute-done | bytes 319520 | tf_op jit(solution)/shard_map/ppermute | solution.py:783
  44.7 17.9 %collective-permute-done.13 = bf16[192,1664]{1,0:T(8,128)(2,1)S(1)} collective-permute-done((bf16[192,1664]{1,0:T(8,128)(2,1)S(1)}, bf16[192,1664]{1,0:T(8,128)(2,1)S(1)}, u32[]{:S(2)}, u32[]{:S(2)}) %collective-permute-start.13) | collective-permute-done | bytes 639008 | tf_op jit(solution)/shard_map/ppermute | solution.py:783
  63.0 4.6 %collective-permute-done.8 = bf16[192,1536]{1,0:T(8,128)(2,1)S(1)} collective-permute-done((bf16[192,1536]{1,0:T(8,128)(2,1)S(1)}, bf16[192,1536]{1,0:T(8,128)(2,1)S(1)}, u32[]{:S(2)}, u32[]{:S(2)}) %collective-permute-start.8) | collective-permute-done | bytes 589856 | tf_op jit(solution)/shard_map/ppermute | solution.py:783
  69.3 2.6 %collective-permute-done.3 = bf16[1,2,256]{2,1,0:T(2,128)(2,1)S(1)} collective-permute-done((bf16[1,2,256]{2,1,0:T(2,128)(2,1)S(1)}, bf16[1,2,256]{2,1,0:T(2,128)(2,1)S(1)}, u32[]{:S(2)}, u32[]{:S(2)}) %collective-permute-start.3) | collective-permute-done | bytes 1056 | tf_op jit(solution)/shard_map/ppermute | solution.py:783
  73.2 12.1 %project.1 = (bf16[2048,768]{1,0:T(8,128)(2,1)}, bf16[768,2048]{1,0:T(8,128)(2,1)}, bf16[512,768]{1,0:T(8,128)(2,1)}, bf16[2048,1536]{1,0:T(8,128)(2,1)}, bf16[7...) custom-call(s32[1]{0:T(128)} %bitcast.near_ref, bf16[512,768]{1,0:T(8,128)(2,1)S(1)} %bitcast.220, ...), custom_call_target="tpu_custom_call" | custom-call | flops 6039797760 | bytes 22020096 | tf_op jit(solution)/shard_map/project/pallas_call | solution.py:324
  85.3 14.7 %attend.1 = (bf16[2,256,768]{2,1,0:T(8,128)(2,1)S(1)}, f32[2,256,768]{2,1,0:T(8,128)}, f32[2,6,1,512]{3,2,1,0:T(1,128)S(1)}) custom-call(bf16[2,256,768]{2,1,0:T(8,128)(2,1)} %bitcast.235, bf16[4,2,256,1536]{3,2,1,0:T(8,128)(2,1)} %bitcast.223, bf16[4,2,256,1536]{3,2,1,0:T(8,128)(2,1)} %bitcast.224, ...), custom_call_target="tpu_custom_call" | custom-call | flops 6442450944 | bytes 12582912 | tf_op jit(solution)/shard_map/attend/pallas_call | solution.py:186
  100.0 2.5 %open_branch.1 = (bf16[512,768]{1,0:T(8,128)(2,1)}, f32[512,768]{1,0:T(8,128)}) custom-call(bf16[512,768]{1,0:T(8,128)(2,1)S(1)} %bitcast.198, bf16[2048,768]{1,0:T(8,128)(2,1)S(1)} %copy-done.1, f32[4,2,1,256]{3,2,1,0:T(1,128)S(1)} %maximum_convert_fusion.refs_4_.refs_5_.flags_ref.refs_6_, f32[16,768]{1,0:T(8,128)S(1)} %get-tuple-element.87.vec_ref.refs_5_, ...), custom_call_target="tpu_custom_call" | custom-call | flops 603979776 | bytes 3932160 | tf_op jit(solution)/shard_map/open_branch/pallas_call | solution.py:384
  105.0 4.8 %all-gather.2.cloned.1.call-done.down_ref.up_ref = bf16[2,4,384,768]{3,2,1,0:T(8,128)(2,1)} async-done(((bf16[2,4,24,768]{3,2,1,0:T(8,128)(2,1)}), bf16[2,4,384,768]{3,2,1,0:T(8,128)(2,1)}) %all-gather.2.cloned.1.call-update) | async-done | bytes 4718608 | tf_op jit(solution)/shard_map/all_gather | solution.py:872
  109.8 21.7 %branch.1 = (f32[512,768]{1,0:T(8,128)}, f32[512,768]{1,0:T(8,128)}, bf16[2,512,768]{2,1,0:T(8,128)(2,1)}, bf16[2,2,192,768]{3,2,1,0:T(8,128)(2,1)}, bf16[2,2,19...) custom-call(s32[2]{0:T(128)S(1)} %pad_add_fusion.places_ref, ...), custom_call_target="tpu_custom_call" | custom-call | flops 14495514624 | bytes 11796480 | tf_op jit(solution)/shard_map/branch/pallas_call | solution.py:487
  135.7 5.9 %between.1 = (f32[512,768]{1,0:T(8,128)}, bf16[512,768]{1,0:T(8,128)(2,1)S(1)}, bf16[2,192,768]{2,1,0:T(8,128)(2,1)}, bf16[2,192,768]{2,1,0:T(8,128)(2,1)}, f32[8,768]{1,0:T(8,128)S(1)}) custom-call(s32[1]{0:T(128)} %bitcast.near_ref, f32[512,768]{1,0:T(8,128)S(1)} %copy-done.3, bf16[2,512,768]{2,1,0:T(8,128)(2,1)S(1)} %collective-permute-done.18.more_ref, ...), custom_call_target="tpu_custom_call" | custom-call | flops 1207959552 | bytes 6291456 | tf_op jit(solution)/shard_map/between/pallas_call | solution.py:573
  141.7 18.5 %attend_back.1 = (bf16[2,256,768]{2,1,0:T(8,128)(2,1)}, bf16[4,2,256,768]{3,2,1,0:T(8,128)(2,1)}, bf16[4,2,256,768]{3,2,1,0:T(8,128)(2,1)}, f32[2,6,1,128]{3,2,1,0:T(1,128)S(1)}, f32[2,6,1,128]{3,2,1,0:T(1,128)S(1)}) custom-call(bf16[2,256,768]{2,1,0:T(8,128)(2,1)S(1)} %bitcast.236, bf16[4,2,256,1536]{3,2,1,0:T(8,128)(2,1)S(1)} %bitcast.227, ...), custom_call_target="tpu_custom_call" | custom-call | flops 12884901888 | bytes 25165824 | tf_op jit(solution)/shard_map/attend_back/pallas_call | solution.py:226
  165.0 8.1 %weight_grads.1 = (bf16[2,192,1536]{2,1,0:T(8,128)(2,1)}, bf16[2,192,1536]{2,1,0:T(8,128)(2,1)}, bf16[2,192,768]{2,1,0:T(8,128)(2,1)}, bf16[2,192,768]{2,1,0:T(8,128)(2,1)}) custom-call(s32[1]{0:T(128)} %bitcast.near_ref, bf16[768,2048]{1,0:T(8,128)(2,1)S(1)} %copy-done.12, bf16[2048,768]{1,0:T(8,128)(2,1)S(1)} %bitcast.230, ...), custom_call_target="tpu_custom_call" | custom-call | flops 6039797760 | bytes 19660800 | tf_op jit(solution)/shard_map/weight_grads/pallas_call | solution.py:626
  188.0 14.6 %first_norm.1 = (bf16[1,512,768]{2,1,0:T(8,128)(2,1)}, bf16[2,512,768]{2,1,0:T(8,128)(2,1)}, f32[512,768]{1,0:T(8,128)}, bf16[2,192,128]{2,1,0:T(8,128)(2,1)S(1)}, bf16[2,192,128]{2,1,0:T(8,128)(2,1)S(1)}) custom-call(s32[1]{0:T(128)} %bitcast.near_ref, bf16[2048,768]{1,0:T(8,128)(2,1)} %bitcast.229, bf16[2048,768]{1,0:T(8,128)(2,1)} %bitcast.231, ...), custom_call_target="tpu_custom_call" | custom-call | flops 6039797760 | bytes 19660800 | tf_op jit(solution)/shard_map/first_norm/pallas_call | solution.py:728
  209.2 2.7 %add_convert_fusion = bf16[1,512,768]{2,1,0:T(8,128)(2,1)} fusion(bf16[1,512,768]{2,1,0:T(8,128)(2,1)} %get-tuple-element.132, bf16[2,512,768]{2,1,0:T(8,128)(2,1)S(1)} %collective-permute-done.30), kind=kLoop, calls=%fused_computation.6 | loop fusion | flops 1572864 | bytes 2359296 | tf_op jit(solution)/shard_map/convert_element_type | solution.py:960
  215.6 2.9 %collective-permute-done.32 = bf16[96,1536]{1,0:T(8,128)(2,1)S(1)} collective-permute-done((bf16[96,1536]{1,0:T(8,128)(2,1)S(1)}, bf16[96,1536]{1,0:T(8,128)(2,1)S(1)}, u32[]{:S(2)}, u32[]{:S(2)}) %collective-permute-start.32) | collective-permute-done | bytes 294944 | tf_op jit(solution)/shard_map/ppermute | solution.py:783
  221.4 6.3 %collective-permute-done.36 = bf16[48,3200]{1,0:T(8,128)(2,1)S(1)} collective-permute-done((bf16[48,3200]{1,0:T(8,128)(2,1)S(1)}, bf16[48,3200]{1,0:T(8,128)(2,1)S(1)}, u32[]{:S(2)}, u32[]{:S(2)}) %collective-permute-start.36) | collective-permute-done | bytes 307232 | tf_op jit(solution)/shard_map/ppermute | solution.py:783
  231.1 2.6 %reshape.726 = f32[24,3072]{1,0:T(8,128)} reshape(f32[24,32,4,24]{3,2,1,0:T(4,128)S(1)} %copy.87) | data formatting | bytes 589824 | tf_op jit(solution)/shard_map/reshape | solution.py:980
  234.5 2.8 %fusion = f32[512,768]{1,0:T(8,128)} fusion(f32[512,768]{1,0:T(8,128)S(1)} %copy-done.14, bf16[2,512,768]{2,1,0:T(8,128)(2,1)} %copy-done.15, bf16[1,512,768]{2,1,0:T(8,128)(2,1)} %collective-permute-done.38, pred[512]{0:T(512)(128)(4,1)S(1)} %copy-done.24), kind=kLoop, calls=%fused_computation.1 | loop fusion | flops 1966080 | bytes 4719104 | tf_op jit(solution)/shard_map/jit(_where)/select_n | solution.py:983
  (235 shorter events, 63.3 us)
Async XLA Ops:
  7.2 102.6 %all-gather.2.cloned.1.call-start = ((), (), s32[]{:S(2)}) async-start(), calls=%async_computation | async-start | bytes 5013504 | tf_op jit(solution)/shard_map/all_gather | solution.py:872
  11.0 25.7 %collective-permute-start = (bf16[512,768]{1,0:T(8,128)(2,1)S(1)}, bf16[512,768]{1,0:T(8,128)(2,1)S(1)}, u32[]{:S(2)}, u32[]{:S(2)}) collective-permute-start(bf16[512,768]{1,0:T(8,128)(2,1)S(1)} %bitcast.218), channel_id=1, source_target_pairs={{0,16},{8,24},{16,0},{24,8},{1,17},{9,25},{17,1},{25,9},{2,18},{10... | collective-permute-start | bytes 2359304 | tf_op jit(solution)/shard_map/ppermute | solution.py:783
  14.0 29.8 %collective-permute-start.1 = (bf16[512,768]{1,0:T(8,128)(2,1)S(1)}, bf16[512,768]{1,0:T(8,128)(2,1)S(1)}, u32[]{:S(2)}, u32[]{:S(2)}) collective-permute-start(bf16[512,768]{1,0:T(8,128)(2,1)S(1)} %bitcast.219), channel_id=1, source_target_pairs={{0,8},{8,0},{16,24},{24,16},{1,9},{9,1},{17,25},{25,17},{2,10},{10... | collective-permute-start | bytes 2359304 | tf_op jit(solution)/shard_map/ppermute | solution.py:783
  14.6 8.3 %collective-permute-start.5 = (bf16[24,1536]{1,0:T(8,128)(2,1)S(1)}, bf16[24,1536]{1,0:T(8,128)(2,1)S(1)}, u32[]{:S(2)}, u32[]{:S(2)}) collective-permute-start(bf16[24,1536]{1,0:T(8,128)(2,1)S(1)} %pad_maximum_fusion.15), channel_id=1, source_target_pairs={{0,4},{1,5},{2,6},{3,7},{4,0},{5,1},{6,2},{7,3},{8,12},{9,13},{10,... | collective-permute-start | bytes 221192 | tf_op jit(solution)/shard_map/ppermute | solution.py:783
  17.6 7.3 %collective-permute-start.10 = (bf16[24,1664]{1,0:T(8,128)(2,1)S(1)}, bf16[24,1664]{1,0:T(8,128)(2,1)S(1)}, u32[]{:S(2)}, u32[]{:S(2)}) collective-permute-start(bf16[24,1664]{1,0:T(8,128)(2,1)S(1)} %constant_dynamic-update-slice_fusion), channel_id=1, source_target_pairs={{0,4},{1,5},{2,6},{3,7},{4,0},{5,1},{6,2},{7,3},{8,12},{9,13},{10,... | collective-permute-start | bytes 239624 | tf_op jit(solution)/shard_map/ppermute | solution.py:783
  25.0 9.2 %collective-permute-start.11 = (bf16[48,1664]{1,0:T(8,128)(2,1)S(1)}, bf16[48,1664]{1,0:T(8,128)(2,1)S(1)}, u32[]{:S(2)}, u32[]{:S(2)}) collective-permute-start(bf16[48,1664]{1,0:T(8,128)(2,1)S(1)} %bitcast.285), channel_id=1, source_target_pairs={{0,2},{1,3},{2,0},{3,1},{4,6},{5,7},{6,4},{7,5},{8,10},{9,11},{10,... | collective-permute-start | bytes 479240 | tf_op jit(solution)/shard_map/ppermute | solution.py:783
  25.6 11.1 %collective-permute-start.6 = (bf16[48,1536]{1,0:T(8,128)(2,1)S(1)}, bf16[48,1536]{1,0:T(8,128)(2,1)S(1)}, u32[]{:S(2)}, u32[]{:S(2)}) collective-permute-start(bf16[48,1536]{1,0:T(8,128)(2,1)S(1)} %bitcast.287), channel_id=1, source_target_pairs={{0,2},{1,3},{2,0},{3,1},{4,6},{5,7},{6,4},{7,5},{8,10},{9,11},{10,... | collective-permute-start | bytes 442376 | tf_op jit(solution)/shard_map/ppermute | solution.py:783
  41.6 21.1 %collective-permute-start.13 = (bf16[192,1664]{1,0:T(8,128)(2,1)S(1)}, bf16[192,1664]{1,0:T(8,128)(2,1)S(1)}, u32[]{:S(2)}, u32[]{:S(2)}) collective-permute-start(bf16[192,1664]{1,0:T(8,128)(2,1)S(1)} %bitcast.243), channel_id=1, source_target_pairs={{0,1},{1,0},{2,3},{3,2},{4,5},{5,4},{6,7},{7,6},{8,9},{9,8},{10,11... | collective-permute-start | bytes 1916936 | tf_op jit(solution)/shard_map/ppermute | solution.py:783
  43.8 23.8 %collective-permute-start.8 = (bf16[192,1536]{1,0:T(8,128)(2,1)S(1)}, bf16[192,1536]{1,0:T(8,128)(2,1)S(1)}, u32[]{:S(2)}, u32[]{:S(2)}) collective-permute-start(bf16[192,1536]{1,0:T(8,128)(2,1)S(1)} %bitcast.248), channel_id=1, source_target_pairs={{0,16},{8,24},{16,0},{24,8},{1,17},{9,25},{17,1},{25,9},{2,18},{10... | collective-permute-start | bytes 1769480 | tf_op jit(solution)/shard_map/ppermute | solution.py:783
  62.9 10.3 %collective-permute-start.14 = (bf16[2,192,1664]{2,1,0:T(8,128)(2,1)S(1)}, bf16[2,192,1664]{2,1,0:T(8,128)(2,1)S(1)}, u32[]{:S(2)}, u32[]{:S(2)}) collective-permute-start(bf16[2,192,1664]{2,1,0:T(8,128)(2,1)S(1)} %bitcast.200), channel_id=1, source_target_pairs={{0,8},{8,0},{16,24},{24,16},{1,9},{9,1},{17,25},{25,17},{2,10},{10... | collective-permute-start | bytes 3833864 | tf_op jit(solution)/shard_map/ppermute | solution.py:783
  69.3 33.5 %collective-permute-start.16 = (bf16[512,768]{1,0:T(8,128)(2,1)S(1)}, bf16[512,768]{1,0:T(8,128)(2,1)S(1)}, u32[]{:S(2)}, u32[]{:S(2)}) collective-permute-start(bf16[512,768]{1,0:T(8,128)(2,1)S(1)} %bitcast.204), channel_id=1, source_target_pairs={{0,8},{8,0},{16,24},{24,16},{1,9},{9,1},{17,25},{25,17},{2,10},{10... | collective-permute-start | bytes 2359304 | tf_op jit(solution)/shard_map/ppermute | solution.py:783
  131.6 28.7 %collective-permute-start.19 = (bf16[768,768]{1,0:T(8,128)(2,1)}, bf16[768,768]{1,0:T(8,128)(2,1)S(1)}, u32[]{:S(2)}, u32[]{:S(2)}) collective-permute-start(bf16[768,768]{1,0:T(8,128)(2,1)} %bitcast.216), channel_id=1, source_target_pairs={{0,16},{8,24},{16,0},{24,8},{1,17},{9,25},{17,1},{25,9},{2,18},{10... | collective-permute-start | bytes 3538952 | tf_op jit(solution)/shard_map/ppermute | solution.py:783
  135.0 28.1 %collective-permute-start.20 = (bf16[768,768]{1,0:T(8,128)(2,1)S(1)}, bf16[768,768]{1,0:T(8,128)(2,1)S(1)}, u32[]{:S(2)}, u32[]{:S(2)}) collective-permute-start(bf16[768,768]{1,0:T(8,128)(2,1)S(1)} %bitcast.202), channel_id=1, source_target_pairs={{0,1},{1,0},{2,3},{3,2},{4,5},{5,4},{6,7},{7,6},{8,9},{9,8},{10,11... | collective-permute-start | bytes 3538952 | tf_op jit(solution)/shard_map/ppermute | solution.py:783
  160.6 15.4 %collective-permute-start.21 = (bf16[384,768]{1,0:T(8,128)(2,1)S(1)}, bf16[384,768]{1,0:T(8,128)(2,1)S(1)}, u32[]{:S(2)}, u32[]{:S(2)}) collective-permute-start(bf16[384,768]{1,0:T(8,128)(2,1)S(1)} %bitcast.211), channel_id=1, source_target_pairs={{0,1},{1,0},{2,3},{3,2},{4,5},{5,4},{6,7},{7,6},{8,9},{9,8},{10,11... | collective-permute-start | bytes 1769480 | tf_op jit(solution)/shard_map/ppermute | solution.py:783
  163.4 14.6 %collective-permute-start.22 = (bf16[384,768]{1,0:T(8,128)(2,1)S(1)}, bf16[384,768]{1,0:T(8,128)(2,1)S(1)}, u32[]{:S(2)}, u32[]{:S(2)}) collective-permute-start(bf16[384,768]{1,0:T(8,128)(2,1)S(1)} %bitcast.213), channel_id=1, source_target_pairs={{0,16},{8,24},{16,0},{24,8},{1,17},{9,25},{17,1},{25,9},{2,18},{10... | collective-permute-start | bytes 1769480 | tf_op jit(solution)/shard_map/ppermute | solution.py:783
  180.6 22.0 %collective-permute-start.26 = (bf16[384,768]{1,0:T(8,128)(2,1)S(1)}, bf16[384,768]{1,0:T(8,128)(2,1)S(1)}, u32[]{:S(2)}, u32[]{:S(2)}) collective-permute-start(bf16[384,768]{1,0:T(8,128)(2,1)S(1)} %bitcast.207), channel_id=1, source_target_pairs={{0,2},{1,3},{2,0},{3,1},{4,6},{5,7},{6,4},{7,5},{8,10},{9,11},{10,... | collective-permute-start | bytes 1769480 | tf_op jit(solution)/shard_map/ppermute | solution.py:783
  184.1 18.7 %collective-permute-start.27 = (bf16[192,1536]{1,0:T(8,128)(2,1)S(1)}, bf16[192,1536]{1,0:T(8,128)(2,1)S(1)}, u32[]{:S(2)}, u32[]{:S(2)}) collective-permute-start(bf16[192,1536]{1,0:T(8,128)(2,1)S(1)} %bitcast.209), channel_id=1, source_target_pairs={{0,1},{1,0},{2,3},{3,2},{4,5},{5,4},{6,7},{7,6},{8,9},{9,8},{10,11... | collective-permute-start | bytes 1769480 | tf_op jit(solution)/shard_map/ppermute | solution.py:783
  186.5 16.5 %collective-permute-start.28 = (bf16[192,1536]{1,0:T(8,128)(2,1)S(1)}, bf16[192,1536]{1,0:T(8,128)(2,1)S(1)}, u32[]{:S(2)}, u32[]{:S(2)}) collective-permute-start(bf16[192,1536]{1,0:T(8,128)(2,1)S(1)} %get-tuple-element.156.refs_14_), channel_id=1, source_target_pairs={{0,16},{8,24},{16,0},{24,8},{1,17},{9,25},{17,1},{25,9},{2,18},{10... | collective-permute-start | bytes 1769480 | tf_op jit(solution)/shard_map/ppermute | solution.py:783
  204.9 16.2 %collective-permute-start.35 = (bf16[192,768]{1,0:T(8,128)(2,1)S(1)}, bf16[192,768]{1,0:T(8,128)(2,1)S(1)}, u32[]{:S(2)}, u32[]{:S(2)}) collective-permute-start(bf16[192,768]{1,0:T(8,128)(2,1)S(1)} %bitcast.281), channel_id=1, source_target_pairs={{0,4},{1,5},{2,6},{3,7},{4,0},{5,1},{6,2},{7,3},{8,12},{9,13},{10,... | collective-permute-start | bytes 884744 | tf_op jit(solution)/shard_map/ppermute | solution.py:783
  206.5 9.1 %collective-permute-start.33 = (bf16[96,1536]{1,0:T(8,128)(2,1)}, bf16[96,1536]{1,0:T(8,128)(2,1)S(1)}, u32[]{:S(2)}, u32[]{:S(2)}) collective-permute-start(bf16[96,1536]{1,0:T(8,128)(2,1)} %bitcast.282), channel_id=1, source_target_pairs={{0,1},{1,0},{2,3},{3,2},{4,5},{5,4},{6,7},{7,6},{8,9},{9,8},{10,11... | collective-permute-start | bytes 884744 | tf_op jit(solution)/shard_map/ppermute | solution.py:783
  208.6 9.9 %collective-permute-start.32 = (bf16[96,1536]{1,0:T(8,128)(2,1)S(1)}, bf16[96,1536]{1,0:T(8,128)(2,1)S(1)}, u32[]{:S(2)}, u32[]{:S(2)}) collective-permute-start(bf16[96,1536]{1,0:T(8,128)(2,1)S(1)} %get-tuple-element.138), channel_id=1, source_target_pairs={{0,16},{8,24},{16,0},{24,8},{1,17},{9,25},{17,1},{25,9},{2,18},{10... | collective-permute-start | bytes 884744 | tf_op jit(solution)/shard_map/ppermute | solution.py:783
  211.9 22.5 %collective-permute-start.38 = (bf16[1,512,768]{2,1,0:T(8,128)(2,1)}, bf16[1,512,768]{2,1,0:T(8,128)(2,1)}, u32[]{:S(2)}, u32[]{:S(2)}) collective-permute-start(bf16[1,512,768]{2,1,0:T(8,128)(2,1)} %add_convert_fusion), channel_id=1, source_target_pairs={{0,16},{8,24},{16,0},{24,8},{1,17},{9,25},{17,1},{25,9},{2,18},{10... | collective-permute-start | bytes 2359304 | tf_op jit(solution)/shard_map/ppermute | solution.py:783
  218.8 8.9 %collective-permute-start.36 = (bf16[48,3200]{1,0:T(8,128)(2,1)S(1)}, bf16[48,3200]{1,0:T(8,128)(2,1)S(1)}, u32[]{:S(2)}, u32[]{:S(2)}) collective-permute-start(bf16[48,3200]{1,0:T(8,128)(2,1)S(1)} %bitcast.279), channel_id=1, source_target_pairs={{0,2},{1,3},{2,0},{3,1},{4,6},{5,7},{6,4},{7,5},{8,10},{9,11},{10,... | collective-permute-start | bytes 921608 | tf_op jit(solution)/shard_map/ppermute | solution.py:783
  227.7 9.5 %collective-permute-start.39 = (bf16[24,3200]{1,0:T(8,128)(2,1)S(1)}, bf16[24,3200]{1,0:T(8,128)(2,1)}, u32[]{:S(2)}, u32[]{:S(2)}) collective-permute-start(bf16[24,3200]{1,0:T(8,128)(2,1)S(1)} %get-tuple-element.180), channel_id=1, source_target_pairs={{0,4},{1,5},{2,6},{3,7},{4,0},{5,1},{6,2},{7,3},{8,12},{9,13},{10,... | collective-permute-start | bytes 460808 | tf_op jit(solution)/shard_map/ppermute | solution.py:783
  (59 other events, 350.3 us)
Sparse Core Ops, SparseCore 0:
  18.9 90.8 all-gather.1

commit v3 on v2

--- a/solution.py
+++ b/solution.py
@@ -842,9 +842,11 @@
     ).reshape(2, 2 * mine, n, width)
     packed_kept, packed_sent = links.pick(packed, near), links.pick(packed, near, True)
     packed_came = links.swap(packed_sent, near)
+    low = links.value[near] == 0
+    packed = jnp.stack([jnp.where(low, packed_kept, packed_came), jnp.where(low, packed_came, packed_kept)], axis=0)
 
     flags = (segments + MASKED * masked).astype(BF16).reshape(1, row_count, patch_count)
-    sources = [after(patches.reshape(tokens, width), packed_sent)]
+    sources = [after(patches.reshape(tokens, width), packed_came)]
     for bit in (first, near):
         flags = jnp.concatenate([flags, links.swap(flags, bit)], axis=0)
         sources += [links.swap(source, bit) for source in sources]
@@ -858,14 +860,12 @@
     columns = jnp.pad(columns, ((0, 0), (0, LANES - columns.shape[1])))
     fourths = [qkv_weight[:, i * half : (i + 1) * half] for i in range(6)]
     fourths += [out_weight[:, :half], out_weight[:, half:]]
-    left = jnp.concatenate(fourths[::2], axis=1)
-    right = jnp.concatenate([*fourths[1::2], columns], axis=1)
+    left = after(jnp.concatenate(fourths[::2], axis=1), packed)
+    right = after(jnp.concatenate([*fourths[1::2], columns], axis=1), packed)
     left = links.gather(left, [*others, second, first], {2: early_ones, 3: late_ones}).reshape(halves, depth, -1)
     right = links.gather(right, [*others, first, second], {}).reshape(halves, depth, -1)
     left_other, right_other = links.swap(left, near), links.swap(right, near)
 
-    low = links.value[near] == 0
-    packed = jnp.stack([jnp.where(low, packed_kept, packed_came), jnp.where(low, packed_came, packed_kept)], axis=0)
     same_core = [
         [(x * 2 + core) * rows + r for x in range(halves) for r in range(rows)] for core in range(2)
     ]

time: 253 us -> 251 us (level)
  waiting for transfers between devices: 69.1 us -> 64.4 us
  starting transfers between devices: 31 us -> 34.9 us
    all_gather x1, waiting for transfers between devices: 4.76 us -> 0.01 us  [body(): lax.all_gather(packed, EVERY, axis=2, tiled=True, axis_index_groups=same_...]
    ppermute x40, starting transfers between devices: 31 us -> 34.8 us  [swap(): lax.ppermute(array, axis, [(i, i ^ mask) for i in range(self.sizes[axis])])]
  transfers between devices with their start and end apart: 41 -> 41, of which waited for: 20 -> 18; matrix products, arithmetic and copies ran while one was open for 10% -> 9% of each run, Pallas kernels for 31% -> 31%
where the time goes in v3:
time: 251 us; the launch traced here: 247 us
  Pallas kernels  97.9 us (39%)
  waiting for transfers between devices  64.4 us (26%)
  starting transfers between devices  34.9 us (14%)
  other arithmetic  18.1 us (7%)
  local copies, waits for them, and re-layouts  16 us (6%)
  between operations  15.3 us (6%)
    ppermute x40, waiting for transfers between devices, swap(): lax.ppermute(array, axis, [(i, i ^ mask) for i in range(self.sizes[axis])])  64.4 us
    ppermute x40, starting transfers between devices, swap(): lax.ppermute(array, axis, [(i, i ^ mask) for i in range(self.sizes[axis])])  34.8 us
    pallas_call x1, Pallas kernels, branch(): pl.pallas_call(kernel, grid_spec=pltpu.PrefetchScalarGridSpec(num_scalar_...  21.7 us
    pallas_call x1, Pallas kernels, attend_back(): pl.pallas_call(kernel, grid=(rows,), in_specs=[tile, keys, pl.BlockSpec((...  18.5 us
    pallas_call x1, Pallas kernels, attend(): pl.pallas_call(attend_kernel, grid=(rows, steps), in_specs=[tile, pl.Bloc...  14.7 us
    pallas_call x1, Pallas kernels, first_norm(): pl.pallas_call(kernel, grid_spec=pltpu.PrefetchScalarGridSpec(num_scalar_...  14.6 us
    pallas_call x1, Pallas kernels, project(): pl.pallas_call(kernel, grid_spec=pltpu.PrefetchScalarGridSpec(num_scalar_...  12.1 us
    pallas_call x1, Pallas kernels, weight_grads(): pl.pallas_call(kernel, grid_spec=pltpu.PrefetchScalarGridSpec(num_scalar_...  8.14 us
  transfers between devices with their start and end apart: 41, of which 18 were waited for; matrix products, arithmetic and copies ran while one was open for 9% of the time, Pallas kernels for 31%

profile of v3, /device:TPU:0, one launch (start us, length us, event | category | flops | bytes accessed | tf_op | source)
XLA Modules:
  0.0 246.6 jit_solution(12415190168403932090)
XLA Ops:
  13.3 3.9 %collective-permute-start.6 = (bf16[24,1536]{1,0:T(8,128)(2,1)S(1)}, bf16[24,1536]{1,0:T(8,128)(2,1)S(1)}, u32[]{:S(2)}, u32[]{:S(2)}) collective-permute-start(bf16[24,1536]{1,0:T(8,128)(2,1)S(1)} %pad_maximum_fusion.15), channel_id=1, source_target_pairs={{0,4},{1,5},{2,6},{3,7},{4,0},{5,1},{6,2},{7,3},{8,12},{9,13},{10,... | collective-permute-start | bytes 221192 | tf_op jit(solution)/shard_map/ppermute | solution.py:783
  19.3 2.2 collective-permute-done.6
  21.4 4.9 %collective-permute-done.11 = bf16[24,1664]{1,0:T(8,128)(2,1)S(1)} collective-permute-done((bf16[24,1664]{1,0:T(8,128)(2,1)S(1)}, bf16[24,1664]{1,0:T(8,128)(2,1)S(1)}, u32[]{:S(2)}, u32[]{:S(2)}) %collective-permute-start.11) | collective-permute-done | bytes 79904 | tf_op jit(solution)/shard_map/ppermute | solution.py:783
  28.6 7.5 %collective-permute-done.12 = bf16[48,1664]{1,0:T(8,128)(2,1)S(1)} collective-permute-done((bf16[48,1664]{1,0:T(8,128)(2,1)S(1)}, bf16[48,1664]{1,0:T(8,128)(2,1)S(1)}, u32[]{:S(2)}, u32[]{:S(2)}) %collective-permute-start.12) | collective-permute-done | bytes 159776 | tf_op jit(solution)/shard_map/ppermute | solution.py:783
  37.2 4.3 %collective-permute-done.7 = bf16[48,1536]{1,0:T(8,128)(2,1)S(1)} collective-permute-done((bf16[48,1536]{1,0:T(8,128)(2,1)S(1)}, bf16[48,1536]{1,0:T(8,128)(2,1)S(1)}, u32[]{:S(2)}, u32[]{:S(2)}) %collective-permute-start.7) | collective-permute-done | bytes 147488 | tf_op jit(solution)/shard_map/ppermute | solution.py:783
  43.2 2.4 collective-permute-done.13
  47.4 6.6 %collective-permute-done.8 = bf16[96,1536]{1,0:T(8,128)(2,1)S(1)} collective-permute-done((bf16[96,1536]{1,0:T(8,128)(2,1)S(1)}, bf16[96,1536]{1,0:T(8,128)(2,1)S(1)}, u32[]{:S(2)}, u32[]{:S(2)}) %collective-permute-start.8) | collective-permute-done | bytes 294944 | tf_op jit(solution)/shard_map/ppermute | solution.py:783
  54.2 13.9 %collective-permute-done.14 = bf16[192,1664]{1,0:T(8,128)(2,1)S(1)} collective-permute-done((bf16[192,1664]{1,0:T(8,128)(2,1)S(1)}, bf16[192,1664]{1,0:T(8,128)(2,1)S(1)}, u32[]{:S(2)}, u32[]{:S(2)}) %collective-permute-start.14) | collective-permute-done | bytes 639008 | tf_op jit(solution)/shard_map/ppermute | solution.py:783
  71.7 3.1 %collective-permute-done.4 = bf16[1,2,256]{2,1,0:T(2,128)(2,1)S(1)} collective-permute-done((bf16[1,2,256]{2,1,0:T(2,128)(2,1)S(1)}, bf16[1,2,256]{2,1,0:T(2,128)(2,1)S(1)}, u32[]{:S(2)}, u32[]{:S(2)}) %collective-permute-start.4) | collective-permute-done | bytes 1056 | tf_op jit(solution)/shard_map/ppermute | solution.py:783
  76.0 12.1 %project.1 = (bf16[2048,768]{1,0:T(8,128)(2,1)}, bf16[768,2048]{1,0:T(8,128)(2,1)}, bf16[512,768]{1,0:T(8,128)(2,1)}, bf16[2048,1536]{1,0:T(8,128)(2,1)}, bf16[7...) custom-call(s32[1]{0:T(128)} %bitcast.near_ref, bf16[512,768]{1,0:T(8,128)(2,1)S(1)} %bitcast.220, ...), custom_call_target="tpu_custom_call" | custom-call | flops 6039797760 | bytes 22020096 | tf_op jit(solution)/shard_map/project/pallas_call | solution.py:324
  88.1 14.7 %attend.1 = (bf16[2,256,768]{2,1,0:T(8,128)(2,1)S(1)}, f32[2,256,768]{2,1,0:T(8,128)}, f32[2,6,1,512]{3,2,1,0:T(1,128)S(1)}) custom-call(bf16[2,256,768]{2,1,0:T(8,128)(2,1)} %bitcast.235, bf16[4,2,256,1536]{3,2,1,0:T(8,128)(2,1)} %bitcast.223, bf16[4,2,256,1536]{3,2,1,0:T(8,128)(2,1)} %bitcast.224, ...), custom_call_target="tpu_custom_call" | custom-call | flops 6442450944 | bytes 12582912 | tf_op jit(solution)/shard_map/attend/pallas_call | solution.py:186
  102.8 2.5 %open_branch.1 = (bf16[512,768]{1,0:T(8,128)(2,1)}, f32[512,768]{1,0:T(8,128)}) custom-call(bf16[512,768]{1,0:T(8,128)(2,1)S(1)} %bitcast.198, bf16[2048,768]{1,0:T(8,128)(2,1)S(1)} %copy-done.1, f32[4,2,1,256]{3,2,1,0:T(1,128)S(1)} %maximum_convert_fusion.refs_4_.refs_5_.flags_ref.refs_6_, f32[16,768]{1,0:T(8,128)S(1)} %get-tuple-element.91.vec_ref.refs_5_, ...), custom_call_target="tpu_custom_call" | custom-call | flops 603979776 | bytes 3932160 | tf_op jit(solution)/shard_map/open_branch/pallas_call | solution.py:384
  107.8 21.7 %branch.1 = (f32[512,768]{1,0:T(8,128)}, f32[512,768]{1,0:T(8,128)}, bf16[2,512,768]{2,1,0:T(8,128)(2,1)}, bf16[2,2,192,768]{3,2,1,0:T(8,128)(2,1)}, bf16[2,2,19...) custom-call(s32[2]{0:T(128)S(1)} %pad_add_fusion.places_ref, ...), custom_call_target="tpu_custom_call" | custom-call | flops 14495514624 | bytes 11796480 | tf_op jit(solution)/shard_map/branch/pallas_call | solution.py:487
  133.9 5.8 %between.1 = (f32[512,768]{1,0:T(8,128)}, bf16[512,768]{1,0:T(8,128)(2,1)S(1)}, bf16[2,192,768]{2,1,0:T(8,128)(2,1)}, bf16[2,192,768]{2,1,0:T(8,128)(2,1)}, f32[8,768]{1,0:T(8,128)S(1)}) custom-call(s32[1]{0:T(128)} %bitcast.near_ref, f32[512,768]{1,0:T(8,128)S(1)} %copy-done.3, bf16[2,512,768]{2,1,0:T(8,128)(2,1)S(1)} %collective-permute-done.18.more_ref, ...), custom_call_target="tpu_custom_call" | custom-call | flops 1207959552 | bytes 6291456 | tf_op jit(solution)/shard_map/between/pallas_call | solution.py:573
  139.8 18.5 %attend_back.1 = (bf16[2,256,768]{2,1,0:T(8,128)(2,1)}, bf16[4,2,256,768]{3,2,1,0:T(8,128)(2,1)}, bf16[4,2,256,768]{3,2,1,0:T(8,128)(2,1)}, f32[2,6,1,128]{3,2,1,0:T(1,128)S(1)}, f32[2,6,1,128]{3,2,1,0:T(1,128)S(1)}) custom-call(bf16[2,256,768]{2,1,0:T(8,128)(2,1)S(1)} %bitcast.236, bf16[4,2,256,1536]{3,2,1,0:T(8,128)(2,1)S(1)} %bitcast.227, ...), custom_call_target="tpu_custom_call" | custom-call | flops 12884901888 | bytes 25165824 | tf_op jit(solution)/shard_map/attend_back/pallas_call | solution.py:226
  162.1 8.1 %weight_grads.1 = (bf16[2,192,1536]{2,1,0:T(8,128)(2,1)}, bf16[2,192,1536]{2,1,0:T(8,128)(2,1)}, bf16[2,192,768]{2,1,0:T(8,128)(2,1)}, bf16[2,192,768]{2,1,0:T(8,128)(2,1)}) custom-call(s32[1]{0:T(128)} %bitcast.near_ref, bf16[768,2048]{1,0:T(8,128)(2,1)S(1)} %copy-done.12, bf16[2048,768]{1,0:T(8,128)(2,1)S(1)} %bitcast.230, ...), custom_call_target="tpu_custom_call" | custom-call | flops 6039797760 | bytes 19660800 | tf_op jit(solution)/shard_map/weight_grads/pallas_call | solution.py:626
  171.5 2.2 collective-permute-done.21
  186.0 14.6 %first_norm.1 = (bf16[1,512,768]{2,1,0:T(8,128)(2,1)}, bf16[2,512,768]{2,1,0:T(8,128)(2,1)}, f32[512,768]{1,0:T(8,128)}, bf16[2,192,128]{2,1,0:T(8,128)(2,1)S(1)}, bf16[2,192,128]{2,1,0:T(8,128)(2,1)S(1)}) custom-call(s32[1]{0:T(128)} %bitcast.near_ref, bf16[2048,768]{1,0:T(8,128)(2,1)} %bitcast.229, bf16[2048,768]{1,0:T(8,128)(2,1)} %bitcast.231, ...), custom_call_target="tpu_custom_call" | custom-call | flops 6039797760 | bytes 19660800 | tf_op jit(solution)/shard_map/first_norm/pallas_call | solution.py:728
  202.9 2.4 collective-permute-start.35
  208.0 2.7 %add_convert_fusion = bf16[1,512,768]{2,1,0:T(8,128)(2,1)} fusion(bf16[1,512,768]{2,1,0:T(8,128)(2,1)} %get-tuple-element.136, bf16[2,512,768]{2,1,0:T(8,128)(2,1)S(1)} %collective-permute-done.30), kind=kLoop, calls=%fused_computation.6 | loop fusion | flops 1572864 | bytes 2359296 | tf_op jit(solution)/shard_map/convert_element_type | solution.py:960
  214.4 2.6 %collective-permute-done.32 = bf16[96,1536]{1,0:T(8,128)(2,1)S(1)} collective-permute-done((bf16[96,1536]{1,0:T(8,128)(2,1)S(1)}, bf16[96,1536]{1,0:T(8,128)(2,1)S(1)}, u32[]{:S(2)}, u32[]{:S(2)}) %collective-permute-start.32) | collective-permute-done | bytes 294944 | tf_op jit(solution)/shard_map/ppermute | solution.py:783
  219.3 6.3 %collective-permute-done.36 = bf16[48,3200]{1,0:T(8,128)(2,1)S(1)} collective-permute-done((bf16[48,3200]{1,0:T(8,128)(2,1)S(1)}, bf16[48,3200]{1,0:T(8,128)(2,1)S(1)}, u32[]{:S(2)}, u32[]{:S(2)}) %collective-permute-start.36) | collective-permute-done | bytes 307232 | tf_op jit(solution)/shard_map/ppermute | solution.py:783
  230.2 2.6 %reshape.726 = f32[24,3072]{1,0:T(8,128)} reshape(f32[24,32,4,24]{3,2,1,0:T(4,128)S(1)} %copy.87) | data formatting | bytes 589824 | tf_op jit(solution)/shard_map/reshape | solution.py:980
  232.8 2.8 %fusion = f32[512,768]{1,0:T(8,128)} fusion(f32[512,768]{1,0:T(8,128)S(1)} %copy-done.14, bf16[2,512,768]{2,1,0:T(8,128)(2,1)} %copy-done.15, bf16[1,512,768]{2,1,0:T(8,128)(2,1)} %collective-permute-done.38, pred[512]{0:T(512)(128)(4,1)S(1)} %copy-done.24), kind=kLoop, calls=%fused_computation.1 | loop fusion | flops 1966080 | bytes 4719104 | tf_op jit(solution)/shard_map/jit(_where)/select_n | solution.py:983
  (235 shorter events, 63.1 us)
Async XLA Ops:
  7.2 100.6 %all-gather.2.cloned.1.call-start = ((), (), s32[]{:S(2)}) async-start(), calls=%async_computation | async-start | bytes 5013504 | tf_op jit(solution)/shard_map/all_gather | solution.py:872
  17.3 24.3 %collective-permute-start.1 = (bf16[512,768]{1,0:T(8,128)(2,1)S(1)}, bf16[512,768]{1,0:T(8,128)(2,1)S(1)}, u32[]{:S(2)}, u32[]{:S(2)}) collective-permute-start(bf16[512,768]{1,0:T(8,128)(2,1)S(1)} %bitcast.218), channel_id=1, source_target_pairs={{0,16},{8,24},{16,0},{24,8},{1,17},{9,25},{17,1},{25,9},{2,18},{10... | collective-permute-start | bytes 2359304 | tf_op jit(solution)/shard_map/ppermute | solution.py:783
  18.8 35.3 %collective-permute-start.2 = (bf16[512,768]{1,0:T(8,128)(2,1)S(1)}, bf16[512,768]{1,0:T(8,128)(2,1)S(1)}, u32[]{:S(2)}, u32[]{:S(2)}) collective-permute-start(bf16[512,768]{1,0:T(8,128)(2,1)S(1)} %bitcast.219), channel_id=1, source_target_pairs={{0,8},{8,0},{16,24},{24,16},{1,9},{9,1},{17,25},{25,17},{2,10},{10... | collective-permute-start | bytes 2359304 | tf_op jit(solution)/shard_map/ppermute | solution.py:783
  26.4 9.6 %collective-permute-start.12 = (bf16[48,1664]{1,0:T(8,128)(2,1)S(1)}, bf16[48,1664]{1,0:T(8,128)(2,1)S(1)}, u32[]{:S(2)}, u32[]{:S(2)}) collective-permute-start(bf16[48,1664]{1,0:T(8,128)(2,1)S(1)} %bitcast.285), channel_id=1, source_target_pairs={{0,2},{1,3},{2,0},{3,1},{4,6},{5,7},{6,4},{7,5},{8,10},{9,11},{10,... | collective-permute-start | bytes 479240 | tf_op jit(solution)/shard_map/ppermute | solution.py:783
  26.5 15.1 %collective-permute-start.7 = (bf16[48,1536]{1,0:T(8,128)(2,1)S(1)}, bf16[48,1536]{1,0:T(8,128)(2,1)S(1)}, u32[]{:S(2)}, u32[]{:S(2)}) collective-permute-start(bf16[48,1536]{1,0:T(8,128)(2,1)S(1)} %bitcast.287), channel_id=1, source_target_pairs={{0,2},{1,3},{2,0},{3,1},{4,6},{5,7},{6,4},{7,5},{8,10},{9,11},{10,... | collective-permute-start | bytes 442376 | tf_op jit(solution)/shard_map/ppermute | solution.py:783
  36.1 9.5 %collective-permute-start.13 = (bf16[96,1664]{1,0:T(8,128)(2,1)S(1)}, bf16[96,1664]{1,0:T(8,128)(2,1)S(1)}, u32[]{:S(2)}, u32[]{:S(2)}) collective-permute-start(bf16[96,1664]{1,0:T(8,128)(2,1)S(1)} %bitcast.258), channel_id=1, source_target_pairs={{0,16},{8,24},{16,0},{24,8},{1,17},{9,25},{17,1},{25,9},{2,18},{10... | collective-permute-start | bytes 958472 | tf_op jit(solution)/shard_map/ppermute | solution.py:783
  41.6 12.4 %collective-permute-start.8 = (bf16[96,1536]{1,0:T(8,128)(2,1)S(1)}, bf16[96,1536]{1,0:T(8,128)(2,1)S(1)}, u32[]{:S(2)}, u32[]{:S(2)}) collective-permute-start(bf16[96,1536]{1,0:T(8,128)(2,1)S(1)} %bitcast.262), channel_id=1, source_target_pairs={{0,1},{1,0},{2,3},{3,2},{4,5},{5,4},{6,7},{7,6},{8,9},{9,8},{10,11... | collective-permute-start | bytes 884744 | tf_op jit(solution)/shard_map/ppermute | solution.py:783
  45.7 8.5 %collective-permute-start.3 = (bf16[512,768]{1,0:T(8,128)(2,1)S(1)}, bf16[512,768]{1,0:T(8,128)(2,1)S(1)}, u32[]{:S(2)}, u32[]{:S(2)}) collective-permute-start(bf16[512,768]{1,0:T(8,128)(2,1)S(1)} %collective-permute-done.1.refs_1_), channel_id=1, source_target_pairs={{0,8},{8,0},{16,24},{24,16},{1,9},{9,1},{17,25},{25,17},{2,10},{10... | collective-permute-start | bytes 2359304 | tf_op jit(solution)/shard_map/ppermute | solution.py:783
  45.8 22.3 %collective-permute-start.14 = (bf16[192,1664]{1,0:T(8,128)(2,1)S(1)}, bf16[192,1664]{1,0:T(8,128)(2,1)S(1)}, u32[]{:S(2)}, u32[]{:S(2)}) collective-permute-start(bf16[192,1664]{1,0:T(8,128)(2,1)S(1)} %bitcast.243), channel_id=1, source_target_pairs={{0,1},{1,0},{2,3},{3,2},{4,5},{5,4},{6,7},{7,6},{8,9},{9,8},{10,11... | collective-permute-start | bytes 1916936 | tf_op jit(solution)/shard_map/ppermute | solution.py:783
  54.2 16.2 %collective-permute-start.9 = (bf16[192,1536]{1,0:T(8,128)(2,1)S(1)}, bf16[192,1536]{1,0:T(8,128)(2,1)S(1)}, u32[]{:S(2)}, u32[]{:S(2)}) collective-permute-start(bf16[192,1536]{1,0:T(8,128)(2,1)S(1)} %bitcast.248), channel_id=1, source_target_pairs={{0,16},{8,24},{16,0},{24,8},{1,17},{9,25},{17,1},{25,9},{2,18},{10... | collective-permute-start | bytes 1769480 | tf_op jit(solution)/shard_map/ppermute | solution.py:783
  71.7 33.9 %collective-permute-start.17 = (bf16[512,768]{1,0:T(8,128)(2,1)S(1)}, bf16[512,768]{1,0:T(8,128)(2,1)S(1)}, u32[]{:S(2)}, u32[]{:S(2)}) collective-permute-start(bf16[512,768]{1,0:T(8,128)(2,1)S(1)} %bitcast.204), channel_id=1, source_target_pairs={{0,8},{8,0},{16,24},{24,16},{1,9},{9,1},{17,25},{25,17},{2,10},{10... | collective-permute-start | bytes 2359304 | tf_op jit(solution)/shard_map/ppermute | solution.py:783
  129.8 28.5 %collective-permute-start.19 = (bf16[768,768]{1,0:T(8,128)(2,1)}, bf16[768,768]{1,0:T(8,128)(2,1)S(1)}, u32[]{:S(2)}, u32[]{:S(2)}) collective-permute-start(bf16[768,768]{1,0:T(8,128)(2,1)} %bitcast.216), channel_id=1, source_target_pairs={{0,16},{8,24},{16,0},{24,8},{1,17},{9,25},{17,1},{25,9},{2,18},{10... | collective-permute-start | bytes 3538952 | tf_op jit(solution)/shard_map/ppermute | solution.py:783
  132.1 28.0 %collective-permute-start.20 = (bf16[768,768]{1,0:T(8,128)(2,1)S(1)}, bf16[768,768]{1,0:T(8,128)(2,1)S(1)}, u32[]{:S(2)}, u32[]{:S(2)}) collective-permute-start(bf16[768,768]{1,0:T(8,128)(2,1)S(1)} %bitcast.202), channel_id=1, source_target_pairs={{0,1},{1,0},{2,3},{3,2},{4,5},{5,4},{6,7},{7,6},{8,9},{9,8},{10,11... | collective-permute-start | bytes 3538952 | tf_op jit(solution)/shard_map/ppermute | solution.py:783
  158.6 15.1 %collective-permute-start.21 = (bf16[384,768]{1,0:T(8,128)(2,1)S(1)}, bf16[384,768]{1,0:T(8,128)(2,1)S(1)}, u32[]{:S(2)}, u32[]{:S(2)}) collective-permute-start(bf16[384,768]{1,0:T(8,128)(2,1)S(1)} %bitcast.211), channel_id=1, source_target_pairs={{0,1},{1,0},{2,3},{3,2},{4,5},{5,4},{6,7},{7,6},{8,9},{9,8},{10,11... | collective-permute-start | bytes 1769480 | tf_op jit(solution)/shard_map/ppermute | solution.py:783
  160.4 14.6 %collective-permute-start.22 = (bf16[384,768]{1,0:T(8,128)(2,1)S(1)}, bf16[384,768]{1,0:T(8,128)(2,1)S(1)}, u32[]{:S(2)}, u32[]{:S(2)}) collective-permute-start(bf16[384,768]{1,0:T(8,128)(2,1)S(1)} %bitcast.213), channel_id=1, source_target_pairs={{0,16},{8,24},{16,0},{24,8},{1,17},{9,25},{17,1},{25,9},{2,18},{10... | collective-permute-start | bytes 1769480 | tf_op jit(solution)/shard_map/ppermute | solution.py:783
  177.5 23.0 %collective-permute-start.26 = (bf16[384,768]{1,0:T(8,128)(2,1)S(1)}, bf16[384,768]{1,0:T(8,128)(2,1)S(1)}, u32[]{:S(2)}, u32[]{:S(2)}) collective-permute-start(bf16[384,768]{1,0:T(8,128)(2,1)S(1)} %bitcast.207), channel_id=1, source_target_pairs={{0,2},{1,3},{2,0},{3,1},{4,6},{5,7},{6,4},{7,5},{8,10},{9,11},{10,... | collective-permute-start | bytes 1769480 | tf_op jit(solution)/shard_map/ppermute | solution.py:783
  181.2 19.5 %collective-permute-start.27 = (bf16[192,1536]{1,0:T(8,128)(2,1)S(1)}, bf16[192,1536]{1,0:T(8,128)(2,1)S(1)}, u32[]{:S(2)}, u32[]{:S(2)}) collective-permute-start(bf16[192,1536]{1,0:T(8,128)(2,1)S(1)} %bitcast.209), channel_id=1, source_target_pairs={{0,1},{1,0},{2,3},{3,2},{4,5},{5,4},{6,7},{7,6},{8,9},{9,8},{10,11... | collective-permute-start | bytes 1769480 | tf_op jit(solution)/shard_map/ppermute | solution.py:783
  184.4 16.5 %collective-permute-start.28 = (bf16[192,1536]{1,0:T(8,128)(2,1)S(1)}, bf16[192,1536]{1,0:T(8,128)(2,1)S(1)}, u32[]{:S(2)}, u32[]{:S(2)}) collective-permute-start(bf16[192,1536]{1,0:T(8,128)(2,1)S(1)} %get-tuple-element.160.refs_14_), channel_id=1, source_target_pairs={{0,16},{8,24},{16,0},{24,8},{1,17},{9,25},{17,1},{25,9},{2,18},{10... | collective-permute-start | bytes 1769480 | tf_op jit(solution)/shard_map/ppermute | solution.py:783
  202.9 16.2 %collective-permute-start.35 = (bf16[192,768]{1,0:T(8,128)(2,1)S(1)}, bf16[192,768]{1,0:T(8,128)(2,1)S(1)}, u32[]{:S(2)}, u32[]{:S(2)}) collective-permute-start(bf16[192,768]{1,0:T(8,128)(2,1)S(1)} %bitcast.281), channel_id=1, source_target_pairs={{0,4},{1,5},{2,6},{3,7},{4,0},{5,1},{6,2},{7,3},{8,12},{9,13},{10,... | collective-permute-start | bytes 884744 | tf_op jit(solution)/shard_map/ppermute | solution.py:783
  205.3 9.1 %collective-permute-start.33 = (bf16[96,1536]{1,0:T(8,128)(2,1)}, bf16[96,1536]{1,0:T(8,128)(2,1)S(1)}, u32[]{:S(2)}, u32[]{:S(2)}) collective-permute-start(bf16[96,1536]{1,0:T(8,128)(2,1)} %bitcast.282), channel_id=1, source_target_pairs={{0,1},{1,0},{2,3},{3,2},{4,5},{5,4},{6,7},{7,6},{8,9},{9,8},{10,11... | collective-permute-start | bytes 884744 | tf_op jit(solution)/shard_map/ppermute | solution.py:783
  206.5 10.4 %collective-permute-start.32 = (bf16[96,1536]{1,0:T(8,128)(2,1)S(1)}, bf16[96,1536]{1,0:T(8,128)(2,1)S(1)}, u32[]{:S(2)}, u32[]{:S(2)}) collective-permute-start(bf16[96,1536]{1,0:T(8,128)(2,1)S(1)} %get-tuple-element.142), channel_id=1, source_target_pairs={{0,16},{8,24},{16,0},{24,8},{1,17},{9,25},{17,1},{25,9},{2,18},{10... | collective-permute-start | bytes 884744 | tf_op jit(solution)/shard_map/ppermute | solution.py:783
  210.7 22.1 %collective-permute-start.38 = (bf16[1,512,768]{2,1,0:T(8,128)(2,1)}, bf16[1,512,768]{2,1,0:T(8,128)(2,1)}, u32[]{:S(2)}, u32[]{:S(2)}) collective-permute-start(bf16[1,512,768]{2,1,0:T(8,128)(2,1)} %add_convert_fusion), channel_id=1, source_target_pairs={{0,16},{8,24},{16,0},{24,8},{1,17},{9,25},{17,1},{25,9},{2,18},{10... | collective-permute-start | bytes 2359304 | tf_op jit(solution)/shard_map/ppermute | solution.py:783
  217.2 8.4 %collective-permute-start.36 = (bf16[48,3200]{1,0:T(8,128)(2,1)S(1)}, bf16[48,3200]{1,0:T(8,128)(2,1)S(1)}, u32[]{:S(2)}, u32[]{:S(2)}) collective-permute-start(bf16[48,3200]{1,0:T(8,128)(2,1)S(1)} %bitcast.279), channel_id=1, source_target_pairs={{0,2},{1,3},{2,0},{3,1},{4,6},{5,7},{6,4},{7,5},{8,10},{9,11},{10,... | collective-permute-start | bytes 921608 | tf_op jit(solution)/shard_map/ppermute | solution.py:783
  225.7 9.9 %collective-permute-start.39 = (bf16[24,3200]{1,0:T(8,128)(2,1)S(1)}, bf16[24,3200]{1,0:T(8,128)(2,1)}, u32[]{:S(2)}, u32[]{:S(2)}) collective-permute-start(bf16[24,3200]{1,0:T(8,128)(2,1)S(1)} %get-tuple-element.184), channel_id=1, source_target_pairs={{0,4},{1,5},{2,6},{3,7},{4,0},{5,1},{6,2},{7,3},{8,12},{9,13},{10,... | collective-permute-start | bytes 460808 | tf_op jit(solution)/shard_map/ppermute | solution.py:783
  (59 other events, 316.2 us)
Sparse Core Ops, SparseCore 0:
  19.0 87.6 all-gather.1

commit v4 on v3

--- a/solution.py
+++ b/solution.py
@@ -531,13 +531,12 @@
 def between(near, d_normed, d_normed_other, middle, pulled, vectors, mixed, weights, halves):
     tokens, width = mixed.shape
     depth = width // (2 * halves)
-    size = tokens // 2
+    size = tokens
 
     def kernel(
         near_ref, dn_ref, more_ref, middle_ref, cot_ref, vec_ref, mixed_ref, w_ref,
-        dmiddle_ref, dmixed_ref, sent_ref, kept_ref, sums_ref, d_attn, grads,
+        dmiddle_ref, dmixed_ref, sent_ref, kept_ref, sums_ref, d_attn,
     ):
-        step = pl.program_id(0)
         gain = vec_ref[GAIN2 : GAIN2 + 1]
         sums = 0.0
         for c in range(0, size, CHUNK):
@@ -555,18 +554,11 @@
         dmixed_ref[...] = dot(d_attn[...], w_ref[...], 1, 1).astype(BF16)
         more = dot(mixed_ref[...], d_attn[...], 0, 0)
 
-        @pl.when(step == 0)
-        def _():
-            sums_ref[...] = sums
-            grads[...] = more
-
-        @pl.when(step == 1)
-        def _():
-            sums_ref[...] += sums
-            value = (grads[...] + more).astype(BF16)
-            for x, (sent, kept) in enumerate(zip(*parted(value, near_ref[0], depth), strict=True)):
-                sent_ref[x] = sent
-                kept_ref[x] = kept
+        sums_ref[...] = sums
+        value = more.astype(BF16)
+        for x, (sent, kept) in enumerate(zip(*parted(value, near_ref[0], depth), strict=True)):
+            sent_ref[x] = sent
+            kept_ref[x] = kept
 
     tile = pl.BlockSpec((size, width), lambda t, _: (t, 0))
     piece = whole(halves, depth, width)
@@ -574,13 +566,13 @@
         kernel,
         grid_spec=pltpu.PrefetchScalarGridSpec(
             num_scalar_prefetch=1,
-            grid=(2,),
+            grid=(1,),
             in_specs=[
                 tile, pl.BlockSpec((1, size, width), lambda t, _: (1, t, 0)), tile, tile,
                 whole(KINDS, width), tile, pl.BlockSpec((width, width), lambda t, _: (0, 3)),
             ],
             out_specs=[tile, tile, piece, piece, whole(8, width)],
-            scratch_shapes=[pltpu.VMEM((size, width), BF16), pltpu.VMEM((width, width), F32)],
+            scratch_shapes=[pltpu.VMEM((size, width), BF16)],
         ),
         out_shape=[
             placed(F32, tokens, width),

time: 251 us -> 251 us (level)
  transfers between devices with their start and end apart: 41 -> 41, of which waited for: 18 -> 19; matrix products, arithmetic and copies ran while one was open for 9% -> 9% of each run, Pallas kernels for 31% -> 31%
where the time goes in v4:
time: 251 us; the launch traced here: 247 us
  Pallas kernels  97.1 us (39%)
  waiting for transfers between devices  65.2 us (26%)
  starting transfers between devices  35 us (14%)
  other arithmetic  18.1 us (7%)
  local copies, waits for them, and re-layouts  15.9 us (6%)
  between operations  15.3 us (6%)
    ppermute x40, waiting for transfers between devices, swap(): lax.ppermute(array, axis, [(i, i ^ mask) for i in range(self.sizes[axis])])  65.1 us
    ppermute x40, starting transfers between devices, swap(): lax.ppermute(array, axis, [(i, i ^ mask) for i in range(self.sizes[axis])])  35 us
    pallas_call x1, Pallas kernels, branch(): pl.pallas_call(kernel, grid_spec=pltpu.PrefetchScalarGridSpec(num_scalar_...  21.7 us
    pallas_call x1, Pallas kernels, attend_back(): pl.pallas_call(kernel, grid=(rows,), in_specs=[tile, keys, pl.BlockSpec((...  18.5 us
    pallas_call x1, Pallas kernels, attend(): pl.pallas_call(attend_kernel, grid=(rows, steps), in_specs=[tile, pl.Bloc...  14.7 us
    pallas_call x1, Pallas kernels, first_norm(): pl.pallas_call(kernel, grid_spec=pltpu.PrefetchScalarGridSpec(num_scalar_...  14.6 us
    pallas_call x1, Pallas kernels, project(): pl.pallas_call(kernel, grid_spec=pltpu.PrefetchScalarGridSpec(num_scalar_...  12.1 us
    pallas_call x1, Pallas kernels, weight_grads(): pl.pallas_call(kernel, grid_spec=pltpu.PrefetchScalarGridSpec(num_scalar_...  8.14 us
  transfers between devices with their start and end apart: 41, of which 19 were waited for; matrix products, arithmetic and copies ran while one was open for 9% of the time, Pallas kernels for 31%

profile of v4, /device:TPU:0, one launch (start us, length us, event | category | flops | bytes accessed | tf_op | source)
XLA Modules:
  0.0 246.6 jit_solution(390830198602743713)
XLA Ops:
  7.2 2.1 reshape.670
  13.3 3.9 %collective-permute-start.6 = (bf16[24,1536]{1,0:T(8,128)(2,1)S(1)}, bf16[24,1536]{1,0:T(8,128)(2,1)S(1)}, u32[]{:S(2)}, u32[]{:S(2)}) collective-permute-start(bf16[24,1536]{1,0:T(8,128)(2,1)S(1)} %pad_maximum_fusion.15), channel_id=1, source_target_pairs={{0,4},{1,5},{2,6},{3,7},{4,0},{5,1},{6,2},{7,3},{8,12},{9,13},{10,... | collective-permute-start | bytes 221192 | tf_op jit(solution)/shard_map/ppermute | solution.py:775
  19.3 2.2 collective-permute-done.6
  21.4 4.9 %collective-permute-done.11 = bf16[24,1664]{1,0:T(8,128)(2,1)S(1)} collective-permute-done((bf16[24,1664]{1,0:T(8,128)(2,1)S(1)}, bf16[24,1664]{1,0:T(8,128)(2,1)S(1)}, u32[]{:S(2)}, u32[]{:S(2)}) %collective-permute-start.11) | collective-permute-done | bytes 79904 | tf_op jit(solution)/shard_map/ppermute | solution.py:775
  28.6 7.5 %collective-permute-done.12 = bf16[48,1664]{1,0:T(8,128)(2,1)S(1)} collective-permute-done((bf16[48,1664]{1,0:T(8,128)(2,1)S(1)}, bf16[48,1664]{1,0:T(8,128)(2,1)S(1)}, u32[]{:S(2)}, u32[]{:S(2)}) %collective-permute-start.12) | collective-permute-done | bytes 159776 | tf_op jit(solution)/shard_map/ppermute | solution.py:775
  37.2 4.3 %collective-permute-done.7 = bf16[48,1536]{1,0:T(8,128)(2,1)S(1)} collective-permute-done((bf16[48,1536]{1,0:T(8,128)(2,1)S(1)}, bf16[48,1536]{1,0:T(8,128)(2,1)S(1)}, u32[]{:S(2)}, u32[]{:S(2)}) %collective-permute-start.7) | collective-permute-done | bytes 147488 | tf_op jit(solution)/shard_map/ppermute | solution.py:775
  43.2 2.4 collective-permute-done.13
  47.4 6.6 %collective-permute-done.8 = bf16[96,1536]{1,0:T(8,128)(2,1)S(1)} collective-permute-done((bf16[96,1536]{1,0:T(8,128)(2,1)S(1)}, bf16[96,1536]{1,0:T(8,128)(2,1)S(1)}, u32[]{:S(2)}, u32[]{:S(2)}) %collective-permute-start.8) | collective-permute-done | bytes 294944 | tf_op jit(solution)/shard_map/ppermute | solution.py:775
  54.2 13.9 %collective-permute-done.14 = bf16[192,1664]{1,0:T(8,128)(2,1)S(1)} collective-permute-done((bf16[192,1664]{1,0:T(8,128)(2,1)S(1)}, bf16[192,1664]{1,0:T(8,128)(2,1)S(1)}, u32[]{:S(2)}, u32[]{:S(2)}) %collective-permute-start.14) | collective-permute-done | bytes 639008 | tf_op jit(solution)/shard_map/ppermute | solution.py:775
  71.7 3.1 %collective-permute-done.4 = bf16[1,2,256]{2,1,0:T(2,128)(2,1)S(1)} collective-permute-done((bf16[1,2,256]{2,1,0:T(2,128)(2,1)S(1)}, bf16[1,2,256]{2,1,0:T(2,128)(2,1)S(1)}, u32[]{:S(2)}, u32[]{:S(2)}) %collective-permute-start.4) | collective-permute-done | bytes 1056 | tf_op jit(solution)/shard_map/ppermute | solution.py:775
  76.0 12.1 %project.1 = (bf16[2048,768]{1,0:T(8,128)(2,1)}, bf16[768,2048]{1,0:T(8,128)(2,1)}, bf16[512,768]{1,0:T(8,128)(2,1)}, bf16[2048,1536]{1,0:T(8,128)(2,1)}, bf16[7...) custom-call(s32[1]{0:T(128)} %bitcast.near_ref, bf16[512,768]{1,0:T(8,128)(2,1)S(1)} %bitcast.220, ...), custom_call_target="tpu_custom_call" | custom-call | flops 6039797760 | bytes 22020096 | tf_op jit(solution)/shard_map/project/pallas_call | solution.py:324
  88.1 14.7 %attend.1 = (bf16[2,256,768]{2,1,0:T(8,128)(2,1)S(1)}, f32[2,256,768]{2,1,0:T(8,128)}, f32[2,6,1,512]{3,2,1,0:T(1,128)S(1)}) custom-call(bf16[2,256,768]{2,1,0:T(8,128)(2,1)} %bitcast.235, bf16[4,2,256,1536]{3,2,1,0:T(8,128)(2,1)} %bitcast.223, bf16[4,2,256,1536]{3,2,1,0:T(8,128)(2,1)} %bitcast.224, ...), custom_call_target="tpu_custom_call" | custom-call | flops 6442450944 | bytes 12582912 | tf_op jit(solution)/shard_map/attend/pallas_call | solution.py:186
  102.8 2.5 %open_branch.1 = (bf16[512,768]{1,0:T(8,128)(2,1)}, f32[512,768]{1,0:T(8,128)}) custom-call(bf16[512,768]{1,0:T(8,128)(2,1)S(1)} %bitcast.198, bf16[2048,768]{1,0:T(8,128)(2,1)S(1)} %copy-done.1, f32[4,2,1,256]{3,2,1,0:T(1,128)S(1)} %maximum_convert_fusion.refs_4_.refs_5_.flags_ref.refs_6_, f32[16,768]{1,0:T(8,128)S(1)} %get-tuple-element.91.vec_ref.refs_5_, ...), custom_call_target="tpu_custom_call" | custom-call | flops 603979776 | bytes 3932160 | tf_op jit(solution)/shard_map/open_branch/pallas_call | solution.py:384
  107.8 21.7 %branch.1 = (f32[512,768]{1,0:T(8,128)}, f32[512,768]{1,0:T(8,128)}, bf16[2,512,768]{2,1,0:T(8,128)(2,1)}, bf16[2,2,192,768]{3,2,1,0:T(8,128)(2,1)}, bf16[2,2,19...) custom-call(s32[2]{0:T(128)S(1)} %pad_add_fusion.places_ref, ...), custom_call_target="tpu_custom_call" | custom-call | flops 14495514624 | bytes 11796480 | tf_op jit(solution)/shard_map/branch/pallas_call | solution.py:487
  133.9 5.0 %between.1 = (f32[512,768]{1,0:T(8,128)}, bf16[512,768]{1,0:T(8,128)(2,1)S(1)}, bf16[2,192,768]{2,1,0:T(8,128)(2,1)}, bf16[2,192,768]{2,1,0:T(8,128)(2,1)}, f32[8,768]{1,0:T(8,128)S(1)}) custom-call(s32[1]{0:T(128)} %bitcast.near_ref, f32[512,768]{1,0:T(8,128)S(1)} %copy-done.3, bf16[2,512,768]{2,1,0:T(8,128)(2,1)S(1)} %collective-permute-done.18.more_ref, ...), custom_call_target="tpu_custom_call" | custom-call | flops 1207959552 | bytes 6291456 | tf_op jit(solution)/shard_map/between/pallas_call | solution.py:565
  138.9 18.5 %attend_back.1 = (bf16[2,256,768]{2,1,0:T(8,128)(2,1)}, bf16[4,2,256,768]{3,2,1,0:T(8,128)(2,1)}, bf16[4,2,256,768]{3,2,1,0:T(8,128)(2,1)}, f32[2,6,1,128]{3,2,1,0:T(1,128)S(1)}, f32[2,6,1,128]{3,2,1,0:T(1,128)S(1)}) custom-call(bf16[2,256,768]{2,1,0:T(8,128)(2,1)S(1)} %bitcast.236, bf16[4,2,256,1536]{3,2,1,0:T(8,128)(2,1)S(1)} %bitcast.227, ...), custom_call_target="tpu_custom_call" | custom-call | flops 12884901888 | bytes 25165824 | tf_op jit(solution)/shard_map/attend_back/pallas_call | solution.py:226
  162.1 8.1 %weight_grads.1 = (bf16[2,192,1536]{2,1,0:T(8,128)(2,1)}, bf16[2,192,1536]{2,1,0:T(8,128)(2,1)}, bf16[2,192,768]{2,1,0:T(8,128)(2,1)}, bf16[2,192,768]{2,1,0:T(8,128)(2,1)}) custom-call(s32[1]{0:T(128)} %bitcast.near_ref, bf16[768,2048]{1,0:T(8,128)(2,1)S(1)} %copy-done.12, bf16[2048,768]{1,0:T(8,128)(2,1)S(1)} %bitcast.230, ...), custom_call_target="tpu_custom_call" | custom-call | flops 6039797760 | bytes 19660800 | tf_op jit(solution)/shard_map/weight_grads/pallas_call | solution.py:618
  186.0 14.6 %first_norm.1 = (bf16[1,512,768]{2,1,0:T(8,128)(2,1)}, bf16[2,512,768]{2,1,0:T(8,128)(2,1)}, f32[512,768]{1,0:T(8,128)}, bf16[2,192,128]{2,1,0:T(8,128)(2,1)S(1)}, bf16[2,192,128]{2,1,0:T(8,128)(2,1)S(1)}) custom-call(s32[1]{0:T(128)} %bitcast.near_ref, bf16[2048,768]{1,0:T(8,128)(2,1)} %bitcast.229, bf16[2048,768]{1,0:T(8,128)(2,1)} %bitcast.231, ...), custom_call_target="tpu_custom_call" | custom-call | flops 6039797760 | bytes 19660800 | tf_op jit(solution)/shard_map/first_norm/pallas_call | solution.py:720
  202.9 2.4 collective-permute-start.35
  208.0 2.7 %add_convert_fusion = bf16[1,512,768]{2,1,0:T(8,128)(2,1)} fusion(bf16[1,512,768]{2,1,0:T(8,128)(2,1)} %get-tuple-element.136, bf16[2,512,768]{2,1,0:T(8,128)(2,1)S(1)} %collective-permute-done.30), kind=kLoop, calls=%fused_computation.6 | loop fusion | flops 1572864 | bytes 2359296 | tf_op jit(solution)/shard_map/convert_element_type | solution.py:952
  214.4 2.6 %collective-permute-done.32 = bf16[96,1536]{1,0:T(8,128)(2,1)S(1)} collective-permute-done((bf16[96,1536]{1,0:T(8,128)(2,1)S(1)}, bf16[96,1536]{1,0:T(8,128)(2,1)S(1)}, u32[]{:S(2)}, u32[]{:S(2)}) %collective-permute-start.32) | collective-permute-done | bytes 294944 | tf_op jit(solution)/shard_map/ppermute | solution.py:775
  219.3 6.3 %collective-permute-done.36 = bf16[48,3200]{1,0:T(8,128)(2,1)S(1)} collective-permute-done((bf16[48,3200]{1,0:T(8,128)(2,1)S(1)}, bf16[48,3200]{1,0:T(8,128)(2,1)S(1)}, u32[]{:S(2)}, u32[]{:S(2)}) %collective-permute-start.36) | collective-permute-done | bytes 307232 | tf_op jit(solution)/shard_map/ppermute | solution.py:775
  230.2 2.6 %reshape.726 = f32[24,3072]{1,0:T(8,128)} reshape(f32[24,32,4,24]{3,2,1,0:T(4,128)S(1)} %copy.87) | data formatting | bytes 589824 | tf_op jit(solution)/shard_map/reshape | solution.py:972
  232.8 2.8 %fusion = f32[512,768]{1,0:T(8,128)} fusion(f32[512,768]{1,0:T(8,128)S(1)} %copy-done.14, bf16[2,512,768]{2,1,0:T(8,128)(2,1)} %copy-done.15, bf16[1,512,768]{2,1,0:T(8,128)(2,1)} %collective-permute-done.38, pred[512]{0:T(512)(128)(4,1)S(1)} %copy-done.24), kind=kLoop, calls=%fused_computation.1 | loop fusion | flops 1966080 | bytes 4719104 | tf_op jit(solution)/shard_map/jit(_where)/select_n | solution.py:975
  (235 shorter events, 64.1 us)
Async XLA Ops:
  7.2 100.6 %all-gather.2.cloned.1.call-start = ((), (), s32[]{:S(2)}) async-start(), calls=%async_computation | async-start | bytes 5013504 | tf_op jit(solution)/shard_map/all_gather | solution.py:864
  17.3 24.3 %collective-permute-start.1 = (bf16[512,768]{1,0:T(8,128)(2,1)S(1)}, bf16[512,768]{1,0:T(8,128)(2,1)S(1)}, u32[]{:S(2)}, u32[]{:S(2)}) collective-permute-start(bf16[512,768]{1,0:T(8,128)(2,1)S(1)} %bitcast.218), channel_id=1, source_target_pairs={{0,16},{8,24},{16,0},{24,8},{1,17},{9,25},{17,1},{25,9},{2,18},{10... | collective-permute-start | bytes 2359304 | tf_op jit(solution)/shard_map/ppermute | solution.py:775
  18.8 35.3 %collective-permute-start.2 = (bf16[512,768]{1,0:T(8,128)(2,1)S(1)}, bf16[512,768]{1,0:T(8,128)(2,1)S(1)}, u32[]{:S(2)}, u32[]{:S(2)}) collective-permute-start(bf16[512,768]{1,0:T(8,128)(2,1)S(1)} %bitcast.219), channel_id=1, source_target_pairs={{0,8},{8,0},{16,24},{24,16},{1,9},{9,1},{17,25},{25,17},{2,10},{10... | collective-permute-start | bytes 2359304 | tf_op jit(solution)/shard_map/ppermute | solution.py:775
  26.4 9.6 %collective-permute-start.12 = (bf16[48,1664]{1,0:T(8,128)(2,1)S(1)}, bf16[48,1664]{1,0:T(8,128)(2,1)S(1)}, u32[]{:S(2)}, u32[]{:S(2)}) collective-permute-start(bf16[48,1664]{1,0:T(8,128)(2,1)S(1)} %bitcast.285), channel_id=1, source_target_pairs={{0,2},{1,3},{2,0},{3,1},{4,6},{5,7},{6,4},{7,5},{8,10},{9,11},{10,... | collective-permute-start | bytes 479240 | tf_op jit(solution)/shard_map/ppermute | solution.py:775
  26.5 15.1 %collective-permute-start.7 = (bf16[48,1536]{1,0:T(8,128)(2,1)S(1)}, bf16[48,1536]{1,0:T(8,128)(2,1)S(1)}, u32[]{:S(2)}, u32[]{:S(2)}) collective-permute-start(bf16[48,1536]{1,0:T(8,128)(2,1)S(1)} %bitcast.287), channel_id=1, source_target_pairs={{0,2},{1,3},{2,0},{3,1},{4,6},{5,7},{6,4},{7,5},{8,10},{9,11},{10,... | collective-permute-start | bytes 442376 | tf_op jit(solution)/shard_map/ppermute | solution.py:775
  36.1 9.5 %collective-permute-start.13 = (bf16[96,1664]{1,0:T(8,128)(2,1)S(1)}, bf16[96,1664]{1,0:T(8,128)(2,1)S(1)}, u32[]{:S(2)}, u32[]{:S(2)}) collective-permute-start(bf16[96,1664]{1,0:T(8,128)(2,1)S(1)} %bitcast.258), channel_id=1, source_target_pairs={{0,16},{8,24},{16,0},{24,8},{1,17},{9,25},{17,1},{25,9},{2,18},{10... | collective-permute-start | bytes 958472 | tf_op jit(solution)/shard_map/ppermute | solution.py:775
  41.6 12.4 %collective-permute-start.8 = (bf16[96,1536]{1,0:T(8,128)(2,1)S(1)}, bf16[96,1536]{1,0:T(8,128)(2,1)S(1)}, u32[]{:S(2)}, u32[]{:S(2)}) collective-permute-start(bf16[96,1536]{1,0:T(8,128)(2,1)S(1)} %bitcast.262), channel_id=1, source_target_pairs={{0,1},{1,0},{2,3},{3,2},{4,5},{5,4},{6,7},{7,6},{8,9},{9,8},{10,11... | collective-permute-start | bytes 884744 | tf_op jit(solution)/shard_map/ppermute | solution.py:775
  45.7 8.5 %collective-permute-start.3 = (bf16[512,768]{1,0:T(8,128)(2,1)S(1)}, bf16[512,768]{1,0:T(8,128)(2,1)S(1)}, u32[]{:S(2)}, u32[]{:S(2)}) collective-permute-start(bf16[512,768]{1,0:T(8,128)(2,1)S(1)} %collective-permute-done.1.refs_1_), channel_id=1, source_target_pairs={{0,8},{8,0},{16,24},{24,16},{1,9},{9,1},{17,25},{25,17},{2,10},{10... | collective-permute-start | bytes 2359304 | tf_op jit(solution)/shard_map/ppermute | solution.py:775
  45.8 22.3 %collective-permute-start.14 = (bf16[192,1664]{1,0:T(8,128)(2,1)S(1)}, bf16[192,1664]{1,0:T(8,128)(2,1)S(1)}, u32[]{:S(2)}, u32[]{:S(2)}) collective-permute-start(bf16[192,1664]{1,0:T(8,128)(2,1)S(1)} %bitcast.243), channel_id=1, source_target_pairs={{0,1},{1,0},{2,3},{3,2},{4,5},{5,4},{6,7},{7,6},{8,9},{9,8},{10,11... | collective-permute-start | bytes 1916936 | tf_op jit(solution)/shard_map/ppermute | solution.py:775
  54.2 16.2 %collective-permute-start.9 = (bf16[192,1536]{1,0:T(8,128)(2,1)S(1)}, bf16[192,1536]{1,0:T(8,128)(2,1)S(1)}, u32[]{:S(2)}, u32[]{:S(2)}) collective-permute-start(bf16[192,1536]{1,0:T(8,128)(2,1)S(1)} %bitcast.248), channel_id=1, source_target_pairs={{0,16},{8,24},{16,0},{24,8},{1,17},{9,25},{17,1},{25,9},{2,18},{10... | collective-permute-start | bytes 1769480 | tf_op jit(solution)/shard_map/ppermute | solution.py:775
  71.7 33.9 %collective-permute-start.17 = (bf16[512,768]{1,0:T(8,128)(2,1)S(1)}, bf16[512,768]{1,0:T(8,128)(2,1)S(1)}, u32[]{:S(2)}, u32[]{:S(2)}) collective-permute-start(bf16[512,768]{1,0:T(8,128)(2,1)S(1)} %bitcast.204), channel_id=1, source_target_pairs={{0,8},{8,0},{16,24},{24,16},{1,9},{9,1},{17,25},{25,17},{2,10},{10... | collective-permute-start | bytes 2359304 | tf_op jit(solution)/shard_map/ppermute | solution.py:775
  129.8 28.5 %collective-permute-start.19 = (bf16[768,768]{1,0:T(8,128)(2,1)}, bf16[768,768]{1,0:T(8,128)(2,1)S(1)}, u32[]{:S(2)}, u32[]{:S(2)}) collective-permute-start(bf16[768,768]{1,0:T(8,128)(2,1)} %bitcast.216), channel_id=1, source_target_pairs={{0,16},{8,24},{16,0},{24,8},{1,17},{9,25},{17,1},{25,9},{2,18},{10... | collective-permute-start | bytes 3538952 | tf_op jit(solution)/shard_map/ppermute | solution.py:775
  132.1 28.0 %collective-permute-start.20 = (bf16[768,768]{1,0:T(8,128)(2,1)S(1)}, bf16[768,768]{1,0:T(8,128)(2,1)S(1)}, u32[]{:S(2)}, u32[]{:S(2)}) collective-permute-start(bf16[768,768]{1,0:T(8,128)(2,1)S(1)} %bitcast.202), channel_id=1, source_target_pairs={{0,1},{1,0},{2,3},{3,2},{4,5},{5,4},{6,7},{7,6},{8,9},{9,8},{10,11... | collective-permute-start | bytes 3538952 | tf_op jit(solution)/shard_map/ppermute | solution.py:775
  158.5 14.8 %collective-permute-start.21 = (bf16[384,768]{1,0:T(8,128)(2,1)S(1)}, bf16[384,768]{1,0:T(8,128)(2,1)S(1)}, u32[]{:S(2)}, u32[]{:S(2)}) collective-permute-start(bf16[384,768]{1,0:T(8,128)(2,1)S(1)} %bitcast.211), channel_id=1, source_target_pairs={{0,1},{1,0},{2,3},{3,2},{4,5},{5,4},{6,7},{7,6},{8,9},{9,8},{10,11... | collective-permute-start | bytes 1769480 | tf_op jit(solution)/shard_map/ppermute | solution.py:775
  160.4 14.6 %collective-permute-start.22 = (bf16[384,768]{1,0:T(8,128)(2,1)S(1)}, bf16[384,768]{1,0:T(8,128)(2,1)S(1)}, u32[]{:S(2)}, u32[]{:S(2)}) collective-permute-start(bf16[384,768]{1,0:T(8,128)(2,1)S(1)} %bitcast.213), channel_id=1, source_target_pairs={{0,16},{8,24},{16,0},{24,8},{1,17},{9,25},{17,1},{25,9},{2,18},{10... | collective-permute-start | bytes 1769480 | tf_op jit(solution)/shard_map/ppermute | solution.py:775
  177.5 23.1 %collective-permute-start.26 = (bf16[384,768]{1,0:T(8,128)(2,1)S(1)}, bf16[384,768]{1,0:T(8,128)(2,1)S(1)}, u32[]{:S(2)}, u32[]{:S(2)}) collective-permute-start(bf16[384,768]{1,0:T(8,128)(2,1)S(1)} %bitcast.207), channel_id=1, source_target_pairs={{0,2},{1,3},{2,0},{3,1},{4,6},{5,7},{6,4},{7,5},{8,10},{9,11},{10,... | collective-permute-start | bytes 1769480 | tf_op jit(solution)/shard_map/ppermute | solution.py:775
  181.2 19.5 %collective-permute-start.27 = (bf16[192,1536]{1,0:T(8,128)(2,1)S(1)}, bf16[192,1536]{1,0:T(8,128)(2,1)S(1)}, u32[]{:S(2)}, u32[]{:S(2)}) collective-permute-start(bf16[192,1536]{1,0:T(8,128)(2,1)S(1)} %bitcast.209), channel_id=1, source_target_pairs={{0,1},{1,0},{2,3},{3,2},{4,5},{5,4},{6,7},{7,6},{8,9},{9,8},{10,11... | collective-permute-start | bytes 1769480 | tf_op jit(solution)/shard_map/ppermute | solution.py:775
  184.4 16.5 %collective-permute-start.28 = (bf16[192,1536]{1,0:T(8,128)(2,1)S(1)}, bf16[192,1536]{1,0:T(8,128)(2,1)S(1)}, u32[]{:S(2)}, u32[]{:S(2)}) collective-permute-start(bf16[192,1536]{1,0:T(8,128)(2,1)S(1)} %get-tuple-element.160.refs_14_), channel_id=1, source_target_pairs={{0,16},{8,24},{16,0},{24,8},{1,17},{9,25},{17,1},{25,9},{2,18},{10... | collective-permute-start | bytes 1769480 | tf_op jit(solution)/shard_map/ppermute | solution.py:775
  202.9 16.2 %collective-permute-start.35 = (bf16[192,768]{1,0:T(8,128)(2,1)S(1)}, bf16[192,768]{1,0:T(8,128)(2,1)S(1)}, u32[]{:S(2)}, u32[]{:S(2)}) collective-permute-start(bf16[192,768]{1,0:T(8,128)(2,1)S(1)} %bitcast.281), channel_id=1, source_target_pairs={{0,4},{1,5},{2,6},{3,7},{4,0},{5,1},{6,2},{7,3},{8,12},{9,13},{10,... | collective-permute-start | bytes 884744 | tf_op jit(solution)/shard_map/ppermute | solution.py:775
  205.3 9.1 %collective-permute-start.33 = (bf16[96,1536]{1,0:T(8,128)(2,1)}, bf16[96,1536]{1,0:T(8,128)(2,1)S(1)}, u32[]{:S(2)}, u32[]{:S(2)}) collective-permute-start(bf16[96,1536]{1,0:T(8,128)(2,1)} %bitcast.282), channel_id=1, source_target_pairs={{0,1},{1,0},{2,3},{3,2},{4,5},{5,4},{6,7},{7,6},{8,9},{9,8},{10,11... | collective-permute-start | bytes 884744 | tf_op jit(solution)/shard_map/ppermute | solution.py:775
  206.5 10.4 %collective-permute-start.32 = (bf16[96,1536]{1,0:T(8,128)(2,1)S(1)}, bf16[96,1536]{1,0:T(8,128)(2,1)S(1)}, u32[]{:S(2)}, u32[]{:S(2)}) collective-permute-start(bf16[96,1536]{1,0:T(8,128)(2,1)S(1)} %get-tuple-element.142), channel_id=1, source_target_pairs={{0,16},{8,24},{16,0},{24,8},{1,17},{9,25},{17,1},{25,9},{2,18},{10... | collective-permute-start | bytes 884744 | tf_op jit(solution)/shard_map/ppermute | solution.py:775
  210.7 22.1 %collective-permute-start.38 = (bf16[1,512,768]{2,1,0:T(8,128)(2,1)}, bf16[1,512,768]{2,1,0:T(8,128)(2,1)}, u32[]{:S(2)}, u32[]{:S(2)}) collective-permute-start(bf16[1,512,768]{2,1,0:T(8,128)(2,1)} %add_convert_fusion), channel_id=1, source_target_pairs={{0,16},{8,24},{16,0},{24,8},{1,17},{9,25},{17,1},{25,9},{2,18},{10... | collective-permute-start | bytes 2359304 | tf_op jit(solution)/shard_map/ppermute | solution.py:775
  217.2 8.4 %collective-permute-start.36 = (bf16[48,3200]{1,0:T(8,128)(2,1)S(1)}, bf16[48,3200]{1,0:T(8,128)(2,1)S(1)}, u32[]{:S(2)}, u32[]{:S(2)}) collective-permute-start(bf16[48,3200]{1,0:T(8,128)(2,1)S(1)} %bitcast.279), channel_id=1, source_target_pairs={{0,2},{1,3},{2,0},{3,1},{4,6},{5,7},{6,4},{7,5},{8,10},{9,11},{10,... | collective-permute-start | bytes 921608 | tf_op jit(solution)/shard_map/ppermute | solution.py:775
  225.7 9.9 %collective-permute-start.39 = (bf16[24,3200]{1,0:T(8,128)(2,1)S(1)}, bf16[24,3200]{1,0:T(8,128)(2,1)}, u32[]{:S(2)}, u32[]{:S(2)}) collective-permute-start(bf16[24,3200]{1,0:T(8,128)(2,1)S(1)} %get-tuple-element.184), channel_id=1, source_target_pairs={{0,4},{1,5},{2,6},{3,7},{4,0},{5,1},{6,2},{7,3},{8,12},{9,13},{10,... | collective-permute-start | bytes 460808 | tf_op jit(solution)/shard_map/ppermute | solution.py:775
  (59 other events, 314.0 us)
Sparse Core Ops, SparseCore 0:
  19.0 87.6 all-gather.1
